TPU v7x, 256 devices: a whole 4x4x8 slice. The times are simulated.
256 devices in a mesh: row: 16 (over y, x), col: 16 (over z, core).
Axes of the slice: x: 4, y: 4, z: 8, core: 2. Of those that a mesh axis runs over, the one named last changes fastest.
Arguments:
- kernel_matrix: float32 [16384, 16384], P('row', 'col'), may hold values from 0 to 3
Outputs:
- factored: float32 [16384, 16384], P('row', 'col')
All inputs are finite; a program needn't handle non-finite values.
Results may differ from a plain program's by a relative error of at most 0.0003.
Values sent between devices are 32-bit elements; how exact they have to be, the bound alone decides.
No kernel may reach another device: no remote copies, remote signals or barrier semaphores. Data moves between devices by JAX's collectives and lax.ppermute only.
A program may use at most 128 MiB of HBM per device.

v0:
```python
import jax
import jax.numpy as jnp
from jax import lax
from jax.sharding import PartitionSpec as P

TILE = 256
STEPS = 3


SHARP = lax.Precision.HIGHEST


def from_root(array, axis, root):
    mine = lax.axis_index(axis) == root
    return lax.psum(jnp.where(mine, array, jnp.zeros_like(array)), axis)


def times_transposed(left, right):
    return lax.dot_general(
        left, right, (((1,), (1,)), ((), ())), precision=SHARP, preferred_element_type=jnp.float32
    )


def factorize(diagonal):
    factor = jnp.linalg.cholesky(diagonal)
    inverse = jax.scipy.linalg.solve_triangular(
        factor, jnp.eye(TILE, dtype=jnp.float32), lower=True
    )
    return (factor, inverse)


def on_device(kernel_matrix):
    rows_axis = lax.axis_size("row")
    cols_axis = lax.axis_size("col")
    row_index = lax.axis_index("row")
    col_index = lax.axis_index("col")
    local_rows = kernel_matrix.shape[0]
    tile_cols = kernel_matrix.shape[1] // TILE
    factor_group = cols_axis // rows_axis
    chosen_slot = col_index // rows_axis
    source_row = col_index % rows_axis
    row_positions = jnp.arange(local_rows, dtype=jnp.int32)
    row_tile_global = row_positions // TILE * rows_axis + row_index
    matrix = kernel_matrix

    def prepare(column, panel_step):
        diag_row = panel_step % rows_axis
        diag_col = panel_step % cols_axis
        diag_tile_row = panel_step // rows_axis
        local_diag = column[diag_tile_row * TILE : (diag_tile_row + 1) * TILE]
        below_mask = (row_tile_global > panel_step)[:, None]
        diagonal = from_root(local_diag, "row", diag_row)
        factor, inverse = factorize(diagonal)
        solved = jnp.where(below_mask, times_transposed(column, inverse), 0.0)
        pieces = from_root(solved, "col", diag_col)
        chosen_pieces = lax.dynamic_index_in_dim(
            pieces.reshape(tile_cols, factor_group, TILE, TILE), chosen_slot, 1, keepdims=False
        )
        crossing = from_root(chosen_pieces.reshape(tile_cols * TILE, TILE), "row", source_row)
        return (factor, pieces, crossing)

    prepared = prepare(matrix[:, 0:TILE], 0)
    for panel_step in range(STEPS):
        block = matrix
        apply_factor, apply_pieces, apply_crossing = prepared
        block_width = block.shape[1] // TILE
        block = block - times_transposed(apply_pieces, apply_crossing)
        block_tiles = (
            0 + jnp.arange(block_width * TILE, dtype=jnp.int32) // TILE
        ) * cols_axis + col_index
        tile_row = panel_step // rows_axis
        on_row = row_index == panel_step % rows_axis
        top_rows = block[tile_row * TILE : (tile_row + 1) * TILE]
        top_rows = jnp.where(on_row & (block_tiles > panel_step)[None, :], 0.0, top_rows)
        block = block.at[tile_row * TILE : (tile_row + 1) * TILE].set(top_rows)
        tile_col = panel_step // cols_axis
        offset = (tile_col - 0) * TILE
        placed = jnp.pad(
            apply_factor, ((tile_row * TILE, local_rows - (tile_row + 1) * TILE), (0, 0))
        )
        written = apply_pieces + jnp.where(on_row, placed, 0.0)
        current = block[:, offset : offset + TILE]
        block = block.at[:, offset : offset + TILE].set(
            jnp.where(col_index == panel_step % cols_axis, written, current)
        )
        matrix = block
        if panel_step + 1 < STEPS:
            next_tile = (panel_step + 1) // cols_axis
            prepared = prepare(matrix[:, next_tile * TILE : (next_tile + 1) * TILE], panel_step + 1)
    return matrix


def solution(mesh):
    placed = (P("row", "col"),)
    return jax.shard_map(
        on_device, mesh=mesh, in_specs=placed, out_specs=P("row", "col"), check_vma=False
    )
```

profile of v0, /device:TPU:1, one launch (start us, length us, event | category | flops | bytes accessed | tf_op | source)
XLA Modules:
  0.0 1186.8 jit_solution(17133992909374628579)
XLA Ops:
  8.5 98.9 %all-reduce.14.cloned.1.call-done = f32[256,256]{0,1:T(8,128)} async-done(((f32[256,256]{0,1:T(8,128)}), f32[256,256]{0,1:T(8,128)}) %all-reduce.14.cloned.1.call-update) | async-done | bytes 262160 | tf_op jit(solution)/shard_map/psum | solution.py:15
  107.4 1.1 copy.3
  109.5 11.7 cholesky.172
  121.4 9.8 custom-call.15
  131.8 11.7 cholesky.189
  146.4 4.4 while.12
  147.3 1.4 dynamic-slice.65
  149.4 1.4 dynamic-slice.65
  150.9 19.7 %custom-call.16 = f32[2,128,128]{1,2,0:T(8,128)S(1)} custom-call(f32[2,128,128]{2,1,0:T(8,128)S(1)} %get-tuple-element.99), custom_call_target="InvertDiagBlocksLowerTriangular" | custom-call | tf_op jit(solution)/shard_map/jit(_solve_triangular)/triangular_solve | solution.py:26
  171.5 3.3 fusion.3
  174.9 112.0 %all-reduce.16.cloned.1.call-done = f32[1024,256]{0,1:T(8,128)} async-done(((f32[1024,256]{0,1:T(8,128)}), f32[1024,256]{0,1:T(8,128)}) %all-reduce.16.cloned.1.call-update) | async-done | bytes 1048592 | tf_op jit(solution)/shard_map/psum | solution.py:15
  286.8 1.1 broadcast_select_fusion.2
  288.7 97.5 %all-reduce.18.cloned.1.call-done = f32[1024,256]{0,1:T(8,128)} async-done(((f32[1024,256]{0,1:T(8,128)}), f32[1024,256]{0,1:T(8,128)}) %all-reduce.18.cloned.1.call-update) | async-done | bytes 1048592 | tf_op jit(solution)/shard_map/psum | solution.py:15
  386.2 6.6 convolution_subtract_fusion.2
  393.2 2.0 copy-done
  395.6 1.9 select_select_fusion.2
  398.7 93.5 %all-reduce.20.cloned.1.call-done = f32[256,256]{0,1:T(8,128)} async-done(((f32[256,256]{0,1:T(8,128)}), f32[256,256]{0,1:T(8,128)}) %all-reduce.20.cloned.1.call-update) | async-done | bytes 262160 | tf_op jit(solution)/shard_map/psum | solution.py:15
  494.3 11.7 cholesky.206
  506.2 9.8 custom-call.17
  516.6 11.7 cholesky.223
  531.8 4.5 while.13
  532.7 1.3 dynamic-slice.67
  534.8 1.3 dynamic-slice.67
  536.3 19.7 %custom-call.18 = f32[2,128,128]{1,2,0:T(8,128)S(1)} custom-call(f32[2,128,128]{2,1,0:T(8,128)S(1)} %get-tuple-element.100), custom_call_target="InvertDiagBlocksLowerTriangular" | custom-call | tf_op jit(solution)/shard_map/jit(_solve_triangular)/triangular_solve | solution.py:26
  556.9 2.1 fusion.1
  559.1 112.0 %all-reduce.22.cloned.1.call-done = f32[1024,256]{0,1:T(8,128)} async-done(((f32[1024,256]{0,1:T(8,128)}), f32[1024,256]{0,1:T(8,128)}) %all-reduce.22.cloned.1.call-update) | async-done | bytes 1048592 | tf_op jit(solution)/shard_map/psum | solution.py:15
  671.1 1.1 broadcast_select_fusion
  673.7 96.7 %all-reduce.24.cloned.1.call-done = f32[1024,256]{0,1:T(8,128)} async-done(((f32[1024,256]{0,1:T(8,128)}), f32[1024,256]{0,1:T(8,128)}) %all-reduce.24.cloned.1.call-update) | async-done | bytes 1048592 | tf_op jit(solution)/shard_map/psum | solution.py:15
  770.4 6.9 convolution_subtract_fusion.1
  777.3 2.3 fusion.6
  779.6 5.4 copy.17
  785.0 3.1 constant_dynamic-update-slice_fusion.3
  789.1 93.7 %all-reduce.26.cloned.1.call-done = f32[256,256]{0,1:T(8,128)} async-done(((f32[256,256]{0,1:T(8,128)}), f32[256,256]{0,1:T(8,128)}) %all-reduce.26.cloned.1.call-update) | async-done | bytes 262160 | tf_op jit(solution)/shard_map/psum | solution.py:15
  884.9 11.7 cholesky.240
  896.7 9.8 custom-call.19
  907.1 11.7 cholesky.257
  921.8 4.6 while.14
  922.7 1.4 dynamic-slice.69
  924.8 1.4 dynamic-slice.69
  926.4 19.7 %custom-call.20 = f32[2,128,128]{1,2,0:T(8,128)S(1)} custom-call(f32[2,128,128]{2,1,0:T(8,128)S(1)} %get-tuple-element.101), custom_call_target="InvertDiagBlocksLowerTriangular" | custom-call | tf_op jit(solution)/shard_map/jit(_solve_triangular)/triangular_solve | solution.py:26
  947.0 2.1 fusion
  949.2 112.0 %all-reduce.28.cloned.1.call-done = f32[1024,256]{0,1:T(8,128)} async-done(((f32[1024,256]{0,1:T(8,128)}), f32[1024,256]{0,1:T(8,128)}) %all-reduce.28.cloned.1.call-update) | async-done | bytes 1048592 | tf_op jit(solution)/shard_map/psum | solution.py:15
  1061.2 1.1 broadcast_select_fusion.1
  1062.3 98.3 %all-reduce.30.cloned.1.call-done = f32[1024,256]{0,1:T(8,128)} async-done(((f32[1024,256]{0,1:T(8,128)}), f32[1024,256]{0,1:T(8,128)}) %all-reduce.30.cloned.1.call-update) | async-done | bytes 1048592 | tf_op jit(solution)/shard_map/psum | solution.py:15
  1160.6 8.4 convolution_subtract_fusion
  1169.0 2.5 fusion.5
  1171.4 3.1 fusion.4
  1174.5 5.3 copy.26
  (129 shorter events, 27.0 us)
Async XLA Ops:
  6.5 100.9 %all-reduce.14.cloned.1.call-start = ((), (), s32[]{:S(2)}) async-start(), calls=%async_computation | async-start | bytes 524288 | tf_op jit(solution)/shard_map/psum | solution.py:15
  8.4 278.5 %all-reduce.16.cloned.1.call-start = ((), (), s32[]{:S(2)}) async-start(), calls=%async_computation.1 | async-start | bytes 2097152 | tf_op jit(solution)/shard_map/psum | solution.py:15
  174.8 211.4 %all-reduce.18.cloned.1.call-start = ((), (), s32[]{:S(2)}) async-start(), calls=%async_computation.2 | async-start | bytes 2097152 | tf_op jit(solution)/shard_map/psum | solution.py:15
  288.0 204.3 %all-reduce.20.cloned.1.call-start = ((), (), s32[]{:S(2)}) async-start(), calls=%async_computation.3 | async-start | bytes 524288 | tf_op jit(solution)/shard_map/psum | solution.py:15
  392.9 2.7 copy-start.1
  393.2 2.0 copy-start
  398.3 272.9 %all-reduce.22.cloned.1.call-start = ((), (), s32[]{:S(2)}) async-start(), calls=%async_computation.4 | async-start | bytes 2097152 | tf_op jit(solution)/shard_map/psum | solution.py:15
  559.1 211.3 %all-reduce.24.cloned.1.call-start = ((), (), s32[]{:S(2)}) async-start(), calls=%async_computation.5 | async-start | bytes 2097152 | tf_op jit(solution)/shard_map/psum | solution.py:15
  671.1 99.2 %copy-start.2 = (f32[1024,256]{0,1:T(8,128)S(1)}, f32[1024,256]{0,1:T(8,128)}, u32[]{:S(2)}) copy-start(f32[1024,256]{0,1:T(8,128)} %all-reduce.22.cloned.1.call-done) | copy-start | bytes 3145732
  672.3 210.5 %all-reduce.26.cloned.1.call-start = ((), (), s32[]{:S(2)}) async-start(), calls=%async_computation.6 | async-start | bytes 524288 | tf_op jit(solution)/shard_map/psum | solution.py:15
  779.6 5.4 copy-start.4
  788.8 272.3 %all-reduce.28.cloned.1.call-start = ((), (), s32[]{:S(2)}) async-start(), calls=%async_computation.7 | async-start | bytes 2097152 | tf_op jit(solution)/shard_map/psum | solution.py:15
  949.1 211.4 %all-reduce.30.cloned.1.call-start = ((), (), s32[]{:S(2)}) async-start(), calls=%async_computation.8 | async-start | bytes 2097152 | tf_op jit(solution)/shard_map/psum | solution.py:15
  1160.6 10.9 copy-start.3
Sparse Core Ops, SparseCore 0:
  10.5 96.8 all-reduce.13
  174.9 111.8 all-reduce.15
  290.1 96.0 all-reduce.17
  398.4 93.7 all-reduce.19
  559.2 111.8 all-reduce.21
  674.2 96.0 all-reduce.23
  789.0 93.7 all-reduce.25
  949.2 111.8 all-reduce.27
  1064.4 96.0 all-reduce.29
where the time goes:
time: 1200 us; the launch traced here: 1190 us
  waiting for transfers between devices  915 us (76%)
  other arithmetic  186 us (16%)
  matrix products  33.6 us (3%)
  local copies, waits for them, and re-layouts  32.5 us (3%)
  between operations  18.1 us (2%)
    psum x9, waiting for transfers between devices, from_root(): return lax.psum(jnp.where(mine, array, jnp.zeros_like(array)), axis)  915 us
    another operation x20, other arithmetic, factorize(): factor = jnp.linalg.cholesky(diagonal)  103 us
    another operation x7, other arithmetic, factorize(): jax.scipy.linalg.solve_triangular(factor, jnp.eye(TILE, dtype=jnp.float32...  60.6 us
    dot_general x6, matrix products, times_transposed(): lax.dot_general(left, right, (((1,), (1,)), ((), ())), precision=SHARP, p...  29.4 us
  transfers between devices with their start and end apart: 9, of which 9 were waited for; matrix products, arithmetic and copies ran while one was open for 0% of the time, Pallas kernels for 0%

commit v1 on v0

v1 whole, which is shorter than its diff:
```python
import jax
import jax.numpy as jnp
from jax import lax
from jax.experimental import pallas as pl
from jax.experimental.pallas import tpu as pltpu
from jax.sharding import PartitionSpec as P

TILE = 256
STEPS = 3
LEAD = TILE * STEPS
BLOCK = 128
SUB = 8
FULL = lax.Precision.HIGHEST

Y_SIZE, X_SIZE, Z_SIZE = 4, 4, 8
X_GROUPS = [[4 * y + x for x in range(4)] for y in range(4)]
Y_GROUPS = [[4 * y + x for y in range(4)] for x in range(4)]
Z_GROUPS = [[2 * z + core for z in range(8)] for core in range(2)]
CORE_SWAP = [(c, c ^ 1) for c in range(16)]


def dot(left, right, dims, precision=FULL):
    return lax.dot_general(
        left, right, (dims, ((), ())), precision=precision, preferred_element_type=jnp.float32
    )


def spread_row(value, i):
    return jnp.broadcast_to(value[i : i + 1, :], value.shape)


def spread_lane(value, i):
    return jnp.broadcast_to(value[:, i : i + 1], value.shape)


def factor_block(load, store):
    count = BLOCK // SUB
    sub = lax.broadcasted_iota(jnp.int32, (SUB, BLOCK), 0)
    lane = lax.broadcasted_iota(jnp.int32, (SUB, BLOCK), 1)
    left = [load(k) for k in range(count)]
    right = [(lane == sub + SUB * k).astype(jnp.float32) for k in range(count)]
    for k in range(count):
        columns = [spread_lane(left[k], SUB * k + m) for m in range(SUB)]
        s = [[spread_row(columns[m], i) for m in range(SUB)] for i in range(SUB)]
        rows_l = [spread_row(left[k], i) for i in range(SUB)]
        rows_r = [spread_row(right[k], i) for i in range(SUB)]
        out_l, out_r = [None] * SUB, [None] * SUB
        for i in range(SUB):
            scale = lax.rsqrt(s[i][i])
            u = [s[i][n] * scale if n > i else None for n in range(SUB)]
            out_l[i], out_r[i] = rows_l[i] * scale, rows_r[i] * scale
            for m in range(SUB):
                if m == i:
                    continue
                w = u[m] if m > i else s[m][i] * scale
                for n in range(i + 1, SUB):
                    s[m][n] = s[m][n] - w * u[n]
                rows_l[m] = rows_l[m] - w * out_l[i]
                rows_r[m] = rows_r[m] - w * out_r[i]
            for n in range(i + 1, SUB):
                s[i][n] = u[n] * scale
            rows_l[i], rows_r[i] = out_l[i] * scale, out_r[i] * scale
        merged_l, merged_r = out_l[0], out_r[0]
        for i in range(1, SUB):
            merged_l = jnp.where(sub == i, out_l[i], merged_l)
            merged_r = jnp.where(sub == i, out_r[i], merged_r)
        store(k, jnp.where(lane >= sub + SUB * k, merged_l, 0.0), merged_r)
        for j in range(k + 1, count):
            weights = [spread_lane(left[j], SUB * k + m) for m in range(SUB)]
            for m in range(SUB):
                left[j] = left[j] - weights[m] * rows_l[m]
                right[j] = right[j] - weights[m] * rows_r[m]


def factor_kernel(a_ref, u_ref, w_ref, work, block_u, block_w):
    count = LEAD // BLOCK
    work[...] = a_ref[...]
    w_ref[...] = jnp.zeros((LEAD, LEAD), jnp.float32)

    def step(k, carry):
        at = pl.ds(pl.multiple_of(k * BLOCK, BLOCK), BLOCK)

        def load(i):
            return work[pl.ds(pl.multiple_of(k * BLOCK + SUB * i, SUB), SUB), at]

        def store(i, upper, lower):
            block_u[SUB * i : SUB * (i + 1), :] = upper
            block_w[SUB * i : SUB * (i + 1), :] = lower

        factor_block(load, store)
        inverse = block_w[...]
        u_ref[at, :] = dot(inverse, work[at, :], ((1,), (0,)))
        u_ref[at, at] = block_u[...]
        row = lax.broadcasted_iota(jnp.int32, (BLOCK, BLOCK), 0)
        col = lax.broadcasted_iota(jnp.int32, (BLOCK, BLOCK), 1)
        w_ref[at, at] = (row == col).astype(jnp.float32)
        w_ref[at, :] = dot(inverse, w_ref[at, :], ((1,), (0,)))

        def update(i, carry):
            to = pl.ds(pl.multiple_of(i * BLOCK, BLOCK), BLOCK)
            weight = u_ref[at, to]
            work[to, :] = work[to, :] - dot(weight, u_ref[at, :], ((0,), (0,)))
            w_ref[to, :] = w_ref[to, :] - dot(weight, w_ref[at, :], ((0,), (0,)))
            return carry

        lax.fori_loop(k + 1, count, update, 0)
        return carry

    lax.fori_loop(0, count, step, 0)


def factorize(lead):
    shape = jax.ShapeDtypeStruct((LEAD, LEAD), jnp.float32)
    vmem = pl.BlockSpec(memory_space=pltpu.VMEM)
    return pl.pallas_call(
        factor_kernel,
        out_shape=(shape, shape),
        in_specs=[vmem],
        out_specs=(vmem, vmem),
        scratch_shapes=[
            pltpu.VMEM((LEAD, LEAD), jnp.float32),
            pltpu.VMEM((BLOCK, BLOCK), jnp.float32),
            pltpu.VMEM((BLOCK, BLOCK), jnp.float32),
        ],
        compiler_params=pltpu.CompilerParams(vmem_limit_bytes=40 * 2**20),
        cost_estimate=pl.CostEstimate(flops=2 * 10**10, bytes_accessed=10**7, transcendentals=0),
    )(lead)


def gather(value, axis, groups):
    copies = jnp.broadcast_to(value[None], (len(groups[0]),) + value.shape)
    return lax.all_to_all(copies, axis, 0, 0, axis_index_groups=groups)


def choose(index, values, start):
    out = jnp.zeros_like(values[0])
    for i, value in enumerate(values):
        out = jnp.where(index == start + i, value, out)
    return out


def on_device(matrix):
    r = lax.axis_index("row")
    c = lax.axis_index("col")
    y, z, core = r // 4, c // 2, c % 2
    half = 512

    first_cols = matrix[:, :TILE]
    first_rows = matrix[:TILE, :]
    keep = lax.dynamic_slice_in_dim(first_cols, core * half, half, 0)
    give = lax.dynamic_slice_in_dim(first_cols, (1 - core) * half, half, 0)
    got = lax.ppermute(give, "col", CORE_SWAP)
    panel_even = jnp.where(core == 0, keep, got)
    panel_odd = jnp.where(core == 0, got, keep)

    column_quarters = [first_rows[:, TILE * s : TILE * (s + 1)] for s in range(4)]
    corner = matrix[:TILE, :TILE]
    message = [jnp.concatenate([column_quarters[s], corner[64 * s : 64 * (s + 1)]]) for s in range(4)]
    arrived = [
        lax.ppermute(message[s], "row", [(x, 4 * s + x) for x in range(3)]) for s in range(1, 4)
    ]
    mine = choose(y, [message[0]] + arrived, 0)
    my_quarter, my_corner = mine[:TILE], mine[TILE:]

    keep = lax.dynamic_slice_in_dim(my_corner, core * 32, 32, 0)
    give = lax.dynamic_slice_in_dim(my_corner, (1 - core) * 32, 32, 0)
    got = lax.ppermute(give, "col", CORE_SWAP)
    even = jnp.where(core == 0, keep, got)
    odd = jnp.where(core == 0, got, keep)
    pair = jnp.stack([even, odd])
    across = lax.ppermute(pair, "col", [(0, 2), (1, 3), (2, 0), (3, 1)])
    zero_side = jnp.where(z == 0, pair, across)
    one_side = jnp.where(z == 0, across, pair)
    three = jnp.concatenate([zero_side, one_side[:1]])
    got = lax.ppermute(three, "col", [(0, 8), (1, 9), (2, 10), (3, 11)])
    three = jnp.where(z < 2, three, got)
    got = lax.ppermute(
        three, "col", [(c0 + d, c0 + d + 4) for c0 in (0, 8) for d in range(4)]
    )
    three = jnp.where(z % 4 < 2, three, got)
    lead_x = gather(three, "row", X_GROUPS)[:3]
    lead_half = gather(lead_x, "row", Y_GROUPS)
    lead_other = lax.ppermute(lead_half, "col", CORE_SWAP)
    lead = jnp.stack(
        [jnp.where(core == 0, lead_half, lead_other), jnp.where(core == 0, lead_other, lead_half)]
    )
    lead = lead.transpose(2, 1, 0, 4, 3, 5).reshape(LEAD, LEAD)

    columns_x = gather(my_quarter, "row", X_GROUPS)[:3]
    columns = gather(columns_x, "row", Y_GROUPS)
    columns = columns.transpose(1, 2, 0, 3).reshape(LEAD, 4 * TILE)

    def chunk(panel, i):
        return lax.slice_in_dim(panel, 64 * i, 64 * (i + 1))

    arrived = []
    for t in range(1, 8):
        at_zero = jnp.stack([chunk(panel_even, t), chunk(panel_odd, t)])
        one = (t + 1) % 8
        at_one = jnp.stack([chunk(panel_even, one), chunk(panel_odd, one)])
        pairs = [(core0 + 2 * z0, core0 + 2 * ((z0 + t) % 8)) for core0 in range(2) for z0 in range(2)]
        arrived.append(lax.ppermute(jnp.where(z == 0, at_zero, at_one), "col", pairs))
    own_zero = jnp.stack([chunk(panel_even, 0), chunk(panel_odd, 0)])
    own_one = chunk(panel_even, 1)
    from_zero = choose(z, [own_zero] + arrived, 0)
    from_one = choose((z + 7) % 8, [own_one] + [a[0] for a in arrived], 0)
    my_chunk = jnp.concatenate([from_zero, from_one[None]])
    rows_half = gather(my_chunk, "col", Z_GROUPS)
    rows_other = lax.ppermute(rows_half, "col", CORE_SWAP)
    rows = jnp.stack(
        [jnp.where(core == 0, rows_half, rows_other), jnp.where(core == 0, rows_other, rows_half)]
    )
    rows = rows.transpose(0, 1, 3, 2, 4).reshape(4 * TILE, LEAD)

    upper, inverse = factorize(lead)
    panel = dot(rows, inverse, ((1,), (1,)), lax.Precision.HIGHEST)
    across = dot(inverse, columns, ((1,), (0,)), lax.Precision.HIGHEST)
    out = matrix - dot(panel, across, ((1,), (0,)), lax.Precision.HIGHEST)

    at = jnp.minimum(c, 2) * TILE
    solved = lax.dynamic_slice_in_dim(panel, at, TILE, 1)
    out = out.at[:, :TILE].set(jnp.where(c < 3, solved, out[:, :TILE]))
    diagonal = lax.dynamic_slice(upper, (at, jnp.minimum(r, 2) * TILE), (TILE, TILE)).T
    below = jnp.tril(jnp.ones((TILE, TILE), bool))
    corner = jnp.where((c < r) | ((c == r) & below), diagonal, 0.0)
    top = jnp.concatenate([corner, jnp.zeros((TILE, 3 * TILE), jnp.float32)], axis=1)
    return out.at[:TILE].set(jnp.where(r < 3, jnp.where(c < 3, top, 0.0), out[:TILE]))


def solution(mesh):
    placed = (P("row", "col"),)
    return jax.shard_map(
        on_device, mesh=mesh, in_specs=placed, out_specs=P("row", "col"), check_vma=False
    )
```

time: 1200 us -> 287 us (0.24)
  waiting for transfers between devices: 915 us -> 68.9 us
  other arithmetic: 186 us -> 15.2 us
  starting transfers between devices: 0.95 us -> 83.7 us
  Pallas kernels: 0 us -> 47.5 us
  between operations: 18.1 us -> 1 us
    psum x9 -> x0, waiting for transfers between devices: 915 us -> none  [from_root(): return lax.psum(jnp.where(mine, array, jnp.zeros_like(array)), axis)]
    another operation x28 -> x5, other arithmetic: 165 us -> 4.42 us  [the longest x1 2.26 us: on_device(): jnp.stack([jnp.where(core == 0, rows_half, rows_other), jnp.where(core ==...]
    ppermute x0 -> x17, starting transfers between devices: none -> 55.2 us  [the longest x7 21.1 us: on_device(): lax.ppermute(jnp.where(z == 0, at_zero, at_one), 'col', pairs)]
    pallas_call x0 -> x1, Pallas kernels: none -> 47.5 us  [factorize(): pl.pallas_call(factor_kernel, out_shape=(shape, shape), in_specs=[vmem],...]
    all_to_all x0 -> x5, waiting for transfers between devices: none -> 47.2 us  [gather(): return lax.all_to_all(copies, axis, 0, 0, axis_index_groups=groups)]
    all_to_all x0 -> x5, starting transfers between devices: none -> 28.5 us  [gather(): return lax.all_to_all(copies, axis, 0, 0, axis_index_groups=groups)]
    ppermute x0 -> x17, waiting for transfers between devices: none -> 21.6 us  [the longest x3 12 us: on_device(): lax.ppermute(message[s], 'row', [(x, 4 * s + x) for x in range(3)])]
    another operation x55 -> x1, local copies, waits for them, and re-layouts: 13.6 us -> 0.87 us  [on_device(): at_one = jnp.stack([chunk(panel_even, one), chunk(panel_odd, one)])]
  transfers between devices with their start and end apart: 9 -> 22, of which waited for: 9 -> 13; matrix products, arithmetic and copies ran while one was open for 0% -> 12% of each run, Pallas kernels for 0% -> 17%
where the time goes in v1:
time: 287 us; the launch traced here: 285 us
  starting transfers between devices  83.7 us (29%)
  waiting for transfers between devices  68.9 us (24%)
  Pallas kernels  47.5 us (17%)
  local copies, waits for them, and re-layouts  37.3 us (13%)
  matrix products  31.3 us (11%)
  other arithmetic  15.2 us (5%)
    pallas_call x1, Pallas kernels, factorize(): pl.pallas_call(factor_kernel, out_shape=(shape, shape), in_specs=[vmem],...  47.5 us
    all_to_all x5, waiting for transfers between devices, gather(): return lax.all_to_all(copies, axis, 0, 0, axis_index_groups=groups)  47.2 us
    dot_general x3, matrix products, dot(): lax.dot_general(left, right, (dims, ((), ())), precision=precision, prefe...  31.3 us
    all_to_all x5, starting transfers between devices, gather(): return lax.all_to_all(copies, axis, 0, 0, axis_index_groups=groups)  28.5 us
    ppermute x7, starting transfers between devices, on_device(): lax.ppermute(jnp.where(z == 0, at_zero, at_one), 'col', pairs)  21.1 us
    ppermute x1, starting transfers between devices, on_device(): rows_other = lax.ppermute(rows_half, 'col', CORE_SWAP)  12.6 us
    ppermute x3, waiting for transfers between devices, on_device(): lax.ppermute(message[s], 'row', [(x, 4 * s + x) for x in range(3)])  12 us
    unnamed x19, local copies, waits for them, and re-layouts  12 us
  transfers between devices with their start and end apart: 22, of which 13 were waited for; matrix products, arithmetic and copies ran while one was open for 12% of the time, Pallas kernels for 17%

profile of v1, /device:TPU:1, one launch (start us, length us, event | category | flops | bytes accessed | tf_op | source)
XLA Modules:
  0.0 284.8 jit_solution(5589759392294761970)
XLA Ops:
  2.3 5.5 %collective-permute-start.9 = (f32[320,256]{1,0:T(8,128)S(1)}, f32[320,256]{1,0:T(8,128)S(1)}, u32[]{:S(2)}, u32[]{:S(2)}) collective-permute-start(f32[320,256]{1,0:T(8,128)S(1)} %pad_maximum_fusion), channel_id=1, source_target_pairs={{0,192},{16,208},{32,224},{1,193},{17,209},{33,225},{2,194},{18,21... | collective-permute-start | bytes 983048 | tf_op jit(solution)/shard_map/ppermute | solution.py:160
  7.8 1.3 collective-permute-start.10
  9.2 1.3 collective-permute-start.11
  10.5 3.6 %collective-permute-done.9 = f32[320,256]{1,0:T(8,128)S(1)} collective-permute-done((f32[320,256]{1,0:T(8,128)S(1)}, f32[320,256]{1,0:T(8,128)S(1)}, u32[]{:S(2)}, u32[]{:S(2)}) %collective-permute-start.9) | collective-permute-done | bytes 327712 | tf_op jit(solution)/shard_map/ppermute | solution.py:160
  14.1 1.3 collective-permute-done.10
  15.5 7.0 %collective-permute-done.11 = f32[320,256]{1,0:T(8,128)S(1)} collective-permute-done((f32[320,256]{1,0:T(8,128)S(1)}, f32[320,256]{1,0:T(8,128)S(1)}, u32[]{:S(2)}, u32[]{:S(2)}) %collective-permute-start.11) | collective-permute-done | bytes 327712 | tf_op jit(solution)/shard_map/ppermute | solution.py:160
  22.6 1.6 collective-permute-start.12
  25.1 3.5 %collective-permute-start.13 = (f32[2,32,256]{2,1,0:T(8,128)S(1)}, f32[2,32,256]{2,1,0:T(8,128)S(1)}, u32[]{:S(2)}, u32[]{:S(2)}) collective-permute-start(f32[2,32,256]{2,1,0:T(8,128)S(1)} %pad_maximum_fusion.12), channel_id=1, source_target_pairs={{0,2},{1,3},{2,0},{3,1},{16,18},{17,19},{18,16},{19,17},{32,34},{3... | collective-permute-start | bytes 196616 | tf_op jit(solution)/shard_map/ppermute | solution.py:171
  28.7 2.0 collective-permute-done.13
  30.8 3.9 %collective-permute-start.14 = (f32[3,32,256]{2,1,0:T(8,128)S(1)}, f32[3,32,256]{2,1,0:T(8,128)S(1)}, u32[]{:S(2)}, u32[]{:S(2)}) collective-permute-start(f32[3,32,256]{2,1,0:T(8,128)S(1)} %pad_maximum_fusion.11), channel_id=1, source_target_pairs={{0,8},{1,9},{2,10},{3,11},{16,24},{17,25},{18,26},{19,27},{32,40},... | collective-permute-start | bytes 294920 | tf_op jit(solution)/shard_map/ppermute | solution.py:175
  34.7 1.8 collective-permute-done.14
  36.5 1.3 collective-permute-start.15
  37.8 1.3 slice.176
  40.2 4.0 %all-to-all-start.1 = ((f32[4,3,32,256]{3,2,1,0:T(8,128)}), f32[4,3,32,256]{3,2,1,0:T(8,128)S(1)}, u32[]{:S(2)}, u32[]{:S(2)}) async-start(f32[4,3,32,256]{3,2,1,0:T(8,128)} %broadcast_in_dim.59), calls=%async_computation.1 | async-start | bytes 786432 | tf_op jit(solution)/shard_map/all_to_all | solution.py:132
  44.3 2.1 collective-permute-start
  46.4 4.0 %all-to-all-done.1 = f32[4,3,32,256]{3,2,1,0:T(8,128)S(1)} async-done(((f32[4,3,32,256]{3,2,1,0:T(8,128)}), f32[4,3,32,256]{3,2,1,0:T(8,128)S(1)}, u32[]{:S(2)}, u32[]{:S(2)}) %all-to-all-start.1) | async-done | bytes 393248 | tf_op jit(solution)/shard_map/all_to_all | solution.py:132
  51.5 3.5 %all-to-all-start.3 = ((f32[4,256,256]{2,1,0:T(8,128)}), f32[4,256,256]{2,1,0:T(8,128)S(1)}, u32[]{:S(2)}, u32[]{:S(2)}) async-start(f32[4,256,256]{2,1,0:T(8,128)} %broadcast_in_dim.61), calls=%async_computation.3 | async-start | bytes 2097152 | tf_op jit(solution)/shard_map/all_to_all | solution.py:132
  57.1 9.5 %all-to-all-done.3 = f32[4,256,256]{2,1,0:T(8,128)S(1)} async-done(((f32[4,256,256]{2,1,0:T(8,128)}), f32[4,256,256]{2,1,0:T(8,128)S(1)}, u32[]{:S(2)}, u32[]{:S(2)}) %all-to-all-start.3) | async-done | bytes 1048608 | tf_op jit(solution)/shard_map/all_to_all | solution.py:132
  67.8 3.5 %all-to-all-start.2 = ((f32[4,3,3,32,256]{4,3,2,1,0:T(8,128)}), f32[4,3,3,32,256]{4,3,2,1,0:T(8,128)S(1)}, u32[]{:S(2)}, u32[]{:S(2)}) async-start(f32[4,3,3,32,256]{4,3,2,1,0:T(8,128)} %broadcast_in_dim.60), calls=%async_computation.2 | async-start | bytes 2359296 | tf_op jit(solution)/shard_map/all_to_all | solution.py:132
  72.2 12.1 %collective-permute-start.1 = (f32[2,64,256]{2,1,0:T(8,128)S(1)}, f32[2,64,256]{2,1,0:T(8,128)S(1)}, u32[]{:S(2)}, u32[]{:S(2)}) collective-permute-start(f32[2,64,256]{2,1,0:T(8,128)S(1)} %get-tuple-element.63), channel_id=1, source_target_pairs={{0,14},{2,0},{1,15},{3,1},{16,30},{18,16},{17,31},{19,17},{32,46},... | collective-permute-start | bytes 393224 | tf_op jit(solution)/shard_map/ppermute | solution.py:202
  84.2 1.3 collective-permute-start.2
  85.5 1.3 collective-permute-start.3
  86.9 1.3 collective-permute-start.4
  88.2 1.8 fusion.8
  91.2 1.9 collective-permute-start.6
  93.2 3.1 %collective-permute-done.2 = f32[2,64,256]{2,1,0:T(8,128)S(1)} collective-permute-done((f32[2,64,256]{2,1,0:T(8,128)S(1)}, f32[2,64,256]{2,1,0:T(8,128)S(1)}, u32[]{:S(2)}, u32[]{:S(2)}) %collective-permute-start.2) | collective-permute-done | bytes 131104 | tf_op jit(solution)/shard_map/ppermute | solution.py:202
  96.3 1.9 collective-permute-start.7
  100.8 1.4 broadcast_in_dim.30
  102.2 12.8 %all-to-all-start = ((f32[8,3,64,256]{3,2,1,0:T(8,128)}), f32[8,3,64,256]{3,2,1,0:T(8,128)}, u32[]{:S(2)}, u32[]{:S(2)}) async-start(f32[8,3,64,256]{3,2,1,0:T(8,128)} %broadcast_in_dim.30), calls=%async_computation | async-start | bytes 3145728 | tf_op jit(solution)/shard_map/all_to_all | solution.py:132
  115.8 5.3 %copy.18 = f32[1024,1024]{0,1:T(8,128)} copy(f32[1024,1024]{1,0:T(8,128)} %param.5) | data formatting | bytes 8388608 | tf_op args[0]
  121.9 33.7 %all-to-all-done = f32[8,3,64,256]{3,2,1,0:T(8,128)} async-done(((f32[8,3,64,256]{3,2,1,0:T(8,128)}), f32[8,3,64,256]{3,2,1,0:T(8,128)}, u32[]{:S(2)}, u32[]{:S(2)}) %all-to-all-start) | async-done | bytes 1572896 | tf_op jit(solution)/shard_map/all_to_all | solution.py:132
  155.5 2.0 broadcast_in_dim.62
  157.5 4.7 %all-to-all-start.4 = ((f32[4,3,256,256]{3,2,1,0:T(8,128)}), f32[4,3,256,256]{3,2,1,0:T(8,128)}, u32[]{:S(2)}, u32[]{:S(2)}) async-start(f32[4,3,256,256]{3,2,1,0:T(8,128)} %broadcast_in_dim.62), calls=%async_computation.4 | async-start | bytes 6291456 | tf_op jit(solution)/shard_map/all_to_all | solution.py:132
  162.2 1.5 select_bitcast_fusion.3
  163.8 1.8 copy.16
  166.1 12.6 %collective-permute-start.8 = (f32[8,3,64,256]{3,2,1,0:T(8,128)}, f32[8,3,64,256]{3,2,1,0:T(8,128)}, u32[]{:S(2)}, u32[]{:S(2)}) collective-permute-start(f32[8,3,64,256]{3,2,1,0:T(8,128)} %all-to-all-done), channel_id=1, source_target_pairs={{0,1},{1,0},{2,3},{3,2},{4,5},{5,4},{6,7},{7,6},{8,9},{9,8},{10,11... | collective-permute-start | bytes 4718600 | tf_op jit(solution)/shard_map/ppermute | solution.py:209
  178.8 47.5 %shard_map.17 = (f32[768,768]{1,0:T(8,128)S(1)}, f32[768,768]{1,0:T(8,128)S(1)}) custom-call(f32[768,768]{1,0:T(8,128)S(1)} %bitcast.110), custom_call_target="tpu_custom_call" | custom-call | flops 20000000000 | bytes 10000000 | tf_op jit(solution)/shard_map/pallas_call | solution.py:115
  226.3 3.9 %copy.17 = f32[3,256,4,256]{3,2,1,0:T(4,128)S(1)} copy(f32[3,256,4,256]{3,1,0,2:T(8,128)} %bitcast.32) | data formatting | bytes 6291456 | tf_op jit(solution)/shard_map/transpose | solution.py:191
  231.0 9.3 %fusion.26 = f32[768,1024]{1,0:T(8,128)} fusion(f32[768,768]{1,0:T(8,128)S(1)} %get-tuple-element.31, f32[768,1024]{1,0:T(8,128)S(1)} %bitcast.113), kind=kOutput, calls=%fused_computation.89 | convolution fusion | flops 7247757312 | bytes 8650752 | tf_op jit(solution)/shard_map/dot_general | solution.py:23
  240.3 2.3 select_bitcast_fusion.1
  242.9 2.4 copy.15
  246.1 7.9 %fusion.25 = f32[1024,768]{1,0:T(8,128)S(1)} fusion(f32[1024,768]{1,0:T(8,128)S(1)} %bitcast.112, f32[768,768]{1,0:T(8,128)S(1)} %get-tuple-element.31), kind=kOutput, calls=%fused_computation.88 | convolution fusion | flops 7247757312 | bytes 8650752 | tf_op jit(solution)/shard_map/dot_general | solution.py:23
  254.0 1.6 copy-done
  256.7 2.9 %copy.23 = f32[1024,256]{0,1:T(8,128)} copy(f32[1024,256]{1,0:T(8,128)} %constant_dynamic-slice_fusion) | data formatting | bytes 2097152
  259.6 14.0 %convolution_subtract_fusion = f32[1024,1024]{0,1:T(8,128)} fusion(f32[1024,1024]{0,1:T(8,128)} %copy.18, f32[1024,768]{1,0:T(8,128)} %copy-done, f32[768,1024]{1,0:T(8,128)S(1)} %copy-done.1), kind=kOutput, calls=%fused_computation.2 | convolution fusion | flops 9664724992 | bytes 14680064 | tf_op jit(solution)/shard_map/dot_general | solution.py:23
  273.7 3.0 %fusion = f32[1024,1024]{0,1:T(8,128)} fusion(f32[1024,1024]{0,1:T(8,128)} %convolution_subtract_fusion, f32[1024,256]{0,1:T(8,128)S(1)} %copy-done.2, pred[]{:T(512)S(6)} %lt.58, pred[]{:T(512)} %compare_reduce_fusion), kind=kLoop, calls=%fused_computation.8 | loop fusion | flops 524288 | bytes 3146241 | tf_op jit(solution)/shard_map/scatter | solution.py:222
  276.7 2.3 fusion.1
  279.0 5.3 %copy.21 = f32[1024,1024]{1,0:T(8,128)} copy(f32[1024,1024]{0,1:T(8,128)} %fusion.1) | data formatting | bytes 8388608 | tf_op jit(solution)/shard_map/scatter | solution.py:227
  (64 shorter events, 18.6 us)
Async XLA Ops:
  2.3 11.8 %collective-permute-start.9 = (f32[320,256]{1,0:T(8,128)S(1)}, f32[320,256]{1,0:T(8,128)S(1)}, u32[]{:S(2)}, u32[]{:S(2)}) collective-permute-start(f32[320,256]{1,0:T(8,128)S(1)} %pad_maximum_fusion), channel_id=1, source_target_pairs={{0,192},{16,208},{32,224},{1,193},{17,209},{33,225},{2,194},{18,21... | collective-permute-start | bytes 983048 | tf_op jit(solution)/shard_map/ppermute | solution.py:160
  7.8 7.7 %collective-permute-start.10 = (f32[320,256]{1,0:T(8,128)S(1)}, f32[320,256]{1,0:T(8,128)S(1)}, u32[]{:S(2)}, u32[]{:S(2)}) collective-permute-start(f32[320,256]{1,0:T(8,128)S(1)} %pad_maximum_fusion.1), channel_id=1, source_target_pairs={{0,128},{16,144},{32,160},{1,129},{17,145},{33,161},{2,130},{18,14... | collective-permute-start | bytes 983048 | tf_op jit(solution)/shard_map/ppermute | solution.py:160
  9.2 13.3 %collective-permute-start.11 = (f32[320,256]{1,0:T(8,128)S(1)}, f32[320,256]{1,0:T(8,128)S(1)}, u32[]{:S(2)}, u32[]{:S(2)}) collective-permute-start(f32[320,256]{1,0:T(8,128)S(1)} %pad_maximum_fusion.2), channel_id=1, source_target_pairs={{0,64},{16,80},{32,96},{1,65},{17,81},{33,97},{2,66},{18,82},{34,9... | collective-permute-start | bytes 983048 | tf_op jit(solution)/shard_map/ppermute | solution.py:160
  22.6 2.5 collective-permute-start.12
  25.1 5.6 %collective-permute-start.13 = (f32[2,32,256]{2,1,0:T(8,128)S(1)}, f32[2,32,256]{2,1,0:T(8,128)S(1)}, u32[]{:S(2)}, u32[]{:S(2)}) collective-permute-start(f32[2,32,256]{2,1,0:T(8,128)S(1)} %pad_maximum_fusion.12), channel_id=1, source_target_pairs={{0,2},{1,3},{2,0},{3,1},{16,18},{17,19},{18,16},{19,17},{32,34},{3... | collective-permute-start | bytes 196616 | tf_op jit(solution)/shard_map/ppermute | solution.py:171
  30.8 5.7 %collective-permute-start.14 = (f32[3,32,256]{2,1,0:T(8,128)S(1)}, f32[3,32,256]{2,1,0:T(8,128)S(1)}, u32[]{:S(2)}, u32[]{:S(2)}) collective-permute-start(f32[3,32,256]{2,1,0:T(8,128)S(1)} %pad_maximum_fusion.11), channel_id=1, source_target_pairs={{0,8},{1,9},{2,10},{3,11},{16,24},{17,25},{18,26},{19,27},{32,40},... | collective-permute-start | bytes 294920 | tf_op jit(solution)/shard_map/ppermute | solution.py:175
  36.5 2.9 %collective-permute-start.15 = (f32[3,32,256]{2,1,0:T(8,128)S(1)}, f32[3,32,256]{2,1,0:T(8,128)S(1)}, u32[]{:S(2)}, u32[]{:S(2)}) collective-permute-start(f32[3,32,256]{2,1,0:T(8,128)S(1)} %broadcast_select_fusion), channel_id=1, source_target_pairs={{0,4},{1,5},{2,6},{3,7},{8,12},{9,13},{10,14},{11,15},{16,20},{17,... | collective-permute-start | bytes 294920 | tf_op jit(solution)/shard_map/ppermute | solution.py:177
  40.2 10.2 %all-to-all-start.1 = ((f32[4,3,32,256]{3,2,1,0:T(8,128)}), f32[4,3,32,256]{3,2,1,0:T(8,128)S(1)}, u32[]{:S(2)}, u32[]{:S(2)}) async-start(f32[4,3,32,256]{3,2,1,0:T(8,128)} %broadcast_in_dim.59), calls=%async_computation.1 | async-start | bytes 786432 | tf_op jit(solution)/shard_map/all_to_all | solution.py:132
  44.3 10.8 %collective-permute-start = (f32[512,256]{1,0:T(8,128)S(1)}, f32[512,256]{1,0:T(8,128)}, u32[]{:S(2)}, u32[]{:S(2)}) collective-permute-start(f32[512,256]{1,0:T(8,128)S(1)} %constant_dynamic-slice_fusion.2), channel_id=1, source_target_pairs={{0,1},{1,0},{2,3},{3,2},{4,5},{5,4},{6,7},{7,6},{8,9},{9,8},{10,11... | collective-permute-start | bytes 1572872 | tf_op jit(solution)/shard_map/ppermute | solution.py:152
  51.5 15.1 %all-to-all-start.3 = ((f32[4,256,256]{2,1,0:T(8,128)}), f32[4,256,256]{2,1,0:T(8,128)S(1)}, u32[]{:S(2)}, u32[]{:S(2)}) async-start(f32[4,256,256]{2,1,0:T(8,128)} %broadcast_in_dim.61), calls=%async_computation.3 | async-start | bytes 2097152 | tf_op jit(solution)/shard_map/all_to_all | solution.py:132
  57.1 14.3 %copy-start.3 = (f32[1,64,256]{2,1,0:T(8,128)S(1)}, f32[1,64,256]{2,1,0:T(8,128)}, u32[]{:S(2)}) copy-start(f32[1,64,256]{2,1,0:T(8,128)} %get-tuple-element.62) | copy-start | bytes 196612
  57.1 14.3 %copy-start.4 = (f32[1,64,256]{2,1,0:T(8,128)S(1)}, f32[1,64,256]{2,1,0:T(8,128)}, u32[]{:S(2)}) copy-start(f32[1,64,256]{2,1,0:T(8,128)} %get-tuple-element.72) | copy-start | bytes 196612
  57.1 14.3 %copy-start.5 = (f32[1,64,256]{2,1,0:T(8,128)S(1)}, f32[1,64,256]{2,1,0:T(8,128)}, u32[]{:S(2)}) copy-start(f32[1,64,256]{2,1,0:T(8,128)} %get-tuple-element.73) | copy-start | bytes 196612
  57.1 14.3 %copy-start.6 = (f32[1,64,256]{2,1,0:T(8,128)S(1)}, f32[1,64,256]{2,1,0:T(8,128)}, u32[]{:S(2)}) copy-start(f32[1,64,256]{2,1,0:T(8,128)} %get-tuple-element.74) | copy-start | bytes 196612
  67.8 33.0 %all-to-all-start.2 = ((f32[4,3,3,32,256]{4,3,2,1,0:T(8,128)}), f32[4,3,3,32,256]{4,3,2,1,0:T(8,128)S(1)}, u32[]{:S(2)}, u32[]{:S(2)}) async-start(f32[4,3,3,32,256]{4,3,2,1,0:T(8,128)} %broadcast_in_dim.60), calls=%async_computation.2 | async-start | bytes 2359296 | tf_op jit(solution)/shard_map/all_to_all | solution.py:132
  72.2 19.1 %collective-permute-start.1 = (f32[2,64,256]{2,1,0:T(8,128)S(1)}, f32[2,64,256]{2,1,0:T(8,128)S(1)}, u32[]{:S(2)}, u32[]{:S(2)}) collective-permute-start(f32[2,64,256]{2,1,0:T(8,128)S(1)} %get-tuple-element.63), channel_id=1, source_target_pairs={{0,14},{2,0},{1,15},{3,1},{16,30},{18,16},{17,31},{19,17},{32,46},... | collective-permute-start | bytes 393224 | tf_op jit(solution)/shard_map/ppermute | solution.py:202
  84.2 12.0 %collective-permute-start.2 = (f32[2,64,256]{2,1,0:T(8,128)S(1)}, f32[2,64,256]{2,1,0:T(8,128)S(1)}, u32[]{:S(2)}, u32[]{:S(2)}) collective-permute-start(f32[2,64,256]{2,1,0:T(8,128)S(1)} %get-tuple-element.64), channel_id=1, source_target_pairs={{0,12},{2,14},{1,13},{3,15},{16,28},{18,30},{17,29},{19,31},{32,44... | collective-permute-start | bytes 393224 | tf_op jit(solution)/shard_map/ppermute | solution.py:202
  85.5 13.8 %collective-permute-start.3 = (f32[2,64,256]{2,1,0:T(8,128)}, f32[2,64,256]{2,1,0:T(8,128)S(1)}, u32[]{:S(2)}, u32[]{:S(2)}) collective-permute-start(f32[2,64,256]{2,1,0:T(8,128)} %get-tuple-element.65), channel_id=1, source_target_pairs={{0,10},{2,12},{1,11},{3,13},{16,26},{18,28},{17,27},{19,29},{32,42... | collective-permute-start | bytes 393224 | tf_op jit(solution)/shard_map/ppermute | solution.py:202
  86.9 12.5 %collective-permute-start.4 = (f32[2,64,256]{2,1,0:T(8,128)}, f32[2,64,256]{2,1,0:T(8,128)S(1)}, u32[]{:S(2)}, u32[]{:S(2)}) collective-permute-start(f32[2,64,256]{2,1,0:T(8,128)} %get-tuple-element.66), channel_id=1, source_target_pairs={{0,8},{2,10},{1,9},{3,11},{16,24},{18,26},{17,25},{19,27},{32,40},... | collective-permute-start | bytes 393224 | tf_op jit(solution)/shard_map/ppermute | solution.py:202
  89.9 9.4 %collective-permute-start.5 = (f32[2,64,256]{2,1,0:T(8,128)}, f32[2,64,256]{2,1,0:T(8,128)S(1)}, u32[]{:S(2)}, u32[]{:S(2)}) collective-permute-start(f32[2,64,256]{2,1,0:T(8,128)} %get-tuple-element.67), channel_id=1, source_target_pairs={{0,6},{2,8},{1,7},{3,9},{16,22},{18,24},{17,23},{19,25},{32,38},{3... | collective-permute-start | bytes 393224 | tf_op jit(solution)/shard_map/ppermute | solution.py:202
  91.2 8.1 %collective-permute-start.6 = (f32[2,64,256]{2,1,0:T(8,128)}, f32[2,64,256]{2,1,0:T(8,128)}, u32[]{:S(2)}, u32[]{:S(2)}) collective-permute-start(f32[2,64,256]{2,1,0:T(8,128)} %get-tuple-element.68), channel_id=1, source_target_pairs={{0,4},{2,6},{1,5},{3,7},{16,20},{18,22},{17,21},{19,23},{32,36},{3... | collective-permute-start | bytes 393224 | tf_op jit(solution)/shard_map/ppermute | solution.py:202
  96.3 3.5 %collective-permute-start.7 = (f32[2,64,256]{2,1,0:T(8,128)}, f32[2,64,256]{2,1,0:T(8,128)}, u32[]{:S(2)}, u32[]{:S(2)}) collective-permute-start(f32[2,64,256]{2,1,0:T(8,128)} %get-tuple-element.69), channel_id=1, source_target_pairs={{0,2},{2,4},{1,3},{3,5},{16,18},{18,20},{17,19},{19,21},{32,34},{3... | collective-permute-start | bytes 393224 | tf_op jit(solution)/shard_map/ppermute | solution.py:202
  102.2 53.3 %all-to-all-start = ((f32[8,3,64,256]{3,2,1,0:T(8,128)}), f32[8,3,64,256]{3,2,1,0:T(8,128)}, u32[]{:S(2)}, u32[]{:S(2)}) async-start(f32[8,3,64,256]{3,2,1,0:T(8,128)} %broadcast_in_dim.30), calls=%async_computation | async-start | bytes 3145728 | tf_op jit(solution)/shard_map/all_to_all | solution.py:132
  115.0 47.2 %collective-permute-start.16 = (f32[4,3,3,32,256]{4,3,2,1,0:T(8,128)S(1)}, f32[4,3,3,32,256]{4,3,2,1,0:T(8,128)}, u32[]{:S(2)}, u32[]{:S(2)}) collective-permute-start(f32[4,3,3,32,256]{4,3,2,1,0:T(8,128)S(1)} %all-to-all-done.2), channel_id=1, source_target_pairs={{0,1},{1,0},{2,3},{3,2},{4,5},{5,4},{6,7},{7,6},{8,9},{9,8},{10,11... | collective-permute-start | bytes 3538952 | tf_op jit(solution)/shard_map/ppermute | solution.py:183
  157.5 68.8 %all-to-all-start.4 = ((f32[4,3,256,256]{3,2,1,0:T(8,128)}), f32[4,3,256,256]{3,2,1,0:T(8,128)}, u32[]{:S(2)}, u32[]{:S(2)}) async-start(f32[4,3,256,256]{3,2,1,0:T(8,128)} %broadcast_in_dim.62), calls=%async_computation.4 | async-start | bytes 6291456 | tf_op jit(solution)/shard_map/all_to_all | solution.py:132
  166.1 74.2 %collective-permute-start.8 = (f32[8,3,64,256]{3,2,1,0:T(8,128)}, f32[8,3,64,256]{3,2,1,0:T(8,128)}, u32[]{:S(2)}, u32[]{:S(2)}) collective-permute-start(f32[8,3,64,256]{3,2,1,0:T(8,128)} %all-to-all-done), channel_id=1, source_target_pairs={{0,1},{1,0},{2,3},{3,2},{4,5},{5,4},{6,7},{7,6},{8,9},{9,8},{10,11... | collective-permute-start | bytes 4718600 | tf_op jit(solution)/shard_map/ppermute | solution.py:209
  254.0 1.6 copy-start
  255.7 4.0 %copy-start.1 = (f32[768,1024]{1,0:T(8,128)S(1)}, f32[768,1024]{1,0:T(8,128)}, u32[]{:S(2)}) copy-start(f32[768,1024]{1,0:T(8,128)} %fusion.26) | copy-start | bytes 9437188
  259.6 14.0 %copy-start.2 = (f32[1024,256]{0,1:T(8,128)S(1)}, f32[1024,256]{0,1:T(8,128)}, u32[]{:S(2)}) copy-start(f32[1024,256]{0,1:T(8,128)} %copy.23) | copy-start | bytes 3145732

commit v2 on v0

v2 whole, which is shorter than its diff:
```python
import jax
import jax.numpy as jnp
from jax import lax
from jax.experimental import pallas as pl
from jax.experimental.pallas import tpu as pltpu
from jax.sharding import PartitionSpec as P

TILE = 256
STEPS = 3
LEAD = TILE * STEPS
BLOCK = 128
SUB = 8
FULL = lax.Precision.HIGHEST

ROW_GROUP = [list(range(16))]
Z_GROUPS = [[2 * z + core for z in range(8)] for core in range(2)]
CORE_SWAP = [(c, c ^ 1) for c in range(16)]
NEAR = [(0, 2), (1, 3), (2, 0), (3, 1)]
EXCHANGE = [(2 * z + k, 2 * (z ^ 1) + k) for z in range(8) for k in range(2) if z % 2 == 0 or k == 0]
FAR = [[(d, d + 4 * i) for d in range(4)] for i in range(4)]
VMEM = pl.BlockSpec(memory_space=pltpu.VMEM)
SMEM = pl.BlockSpec(memory_space=pltpu.SMEM)
NORMAL = ((1,), (0,))
RIGHT_T = ((1,), (1,))
LEFT_T = ((0,), (1,))


def dot(left, right, dims):
    return lax.dot_general(
        left, right, (dims, ((), ())), precision=FULL, preferred_element_type=jnp.float32
    )


def split(value):
    high = value.astype(jnp.bfloat16)
    return high, (value - high.astype(jnp.float32)).astype(jnp.bfloat16)


def spread_lane(value, i):
    return jnp.broadcast_to(value[:, i : i + 1], value.shape)


def factor_block(load, store, shared):
    count = BLOCK // SUB
    sub = lax.broadcasted_iota(jnp.int32, (SUB, BLOCK), 0)
    lane = lax.broadcasted_iota(jnp.int32, (SUB, BLOCK), 1)
    left = [load(k) for k in range(count)]
    right = [(lane == sub + SUB * k).astype(jnp.float32) for k in range(count)]
    for k in range(count):
        for m in range(SUB):
            shared[k % 2, m] = spread_lane(left[k], SUB * k + m)
        shared[k % 2, SUB] = left[k]
        shared[k % 2, SUB + 1] = right[k]
        row = lambda slot, i: jnp.broadcast_to(shared[k % 2, slot, i : i + 1, :], (SUB, BLOCK))
        s = [[None] * SUB for _ in range(SUB)]
        for i in range(SUB):
            for m in range(i, SUB):
                s[i][m] = s[m][i] = row(m, i)
        rows_l = [row(SUB, i) for i in range(SUB)]
        rows_r = [row(SUB + 1, i) for i in range(SUB)]
        out_l, out_r = [None] * SUB, [None] * SUB
        for i in range(0, SUB, 2):
            j = i + 1
            a, b, c = s[i][i], s[i][j], s[j][j]
            det = a * c - b * b
            root_a, root_det = lax.rsqrt(a), lax.rsqrt(det)
            second, inverse = a * root_a * root_det, root_det * root_det
            upper = b * root_a
            out_l[i], out_r[i] = rows_l[i] * root_a, rows_r[i] * root_a
            out_l[j] = (rows_l[j] - upper * out_l[i]) * second
            out_r[j] = (rows_r[j] - upper * out_r[i]) * second
            first_l, second_l = c * rows_l[i] - b * rows_l[j], a * rows_l[j] - b * rows_l[i]
            first_r, second_r = c * rows_r[i] - b * rows_r[j], a * rows_r[j] - b * rows_r[i]
            first, last = [None] * SUB, [None] * SUB
            for n in range(i + 2, SUB):
                first[n], last[n] = c * s[i][n] - b * s[j][n], a * s[j][n] - b * s[i][n]
            for m in range(SUB):
                if m in (i, j):
                    continue
                g, h = s[m][i], s[m][j]
                for n in range(i + 2, SUB):
                    if m > i and n < m:
                        continue
                    s[m][n] = s[m][n] - (g * first[n] + h * last[n]) * inverse
                    if m > i:
                        s[n][m] = s[m][n]
                rows_l[m] = rows_l[m] - (g * first_l + h * second_l) * inverse
                rows_r[m] = rows_r[m] - (g * first_r + h * second_r) * inverse
            for n in range(i + 2, SUB):
                s[i][n], s[j][n] = first[n] * inverse, last[n] * inverse
            rows_l[i], rows_l[j] = first_l * inverse, second_l * inverse
            rows_r[i], rows_r[j] = first_r * inverse, second_r * inverse
        merged_l, merged_r = out_l[0], out_r[0]
        for i in range(1, SUB):
            merged_l = jnp.where(sub == i, out_l[i], merged_l)
            merged_r = jnp.where(sub == i, out_r[i], merged_r)
        store(k, jnp.where(lane >= sub + SUB * k, merged_l, 0.0), merged_r)
        for j in range(k + 1, count):
            weights = [spread_lane(left[j], SUB * k + m) for m in range(SUB)]
            for m in range(SUB):
                left[j] = left[j] - weights[m] * rows_l[m]
                right[j] = right[j] - weights[m] * rows_r[m]


def factor_tile(tile, factor, inverse, upper, lower, shared):
    def block(start):
        def load(k):
            return tile[start + SUB * k : start + SUB * (k + 1), start : start + BLOCK]

        def store(k, rows_u, rows_w):
            upper[SUB * k : SUB * (k + 1), :] = rows_u
            lower[SUB * k : SUB * (k + 1), :] = rows_w

        factor_block(load, store, shared)
        end = start + BLOCK
        factor[start:end, start:end] = upper[...].T
        inverse[start:end, start:end] = lower[...]

    zeros = jnp.zeros((BLOCK, BLOCK), jnp.float32)
    block(0)
    first = lower[...]
    side = dot(tile[BLOCK:, :BLOCK], first, RIGHT_T)
    tile[BLOCK:, BLOCK:] = tile[BLOCK:, BLOCK:] - dot(side, side, RIGHT_T)
    factor[BLOCK:, :BLOCK] = side
    factor[:BLOCK, BLOCK:] = zeros
    inverse[:BLOCK, BLOCK:] = zeros
    block(BLOCK)
    inverse[BLOCK:, :BLOCK] = -dot(lower[...], dot(side, first, NORMAL), NORMAL)


def lead_kernel(where, mine, other, factors, inverses, sides, tiles, upper, lower, shared):
    def place(source, half):
        for y in range(4):
            for x in range(STEPS):
                for w in range(2):
                    start = 64 * y + 32 * half
                    tiles[x, w, start : start + 32, :] = source[4 * y + x, w]

    for core in range(2):

        @pl.when(where[2] == core)
        def _(core=core):
            place(mine, core)
            place(other, 1 - core)

    def step(j, carry):
        factor_tile(tiles.at[j, 0], factors.at[j], inverses.at[j], upper, lower, shared)

        @pl.when(j == 0)
        def _():
            one = dot(tiles[0, 1], inverses[0], LEFT_T)
            tiles[1, 0] = tiles[1, 0] - dot(one, one, RIGHT_T)
            sides[0] = one
            two = dot(tiles[2, 1], inverses[0], RIGHT_T)
            sides[1] = two
            tiles[1, 1] = tiles[1, 1] - dot(one, two, RIGHT_T)
            tiles[2, 0] = tiles[2, 0] - dot(two, two, RIGHT_T)

        @pl.when(j == 1)
        def _():
            two = dot(tiles[1, 1], inverses[1], LEFT_T)
            sides[2] = two
            tiles[2, 0] = tiles[2, 0] - dot(two, two, RIGHT_T)

        return carry

    lax.fori_loop(0, STEPS, step, 0)


def factorize(where, mine, other):
    three = jax.ShapeDtypeStruct((STEPS, TILE, TILE), jnp.float32)
    return pl.pallas_call(
        lead_kernel,
        out_shape=(three, three, three),
        in_specs=[SMEM, VMEM, VMEM],
        out_specs=(VMEM, VMEM, VMEM),
        scratch_shapes=[
            pltpu.VMEM((STEPS, 2, TILE, TILE), jnp.float32),
            pltpu.VMEM((BLOCK, BLOCK), jnp.float32),
            pltpu.VMEM((BLOCK, BLOCK), jnp.float32),
            pltpu.VMEM((2, SUB + 2, SUB, BLOCK), jnp.float32),
        ],
        compiler_params=pltpu.CompilerParams(vmem_limit_bytes=56 * 2**20),
        cost_estimate=pl.CostEstimate(flops=3 * 10**10, bytes_accessed=10**6, transcendentals=0),
    )(where, mine, other)


def update_kernel(
    where, a, mine, other, e, factors, inverses, sides, out, panel, q, q_high, q_low, block
):
    r, c, core = where[0], where[1], where[2]
    t = pl.program_id(0)

    @pl.when(t == 0)
    def _():
        def row(j):
            return jnp.concatenate([e[4 * s + j] for s in range(4)], axis=1)

        q0 = dot(inverses[0], row(0), NORMAL)
        q[...] = q0
        q1 = dot(inverses[1], row(1) - dot(sides[0], q0, NORMAL), NORMAL)
        q_high[:TILE, :], q_low[:TILE, :] = split(q1)
        q2 = row(2) - dot(sides[1], q0, NORMAL) - dot(sides[2], q1, NORMAL)
        q_high[TILE:, :], q_low[TILE:, :] = split(dot(inverses[2], q2, NORMAL))

    def place(lower, upper):
        for i in range(2):
            z, rows = 2 * t + i, 128 * i
            block[rows : rows + 128, :TILE] = lower[z, :128]
            block[rows : rows + 128, TILE : 2 * TILE] = upper[z, :128]
            block[rows : rows + 64, 2 * TILE :] = lower[z, 128:]
            block[rows + 64 : rows + 128, 2 * TILE :] = upper[z, 128:]

    @pl.when(core == 0)
    def _():
        place(mine, other)

    @pl.when(core != 0)
    def _():
        place(other, mine)

    p0 = dot(block[:, :TILE], inverses[0], RIGHT_T)
    p1 = block[:, TILE : 2 * TILE] - dot(p0, sides[0], RIGHT_T)
    p1 = dot(p1, inverses[1], RIGHT_T)
    p2 = block[:, 2 * TILE :] - dot(p0, sides[1], RIGHT_T) - dot(p1, sides[2], RIGHT_T)
    p2 = dot(p2, inverses[2], RIGHT_T)
    panel[:, :TILE] = p0
    panel[:, TILE : 2 * TILE] = p1
    panel[:, 2 * TILE :] = p2
    high, low = split(panel[:, TILE:])
    short = lambda x, y: jnp.dot(x, y, preferred_element_type=jnp.float32)
    qh = q_high[...]
    out[...] = a[...] - (
        dot(p0, q[...], NORMAL) + (short(high, qh) + (short(high, q_low[...]) + short(low, qh)))
    )

    for k in range(STEPS):

        @pl.when(c == k)
        def _(k=k):
            out[:, :TILE] = panel[:, TILE * k : TILE * (k + 1)]

        @pl.when((t == 0) & (r == k))
        def _(k=k):
            out[:, TILE:] = jnp.zeros((TILE, 3 * TILE), jnp.float32)

            @pl.when(c == k)
            def _():
                out[:, :TILE] = factors[k]

            @pl.when(c > k)
            def _():
                out[:, :TILE] = jnp.zeros((TILE, TILE), jnp.float32)


def update(where, matrix, *operands):
    whole = lambda x: pl.BlockSpec(x.shape, lambda t: (0,) * x.ndim)
    row_tile = pl.BlockSpec((TILE, 4 * TILE), lambda t: (t, 0))
    half = pltpu.VMEM((LEAD - TILE, 4 * TILE), jnp.bfloat16)
    return pl.pallas_call(
        update_kernel,
        grid=(4,),
        out_shape=jax.ShapeDtypeStruct(matrix.shape, jnp.float32),
        in_specs=[SMEM, row_tile] + [whole(x) for x in operands],
        out_specs=row_tile,
        scratch_shapes=[
            pltpu.VMEM((TILE, LEAD), jnp.float32),
            pltpu.VMEM((TILE, 4 * TILE), jnp.float32),
            half,
            half,
            pltpu.VMEM((TILE, LEAD), jnp.float32),
        ],
        compiler_params=pltpu.CompilerParams(vmem_limit_bytes=56 * 2**20),
        cost_estimate=pl.CostEstimate(flops=2 * 10**10, bytes_accessed=10**7, transcendentals=0),
    )(where, matrix, *operands)


def after(value, *others):
    return lax.optimization_barrier((value,) + others)[0]


def gather(value, axis, groups):
    copies = jnp.broadcast_to(value[None], (len(groups[0]),) + value.shape)
    return lax.all_to_all(copies, axis, 0, 0, axis_index_groups=groups)


def choose(index, values):
    out = jnp.zeros_like(values[0])
    for i, value in enumerate(values):
        out = jnp.where(index == i, value, out)
    return out


def on_device(matrix):
    r = lax.axis_index("row")
    c = lax.axis_index("col")
    y, x, z, core = r // 4, r % 4, c // 2, c % 2
    where = jnp.stack([r, c, core]).astype(jnp.int32)
    swap = lambda value: lax.ppermute(value, "col", CORE_SWAP)

    def spread(values):
        sent = [lax.ppermute(values[i], "col", FAR[i]) for i in (1, 2, 3)]
        return choose(z // 2, [values[0]] + sent)

    def halves(value):
        size = value.shape[0] // 2
        keep = lax.dynamic_slice_in_dim(value, core * size, size, 0)
        got = swap(lax.dynamic_slice_in_dim(value, (1 - core) * size, size, 0))
        return jnp.stack([jnp.where(core == 0, keep, got), jnp.where(core == 0, got, keep)])

    corner, top, side = matrix[:TILE, :TILE], matrix[:TILE, :], matrix[:, :TILE]
    down = lambda value, s: lax.ppermute(value, "row", [(x0, 4 * s + x0) for x0 in range(3)])

    quarters = [corner[64 * s : 64 * (s + 1)] for s in range(4)]
    quarter = choose(y, [quarters[0]] + [down(quarters[s], s) for s in range(1, 4)])
    pair = halves(quarter)
    across = lax.ppermute(pair, "col", NEAR)
    t0, t1 = jnp.where(z == 0, pair, across)[0], jnp.where(z == 0, pair, across)[1]
    t2 = jnp.where(z == 0, across, pair)[0]
    two = spread([jnp.stack([choose(x, [t0, t1, t2]), choose(x, [t1, t2, t0])])] * 4)

    column = choose(
        y, [top[:, :TILE]] + [down(top[:, TILE * s : TILE * (s + 1)], s) for s in range(1, 4)]
    )

    chunks = side.reshape(4, 2, 128, TILE)
    sent = [chunks[0]] + [lax.ppermute(chunks[i], "col", FAR[i][:3]) for i in (1, 2, 3)]
    two, column, sent = lax.optimization_barrier((two, column, sent))
    e = lax.all_gather(column, "row")
    lead_mine = gather(two, "row", ROW_GROUP)

    couple = choose(z // 2, sent)
    got = lax.ppermute(jnp.where(z % 2 == 0, couple[1], couple[0]), "col", EXCHANGE)
    first = jnp.where(z % 2 == 0, couple[0], got)
    third = jnp.where(z % 2 == 0, got, couple[1])
    got = lax.ppermute(third[64:], "col", [(2 * i, 2 * i + 1) for i in range(8)])
    my_chunk = jnp.concatenate([first, jnp.where(core == 0, third[:64], got)])
    lead_mine, my_chunk = lax.optimization_barrier((lead_mine, my_chunk))
    lead_other = swap(lead_mine)
    rows_mine = gather(my_chunk, "col", Z_GROUPS)
    factors, inverses, sides = factorize(where, lead_mine, lead_other)
    rows_mine, factors = lax.optimization_barrier((rows_mine, factors))
    rows_other = swap(rows_mine)
    return update(where, matrix, rows_mine, rows_other, e, factors, inverses, sides)


def solution(mesh):
    placed = (P("row", "col"),)
    return jax.shard_map(
        on_device, mesh=mesh, in_specs=placed, out_specs=P("row", "col"), check_vma=False
    )
```

time: 1200 us -> 171 us (0.14); the launches traced: 1190 us -> 170 us
  waiting for transfers between devices: 915 us -> 39.1 us
  other arithmetic: 186 us -> 3.76 us
  Pallas kernels: 0 us -> 55.4 us
  starting transfers between devices: 0.95 us -> 53.5 us
  matrix products: 33.6 us -> 0 us
  local copies, waits for them, and re-layouts: 32.5 us -> 4.48 us
    psum x9 -> x0, waiting for transfers between devices: 915 us -> none  [from_root(): return lax.psum(jnp.where(mine, array, jnp.zeros_like(array)), axis)]
    another operation x28 -> x4, other arithmetic: 165 us -> 0.67 us  [the longest x1 0.65 us: on_device(): where = jnp.stack([r, c, core]).astype(jnp.int32)]
    pallas_call x0 -> x2, Pallas kernels: none -> 55.4 us  [the longest x1 28 us: factorize(): pl.pallas_call(lead_kernel, out_shape=(three, three, three), in_specs=[SM...]
    ppermute x0 -> x18, starting transfers between devices: none -> 40.9 us  [the longest x6 14.2 us: on_device(): lax.ppermute(value, 'row', [(x0, 4 * s + x0) for x0 in range(3)])]
    dot_general x6 -> x0, matrix products: 29.4 us -> none  [times_transposed(): lax.dot_general(left, right, (((1,), (1,)), ((), ())), precision=SHARP, p...]
    ppermute x0 -> x18, waiting for transfers between devices: none -> 24.8 us  [the longest x3 8.97 us: on_device(): lax.ppermute(chunks[i], 'col', FAR[i][:3])]
    all_to_all x0 -> x2, waiting for transfers between devices: none -> 14.3 us  [gather(): return lax.all_to_all(copies, axis, 0, 0, axis_index_groups=groups)]
    another operation x55 -> x0, local copies, waits for them, and re-layouts: 13.6 us -> none  [the longest x34 12.7 us: factorize(): jax.scipy.linalg.solve_triangular(factor, jnp.eye(TILE, dtype=jnp.float32...]
  transfers between devices with their start and end apart: 9 -> 21, of which waited for: 9 -> 9; matrix products, arithmetic and copies ran while one was open for 0% -> 4% of each run, Pallas kernels for 0% -> 16%
where the time goes in v2:
time: 171 us; the launch traced here: 170 us
  Pallas kernels  55.4 us (32%)
  starting transfers between devices  53.5 us (31%)
  waiting for transfers between devices  39.1 us (23%)
  between operations  13.8 us (8%)
  local copies, waits for them, and re-layouts  4.48 us (3%)
  other arithmetic  3.76 us (2%)
    pallas_call x1, Pallas kernels, factorize(): pl.pallas_call(lead_kernel, out_shape=(three, three, three), in_specs=[SM...  28 us
    pallas_call x1, Pallas kernels, update(): pl.pallas_call(update_kernel, grid=(4,), out_shape=jax.ShapeDtypeStruct(m...  27.4 us
    all_to_all x2, waiting for transfers between devices, gather(): return lax.all_to_all(copies, axis, 0, 0, axis_index_groups=groups)  14.3 us
    ppermute x6, starting transfers between devices, on_device(): lax.ppermute(value, 'row', [(x0, 4 * s + x0) for x0 in range(3)])  14.2 us
    all_to_all x2, starting transfers between devices, gather(): return lax.all_to_all(copies, axis, 0, 0, axis_index_groups=groups)  12.6 us
    ppermute x3, waiting for transfers between devices, on_device(): lax.ppermute(chunks[i], 'col', FAR[i][:3])  8.97 us
    ppermute x1, waiting for transfers between devices, on_device(): lax.ppermute(third[64:], 'col', [(2 * i, 2 * i + 1) for i in range(8)])  8.62 us
    ppermute x3, starting transfers between devices, spread(): sent = [lax.ppermute(values[i], 'col', FAR[i]) for i in (1, 2, 3)]  7.89 us
  transfers between devices with their start and end apart: 21, of which 9 were waited for; matrix products, arithmetic and copies ran while one was open for 4% of the time, Pallas kernels for 16%

profile of v2, /device:TPU:1, one launch (start us, length us, event | category | flops | bytes accessed | tf_op | source)
XLA Modules:
  0.0 170.0 jit_solution(10113046261324090113)
XLA Ops:
  6.5 0.9 fusion.8
  7.5 4.0 %collective-permute-start.2 = (f32[64,256]{1,0:T(8,128)S(1)}, f32[64,256]{1,0:T(8,128)S(1)}, u32[]{:S(2)}, u32[]{:S(2)}) collective-permute-start(f32[64,256]{1,0:T(8,128)S(1)} %get-tuple-element.41), channel_id=1, source_target_pairs={{0,64},{16,80},{32,96},{1,65},{17,81},{33,97},{2,66},{18,82},{34,9... | collective-permute-start | bytes 196616 | tf_op jit(solution)/shard_map/ppermute | solution.py:312
  11.5 2.3 %collective-permute-start.1 = (f32[64,256]{1,0:T(8,128)S(1)}, f32[64,256]{1,0:T(8,128)S(1)}, u32[]{:S(2)}, u32[]{:S(2)}) collective-permute-start(f32[64,256]{1,0:T(8,128)S(1)} %get-tuple-element.42), channel_id=1, source_target_pairs={{0,128},{16,144},{32,160},{1,129},{17,145},{33,161},{2,130},{18,14... | collective-permute-start | bytes 196616 | tf_op jit(solution)/shard_map/ppermute | solution.py:312
  13.8 1.3 collective-permute-start
  15.1 0.0 collective-permute-done.2
  15.1 0.0 collective-permute-done.1
  15.2 1.2 collective-permute-done
  16.4 0.9 select_select_fusion.3
  17.3 1.6 collective-permute-start.3
  18.9 0.9 collective-permute-done.3
  19.8 3.5 %collective-permute-start.4 = (f32[2,32,256]{2,1,0:T(8,128)S(1)}, f32[2,32,256]{2,1,0:T(8,128)S(1)}, u32[]{:S(2)}, u32[]{:S(2)}) collective-permute-start(f32[2,32,256]{2,1,0:T(8,128)S(1)} %pad_maximum_fusion.1), channel_id=1, source_target_pairs={{0,2},{1,3},{2,0},{3,1},{16,18},{17,19},{18,16},{19,17},{32,34},{3... | collective-permute-start | bytes 196616 | tf_op jit(solution)/shard_map/ppermute | solution.py:317
  23.3 1.2 fusion.7
  24.5 1.3 collective-permute-start.10
  25.8 3.6 %collective-permute-start.9 = (f32[256,256]{1,0:T(8,128)S(1)}, f32[256,256]{1,0:T(8,128)S(1)}, u32[]{:S(2)}, u32[]{:S(2)}) collective-permute-start(f32[256,256]{1,0:T(8,128)S(1)} %get-tuple-element.39), channel_id=1, source_target_pairs={{0,128},{16,144},{32,160},{1,129},{17,145},{33,161},{2,130},{18,14... | collective-permute-start | bytes 786440 | tf_op jit(solution)/shard_map/ppermute | solution.py:312
  29.4 1.7 collective-permute-start.8
  31.1 0.0 collective-permute-done.4
  31.2 2.0 %collective-permute-start.7 = (f32[2,32,256]{2,1,0:T(8,128)S(1)}, f32[2,32,256]{2,1,0:T(8,128)S(1)}, u32[]{:S(2)}, u32[]{:S(2)}) collective-permute-start(f32[2,32,256]{2,1,0:T(8,128)S(1)} %pad_maximum_fusion.2), channel_id=1, source_target_pairs={{0,4},{1,5},{2,6},{3,7},{16,20},{17,21},{18,22},{19,23},{32,36},{3... | collective-permute-start | bytes 196616 | tf_op jit(solution)/shard_map/ppermute | solution.py:302
  33.2 4.6 %collective-permute-start.6 = (f32[2,32,256]{2,1,0:T(8,128)S(1)}, f32[2,32,256]{2,1,0:T(8,128)S(1)}, u32[]{:S(2)}, u32[]{:S(2)}) collective-permute-start(f32[2,32,256]{2,1,0:T(8,128)S(1)} %pad_maximum_fusion.2), channel_id=1, source_target_pairs={{0,8},{1,9},{2,10},{3,11},{16,24},{17,25},{18,26},{19,27},{32,40},... | collective-permute-start | bytes 196616 | tf_op jit(solution)/shard_map/ppermute | solution.py:302
  37.8 0.0 collective-permute-done.10
  37.8 1.3 collective-permute-start.5
  39.1 0.0 collective-permute-done.9
  39.1 0.0 collective-permute-done.8
  39.2 2.0 %fusion.6 = (f32[256,256]{1,0:T(8,128)S(1)}, f32[256,256]{1,0:T(8,128)}, f32[256,256]{1,0:T(8,128)S(1)}, f32[256,256]{1,0:T(8,128)S(1)}, f32[256,256]{1,0:T(8,128)S(1)}) fusion(f32[1024,1024]{1,0:T(8,128)} %a.1, f32[256,256]{1,0:T(8,128)S(1)} %collective-permute-done.8, f32[256,256]{1,0:T(8,128)S(1)} %collective-permute-done.9, ...), kind=kLoop, calls=%fused_computation.24 | loop fusion | flops 262144 | bytes 3145732 | tf_op jit(solution)/shard_map/slice | solution.py:327
  41.2 2.9 %collective-permute-start.13 = (f32[2,128,256]{2,1,0:T(8,128)S(1)}, f32[2,128,256]{2,1,0:T(8,128)S(1)}, u32[]{:S(2)}, u32[]{:S(2)}) collective-permute-start(f32[2,128,256]{2,1,0:T(8,128)S(1)} %bitcast.27), channel_id=1, source_target_pairs={{0,12},{1,13},{2,14},{16,28},{17,29},{18,30},{32,44},{33,45},{34,4... | collective-permute-start | bytes 786440 | tf_op jit(solution)/shard_map/ppermute | solution.py:327
  44.1 1.6 collective-permute-start.12
  45.7 0.0 collective-permute-done.7
  45.7 1.3 collective-permute-start.11
  47.1 0.0 collective-permute-done.5
  47.1 7.4 %collective-permute-done.13 = f32[2,128,256]{2,1,0:T(8,128)S(1)} collective-permute-done((f32[2,128,256]{2,1,0:T(8,128)S(1)}, f32[2,128,256]{2,1,0:T(8,128)S(1)}, u32[]{:S(2)}, u32[]{:S(2)}) %collective-permute-start.13) | collective-permute-done | bytes 262176 | tf_op jit(solution)/shard_map/ppermute | solution.py:327
  54.5 1.6 collective-permute-done.11
  56.1 0.0 all-gather.3.cloned.1.call-update
  56.1 1.1 broadcast_in_dim.27
  57.2 7.5 %all-to-all-start = ((f32[16,2,32,256]{3,2,1,0:T(8,128)}), f32[16,2,32,256]{3,2,1,0:T(8,128)S(1)}, u32[]{:S(2)}, u32[]{:S(2)}) async-start(f32[16,2,32,256]{3,2,1,0:T(8,128)} %broadcast_in_dim.27), calls=%async_computation | async-start | bytes 2097152 | tf_op jit(solution)/shard_map/all_to_all | solution.py:284
  64.8 0.1 select_select_fusion
  64.9 1.3 collective-permute-start.14
  66.2 1.9 %collective-permute-done.14 = f32[128,256]{1,0:T(8,128)S(1)} collective-permute-done((f32[128,256]{1,0:T(8,128)S(1)}, f32[128,256]{1,0:T(8,128)S(1)}, u32[]{:S(2)}, u32[]{:S(2)}) %collective-permute-start.14) | collective-permute-done | bytes 131104 | tf_op jit(solution)/shard_map/ppermute | solution.py:333
  68.2 1.3 collective-permute-start.15
  69.5 8.6 %collective-permute-done.15 = f32[64,256]{1,0:T(8,128)S(1)} collective-permute-done((f32[64,256]{1,0:T(8,128)S(1)}, f32[64,256]{1,0:T(8,128)S(1)}, u32[]{:S(2)}, u32[]{:S(2)}) %collective-permute-start.15) | collective-permute-done | bytes 65568 | tf_op jit(solution)/shard_map/ppermute | solution.py:336
  78.1 1.9 %all-to-all-done.mine = f32[16,2,32,256]{3,2,1,0:T(8,128)S(1)} async-done(((f32[16,2,32,256]{3,2,1,0:T(8,128)}), f32[16,2,32,256]{3,2,1,0:T(8,128)S(1)}, u32[]{:S(2)}, u32[]{:S(2)}) %all-to-all-start) | async-done | bytes 1048608 | tf_op jit(solution)/shard_map/all_to_all | solution.py:284
  80.0 4.8 %collective-permute-start.16 = (f32[16,2,32,256]{3,2,1,0:T(8,128)S(1)}, f32[16,2,32,256]{3,2,1,0:T(8,128)}, u32[]{:S(2)}, u32[]{:S(2)}) collective-permute-start(f32[16,2,32,256]{3,2,1,0:T(8,128)S(1)} %all-to-all-done.mine), channel_id=1, source_target_pairs={{0,1},{1,0},{2,3},{3,2},{4,5},{5,4},{6,7},{7,6},{8,9},{9,8},{10,11... | collective-permute-start | bytes 3145736 | tf_op jit(solution)/shard_map/ppermute | solution.py:299
  84.8 0.6 pad_add_fusion.where
  85.4 1.3 broadcast_in_dim.29
  86.7 5.1 %all-to-all-start.1 = ((f32[8,192,256]{2,1,0:T(8,128)}), f32[8,192,256]{2,1,0:T(8,128)S(1)}, u32[]{:S(2)}, u32[]{:S(2)}) async-start(f32[8,192,256]{2,1,0:T(8,128)} %broadcast_in_dim.29), calls=%async_computation.1 | async-start | bytes 3145728 | tf_op jit(solution)/shard_map/all_to_all | solution.py:284
  91.8 28.0 %shard_map.17 = (f32[3,256,256]{2,1,0:T(8,128)}, f32[3,256,256]{2,1,0:T(8,128)}, f32[3,256,256]{2,1,0:T(8,128)}) custom-call(s32[3]{0:T(128)} %pad_add_fusion.where, f32[16,2,32,256]{3,2,1,0:T(8,128)} %copy-done.1, f32[16,2,32,256]{3,2,1,0:T(8,128)} %collective-permute-done.16.other), custom_call_target="tpu_custom_call" | custom-call | flops 30000001024 | bytes 1000000 | tf_op jit(solution)/shard_map/pallas_call | solution.py:172
  119.8 12.4 %all-to-all-done.1.mine = f32[8,192,256]{2,1,0:T(8,128)S(1)} async-done(((f32[8,192,256]{2,1,0:T(8,128)}), f32[8,192,256]{2,1,0:T(8,128)S(1)}, u32[]{:S(2)}, u32[]{:S(2)}) %all-to-all-start.1) | async-done | bytes 1572896 | tf_op jit(solution)/shard_map/all_to_all | solution.py:284
  132.2 0.5 collective-permute-start.17
  132.7 3.2 %collective-permute-done.17.other = f32[8,192,256]{2,1,0:T(8,128)} collective-permute-done((f32[8,192,256]{2,1,0:T(8,128)S(1)}, f32[8,192,256]{2,1,0:T(8,128)}, u32[]{:S(2)}, u32[]{:S(2)}) %collective-permute-start.17) | collective-permute-done | bytes 1572896 | tf_op jit(solution)/shard_map/ppermute | solution.py:299
  135.8 27.4 %shard_map.18 = f32[1024,1024]{1,0:T(8,128)} custom-call(s32[3]{0:T(128)} %pad_add_fusion.where, f32[1024,1024]{1,0:T(8,128)} %a.1, f32[8,192,256]{2,1,0:T(8,128)} %copy-done, f32[8,192,256]{2,1,0:T(8,128)} %collective-permute-done.17.other, f32[16,256,256]{2,1,0:T(8,128)} %bitcast.28, f32[3,256,256]{2,1,0:T(8,128)} %get-tuple-element.28.factors, ...), custom_call_target="tpu_custom_call" | custom-call | flops 20000000000 | bytes 10000000 | tf_op jit(solution)/shard_map/pallas_call | solution.py:260
  (22 shorter events, 0.2 us)
Async XLA Ops:
  6.5 129.3 %all-gather.3.cloned.1.call-start = ((), (), s32[]{:S(2)}) async-start(), calls=%async_computation.2 | async-start | bytes 4456448 | tf_op jit(solution)/shard_map/all_gather | solution.py:329
  7.5 7.7 %collective-permute-start.2 = (f32[64,256]{1,0:T(8,128)S(1)}, f32[64,256]{1,0:T(8,128)S(1)}, u32[]{:S(2)}, u32[]{:S(2)}) collective-permute-start(f32[64,256]{1,0:T(8,128)S(1)} %get-tuple-element.41), channel_id=1, source_target_pairs={{0,64},{16,80},{32,96},{1,65},{17,81},{33,97},{2,66},{18,82},{34,9... | collective-permute-start | bytes 196616 | tf_op jit(solution)/shard_map/ppermute | solution.py:312
  11.5 3.6 %collective-permute-start.1 = (f32[64,256]{1,0:T(8,128)S(1)}, f32[64,256]{1,0:T(8,128)S(1)}, u32[]{:S(2)}, u32[]{:S(2)}) collective-permute-start(f32[64,256]{1,0:T(8,128)S(1)} %get-tuple-element.42), channel_id=1, source_target_pairs={{0,128},{16,144},{32,160},{1,129},{17,145},{33,161},{2,130},{18,14... | collective-permute-start | bytes 196616 | tf_op jit(solution)/shard_map/ppermute | solution.py:312
  13.8 2.6 %collective-permute-start = (f32[64,256]{1,0:T(8,128)S(1)}, f32[64,256]{1,0:T(8,128)S(1)}, u32[]{:S(2)}, u32[]{:S(2)}) collective-permute-start(f32[64,256]{1,0:T(8,128)S(1)} %get-tuple-element.43), channel_id=1, source_target_pairs={{0,192},{16,208},{32,224},{1,193},{17,209},{33,225},{2,194},{18,21... | collective-permute-start | bytes 196616 | tf_op jit(solution)/shard_map/ppermute | solution.py:312
  17.3 2.5 %collective-permute-start.3 = (f32[32,256]{1,0:T(8,128)S(1)}, f32[32,256]{1,0:T(8,128)S(1)}, u32[]{:S(2)}, u32[]{:S(2)}) collective-permute-start(f32[32,256]{1,0:T(8,128)S(1)} %constant_dynamic-slice_fusion), channel_id=1, source_target_pairs={{0,1},{1,0},{2,3},{3,2},{4,5},{5,4},{6,7},{7,6},{8,9},{9,8},{10,11... | collective-permute-start | bytes 98312 | tf_op jit(solution)/shard_map/ppermute | solution.py:299
  19.8 11.4 %collective-permute-start.4 = (f32[2,32,256]{2,1,0:T(8,128)S(1)}, f32[2,32,256]{2,1,0:T(8,128)S(1)}, u32[]{:S(2)}, u32[]{:S(2)}) collective-permute-start(f32[2,32,256]{2,1,0:T(8,128)S(1)} %pad_maximum_fusion.1), channel_id=1, source_target_pairs={{0,2},{1,3},{2,0},{3,1},{16,18},{17,19},{18,16},{19,17},{32,34},{3... | collective-permute-start | bytes 196616 | tf_op jit(solution)/shard_map/ppermute | solution.py:317
  24.5 13.3 %collective-permute-start.10 = (f32[256,256]{1,0:T(8,128)S(1)}, f32[256,256]{1,0:T(8,128)S(1)}, u32[]{:S(2)}, u32[]{:S(2)}) collective-permute-start(f32[256,256]{1,0:T(8,128)S(1)} %get-tuple-element.38), channel_id=1, source_target_pairs={{0,64},{16,80},{32,96},{1,65},{17,81},{33,97},{2,66},{18,82},{34,9... | collective-permute-start | bytes 786440 | tf_op jit(solution)/shard_map/ppermute | solution.py:312
  25.8 13.3 %collective-permute-start.9 = (f32[256,256]{1,0:T(8,128)S(1)}, f32[256,256]{1,0:T(8,128)S(1)}, u32[]{:S(2)}, u32[]{:S(2)}) collective-permute-start(f32[256,256]{1,0:T(8,128)S(1)} %get-tuple-element.39), channel_id=1, source_target_pairs={{0,128},{16,144},{32,160},{1,129},{17,145},{33,161},{2,130},{18,14... | collective-permute-start | bytes 786440 | tf_op jit(solution)/shard_map/ppermute | solution.py:312
  29.4 9.7 %collective-permute-start.8 = (f32[256,256]{1,0:T(8,128)S(1)}, f32[256,256]{1,0:T(8,128)S(1)}, u32[]{:S(2)}, u32[]{:S(2)}) collective-permute-start(f32[256,256]{1,0:T(8,128)S(1)} %get-tuple-element.40), channel_id=1, source_target_pairs={{0,192},{16,208},{32,224},{1,193},{17,209},{33,225},{2,194},{18,21... | collective-permute-start | bytes 786440 | tf_op jit(solution)/shard_map/ppermute | solution.py:312
  31.2 14.5 %collective-permute-start.7 = (f32[2,32,256]{2,1,0:T(8,128)S(1)}, f32[2,32,256]{2,1,0:T(8,128)S(1)}, u32[]{:S(2)}, u32[]{:S(2)}) collective-permute-start(f32[2,32,256]{2,1,0:T(8,128)S(1)} %pad_maximum_fusion.2), channel_id=1, source_target_pairs={{0,4},{1,5},{2,6},{3,7},{16,20},{17,21},{18,22},{19,23},{32,36},{3... | collective-permute-start | bytes 196616 | tf_op jit(solution)/shard_map/ppermute | solution.py:302
  33.2 13.8 %collective-permute-start.6 = (f32[2,32,256]{2,1,0:T(8,128)S(1)}, f32[2,32,256]{2,1,0:T(8,128)S(1)}, u32[]{:S(2)}, u32[]{:S(2)}) collective-permute-start(f32[2,32,256]{2,1,0:T(8,128)S(1)} %pad_maximum_fusion.2), channel_id=1, source_target_pairs={{0,8},{1,9},{2,10},{3,11},{16,24},{17,25},{18,26},{19,27},{32,40},... | collective-permute-start | bytes 196616 | tf_op jit(solution)/shard_map/ppermute | solution.py:302
  37.8 9.3 %collective-permute-start.5 = (f32[2,32,256]{2,1,0:T(8,128)S(1)}, f32[2,32,256]{2,1,0:T(8,128)S(1)}, u32[]{:S(2)}, u32[]{:S(2)}) collective-permute-start(f32[2,32,256]{2,1,0:T(8,128)S(1)} %pad_maximum_fusion.2), channel_id=1, source_target_pairs={{0,12},{1,13},{2,14},{3,15},{16,28},{17,29},{18,30},{19,31},{32,44... | collective-permute-start | bytes 196616 | tf_op jit(solution)/shard_map/ppermute | solution.py:302
  41.2 13.3 %collective-permute-start.13 = (f32[2,128,256]{2,1,0:T(8,128)S(1)}, f32[2,128,256]{2,1,0:T(8,128)S(1)}, u32[]{:S(2)}, u32[]{:S(2)}) collective-permute-start(f32[2,128,256]{2,1,0:T(8,128)S(1)} %bitcast.27), channel_id=1, source_target_pairs={{0,12},{1,13},{2,14},{16,28},{17,29},{18,30},{32,44},{33,45},{34,4... | collective-permute-start | bytes 786440 | tf_op jit(solution)/shard_map/ppermute | solution.py:327
  44.1 10.3 %collective-permute-start.12 = (f32[2,128,256]{2,1,0:T(8,128)S(1)}, f32[2,128,256]{2,1,0:T(8,128)S(1)}, u32[]{:S(2)}, u32[]{:S(2)}) collective-permute-start(f32[2,128,256]{2,1,0:T(8,128)S(1)} %bitcast.26), channel_id=1, source_target_pairs={{0,8},{1,9},{2,10},{16,24},{17,25},{18,26},{32,40},{33,41},{34,42}... | collective-permute-start | bytes 786440 | tf_op jit(solution)/shard_map/ppermute | solution.py:327
  45.7 10.4 %collective-permute-start.11 = (f32[2,128,256]{2,1,0:T(8,128)S(1)}, f32[2,128,256]{2,1,0:T(8,128)S(1)}, u32[]{:S(2)}, u32[]{:S(2)}) collective-permute-start(f32[2,128,256]{2,1,0:T(8,128)S(1)} %bitcast.25), channel_id=1, source_target_pairs={{0,4},{1,5},{2,6},{16,20},{17,21},{18,22},{32,36},{33,37},{34,38},... | collective-permute-start | bytes 786440 | tf_op jit(solution)/shard_map/ppermute | solution.py:327
  57.2 22.8 %all-to-all-start = ((f32[16,2,32,256]{3,2,1,0:T(8,128)}), f32[16,2,32,256]{3,2,1,0:T(8,128)S(1)}, u32[]{:S(2)}, u32[]{:S(2)}) async-start(f32[16,2,32,256]{3,2,1,0:T(8,128)} %broadcast_in_dim.27), calls=%async_computation | async-start | bytes 2097152 | tf_op jit(solution)/shard_map/all_to_all | solution.py:284
  64.9 3.2 %collective-permute-start.14 = (f32[128,256]{1,0:T(8,128)S(1)}, f32[128,256]{1,0:T(8,128)S(1)}, u32[]{:S(2)}, u32[]{:S(2)}) collective-permute-start(f32[128,256]{1,0:T(8,128)S(1)} %fusion.1), channel_id=1, source_target_pairs={{0,2},{1,3},{2,0},{4,6},{5,7},{6,4},{8,10},{9,11},{10,8},{12,14},{... | collective-permute-start | bytes 393224 | tf_op jit(solution)/shard_map/ppermute | solution.py:333
  68.2 9.9 %collective-permute-start.15 = (f32[64,256]{1,0:T(8,128)S(1)}, f32[64,256]{1,0:T(8,128)S(1)}, u32[]{:S(2)}, u32[]{:S(2)}) collective-permute-start(f32[64,256]{1,0:T(8,128)S(1)} %slice.102), channel_id=1, source_target_pairs={{0,1},{2,3},{4,5},{6,7},{8,9},{10,11},{12,13},{14,15},{16,17},{18,... | collective-permute-start | bytes 196616 | tf_op jit(solution)/shard_map/ppermute | solution.py:336
  80.0 11.8 %copy-start.1 = (f32[16,2,32,256]{3,2,1,0:T(8,128)}, f32[16,2,32,256]{3,2,1,0:T(8,128)S(1)}, u32[]{:S(2)}) copy-start(f32[16,2,32,256]{3,2,1,0:T(8,128)S(1)} %all-to-all-done.mine) | copy-start | bytes 3145732
  80.0 11.8 %collective-permute-start.16 = (f32[16,2,32,256]{3,2,1,0:T(8,128)S(1)}, f32[16,2,32,256]{3,2,1,0:T(8,128)}, u32[]{:S(2)}, u32[]{:S(2)}) collective-permute-start(f32[16,2,32,256]{3,2,1,0:T(8,128)S(1)} %all-to-all-done.mine), channel_id=1, source_target_pairs={{0,1},{1,0},{2,3},{3,2},{4,5},{5,4},{6,7},{7,6},{8,9},{9,8},{10,11... | collective-permute-start | bytes 3145736 | tf_op jit(solution)/shard_map/ppermute | solution.py:299
  86.7 45.5 %all-to-all-start.1 = ((f32[8,192,256]{2,1,0:T(8,128)}), f32[8,192,256]{2,1,0:T(8,128)S(1)}, u32[]{:S(2)}, u32[]{:S(2)}) async-start(f32[8,192,256]{2,1,0:T(8,128)} %broadcast_in_dim.29), calls=%async_computation.1 | async-start | bytes 3145728 | tf_op jit(solution)/shard_map/all_to_all | solution.py:284
  132.2 3.6 %copy-start = (f32[8,192,256]{2,1,0:T(8,128)}, f32[8,192,256]{2,1,0:T(8,128)S(1)}, u32[]{:S(2)}) copy-start(f32[8,192,256]{2,1,0:T(8,128)S(1)} %all-to-all-done.1.mine) | copy-start | bytes 4718596
  132.2 3.6 %collective-permute-start.17 = (f32[8,192,256]{2,1,0:T(8,128)S(1)}, f32[8,192,256]{2,1,0:T(8,128)}, u32[]{:S(2)}, u32[]{:S(2)}) collective-permute-start(f32[8,192,256]{2,1,0:T(8,128)S(1)} %all-to-all-done.1.mine), channel_id=1, source_target_pairs={{0,1},{1,0},{2,3},{3,2},{4,5},{5,4},{6,7},{7,6},{8,9},{9,8},{10,11... | collective-permute-start | bytes 4718600 | tf_op jit(solution)/shard_map/ppermute | solution.py:299
Sparse Core Ops, SparseCore 0:
  56.2 62.0 all-gather.2

commit v3 on v2

--- a/solution.py
+++ b/solution.py
@@ -29,11 +29,6 @@
     return lax.dot_general(
         left, right, (dims, ((), ())), precision=FULL, preferred_element_type=jnp.float32
     )
-
-
-def split(value):
-    high = value.astype(jnp.bfloat16)
-    return high, (value - high.astype(jnp.float32)).astype(jnp.bfloat16)
 
 
 def spread_lane(value, i):
@@ -185,23 +180,70 @@
     )(where, mine, other)
 
 
+def parts(value, count):
+    out = []
+    for _ in range(count):
+        out.append(value.astype(jnp.bfloat16))
+        value = value - out[-1].astype(jnp.float32)
+    return out
+
+
+def stack(ref, value, count):
+    size = value.shape[0]
+    for i, part in enumerate(parts(value, count)):
+        start = size * (count - 1 - i)
+        ref[start : start + size, :] = part
+
+
+def times(value, ref, count):
+    size = value.shape[1]
+    total = None
+    for i, part in reversed(list(enumerate(parts(value, count)))):
+        left = jnp.concatenate([part] * (count - i), axis=1)
+        product = jnp.dot(left, ref[size * i :, :], preferred_element_type=jnp.float32)
+        total = product if total is None else total + product
+    return total
+
+
+def across_kernel(e, inverses, sides, q):
+    def row(j):
+        return jnp.concatenate([e[4 * s + j] for s in range(4)], axis=1)
+
+    q0 = dot(inverses[0], row(0), NORMAL)
+    stack(q.at[:LEAD], q0, 3)
+    q1 = dot(inverses[1], row(1) - dot(sides[0], q0, NORMAL), NORMAL)
+    q2 = row(2) - dot(sides[1], q0, NORMAL) - dot(sides[2], q1, NORMAL)
+    q2 = dot(inverses[2], q2, NORMAL)
+    for i, value in enumerate((q1, q2)):
+        high, low = parts(value, 2)
+        start = LEAD + TILE * i
+        q[start : start + TILE, :] = high
+        q[start + 2 * TILE : start + 3 * TILE, :] = low
+
+
+def across(e, inverses, sides):
+    return pl.pallas_call(
+        across_kernel,
+        out_shape=jax.ShapeDtypeStruct((7 * TILE, 4 * TILE), jnp.bfloat16),
+        in_specs=[VMEM] * 3,
+        out_specs=VMEM,
+        compiler_params=pltpu.CompilerParams(vmem_limit_bytes=56 * 2**20),
+        cost_estimate=pl.CostEstimate(flops=10**10, bytes_accessed=10**7, transcendentals=0),
+    )(e, inverses, sides)
+
+
 def update_kernel(
-    where, a, mine, other, e, factors, inverses, sides, out, panel, q, q_high, q_low, block
+    where, a, mine, other, q, factors, inverses, sides, out, panel, block, right0, right1, rights
 ):
     r, c, core = where[0], where[1], where[2]
     t = pl.program_id(0)
 
     @pl.when(t == 0)
     def _():
-        def row(j):
-            return jnp.concatenate([e[4 * s + j] for s in range(4)], axis=1)
-
-        q0 = dot(inverses[0], row(0), NORMAL)
-        q[...] = q0
-        q1 = dot(inverses[1], row(1) - dot(sides[0], q0, NORMAL), NORMAL)
-        q_high[:TILE, :], q_low[:TILE, :] = split(q1)
-        q2 = row(2) - dot(sides[1], q0, NORMAL) - dot(sides[2], q1, NORMAL)
-        q_high[TILE:, :], q_low[TILE:, :] = split(dot(inverses[2], q2, NORMAL))
+        stack(right0, inverses[0].T, 3)
+        stack(right1, jnp.concatenate([sides[0].T, sides[1].T], axis=1), 3)
+        for i, value in enumerate((inverses[1], sides[2], inverses[2])):
+            stack(rights.at[i], value.T, 2)
 
     def place(lower, upper):
         for i in range(2):
@@ -219,20 +261,22 @@
     def _():
         place(other, mine)
 
-    p0 = dot(block[:, :TILE], inverses[0], RIGHT_T)
-    p1 = block[:, TILE : 2 * TILE] - dot(p0, sides[0], RIGHT_T)
-    p1 = dot(p1, inverses[1], RIGHT_T)
-    p2 = block[:, 2 * TILE :] - dot(p0, sides[1], RIGHT_T) - dot(p1, sides[2], RIGHT_T)
-    p2 = dot(p2, inverses[2], RIGHT_T)
+    p0 = times(block[:, :TILE], right0, 3)
+    removed = times(p0, right1, 3)
+    p1 = times(block[:, TILE : 2 * TILE] - removed[:, :TILE], rights.at[0], 2)
+    p2 = block[:, 2 * TILE :] - removed[:, TILE:] - times(p1, rights.at[1], 2)
+    p2 = times(p2, rights.at[2], 2)
     panel[:, :TILE] = p0
     panel[:, TILE : 2 * TILE] = p1
     panel[:, 2 * TILE :] = p2
-    high, low = split(panel[:, TILE:])
+
+    first, second, third = parts(p0, 3)
+    high, low = parts(panel[:, TILE:], 2)
     short = lambda x, y: jnp.dot(x, y, preferred_element_type=jnp.float32)
-    qh = q_high[...]
-    out[...] = a[...] - (
-        dot(p0, q[...], NORMAL) + (short(high, qh) + (short(high, q_low[...]) + short(low, qh)))
-    )
+    total = short(third, q[2 * TILE : 3 * TILE, :])
+    total = total + short(jnp.concatenate([second, second, low], axis=1), q[TILE : 5 * TILE, :])
+    total = total + short(jnp.concatenate([first, first, first, high, high], axis=1), q[...])
+    out[...] = a[...] - total
 
     for k in range(STEPS):
 
@@ -256,7 +300,6 @@
 def update(where, matrix, *operands):
     whole = lambda x: pl.BlockSpec(x.shape, lambda t: (0,) * x.ndim)
     row_tile = pl.BlockSpec((TILE, 4 * TILE), lambda t: (t, 0))
-    half = pltpu.VMEM((LEAD - TILE, 4 * TILE), jnp.bfloat16)
     return pl.pallas_call(
         update_kernel,
         grid=(4,),
@@ -265,10 +308,10 @@
         out_specs=row_tile,
         scratch_shapes=[
             pltpu.VMEM((TILE, LEAD), jnp.float32),
-            pltpu.VMEM((TILE, 4 * TILE), jnp.float32),
-            half,
-            half,
             pltpu.VMEM((TILE, LEAD), jnp.float32),
+            pltpu.VMEM((3 * TILE, TILE), jnp.bfloat16),
+            pltpu.VMEM((3 * TILE, 2 * TILE), jnp.bfloat16),
+            pltpu.VMEM((STEPS, 2 * TILE, TILE), jnp.bfloat16),
         ],
         compiler_params=pltpu.CompilerParams(vmem_limit_bytes=56 * 2**20),
         cost_estimate=pl.CostEstimate(flops=2 * 10**10, bytes_accessed=10**7, transcendentals=0),
@@ -314,18 +357,18 @@
     quarters = [corner[64 * s : 64 * (s + 1)] for s in range(4)]
     quarter = choose(y, [quarters[0]] + [down(quarters[s], s) for s in range(1, 4)])
     pair = halves(quarter)
-    across = lax.ppermute(pair, "col", NEAR)
-    t0, t1 = jnp.where(z == 0, pair, across)[0], jnp.where(z == 0, pair, across)[1]
-    t2 = jnp.where(z == 0, across, pair)[0]
+    next_door = lax.ppermute(pair, "col", NEAR)
+    t0, t1 = jnp.where(z == 0, pair, next_door)[0], jnp.where(z == 0, pair, next_door)[1]
+    t2 = jnp.where(z == 0, next_door, pair)[0]
     two = spread([jnp.stack([choose(x, [t0, t1, t2]), choose(x, [t1, t2, t0])])] * 4)
 
     column = choose(
         y, [top[:, :TILE]] + [down(top[:, TILE * s : TILE * (s + 1)], s) for s in range(1, 4)]
     )
 
-    chunks = side.reshape(4, 2, 128, TILE)
+    chunks = after(side, two).reshape(4, 2, 128, TILE)
     sent = [chunks[0]] + [lax.ppermute(chunks[i], "col", FAR[i][:3]) for i in (1, 2, 3)]
-    two, column, sent = lax.optimization_barrier((two, column, sent))
+    two, column = lax.optimization_barrier((two, column))
     e = lax.all_gather(column, "row")
     lead_mine = gather(two, "row", ROW_GROUP)
 
@@ -339,9 +382,10 @@
     lead_other = swap(lead_mine)
     rows_mine = gather(my_chunk, "col", Z_GROUPS)
     factors, inverses, sides = factorize(where, lead_mine, lead_other)
-    rows_mine, factors = lax.optimization_barrier((rows_mine, factors))
+    q = across(e, inverses, sides)
+    rows_mine, q = lax.optimization_barrier((rows_mine, q))
     rows_other = swap(rows_mine)
-    return update(where, matrix, rows_mine, rows_other, e, factors, inverses, sides)
+    return update(where, matrix, rows_mine, rows_other, q, factors, inverses, sides)
 
 
 def solution(mesh):

time: 171 us -> 158 us (0.924)
  starting transfers between devices: 53.5 us -> 45.1 us
  waiting for transfers between devices: 39.1 us -> 31.1 us
  Pallas kernels: 55.4 us -> 58.4 us
    pallas_call x0 -> x1, Pallas kernels: none -> 9.92 us  [across(): pl.pallas_call(across_kernel, out_shape=jax.ShapeDtypeStruct((7 * TILE, 4...]
    pallas_call x1, Pallas kernels: 27.4 us -> 20.1 us  [update(): pl.pallas_call(update_kernel, grid=(4,), out_shape=jax.ShapeDtypeStruct(m...]
    ppermute x3, waiting for transfers between devices: 8.97 us -> 2.38 us  [on_device(): lax.ppermute(chunks[i], 'col', FAR[i][:3])]
    all_to_all x2, waiting for transfers between devices: 14.3 us -> 8.66 us  [gather(): return lax.all_to_all(copies, axis, 0, 0, axis_index_groups=groups)]
    ppermute x6, waiting for transfers between devices: 1.26 us -> 6.8 us  [on_device(): lax.ppermute(value, 'row', [(x0, 4 * s + x0) for x0 in range(3)])]
    ppermute x1, waiting for transfers between devices: 8.62 us -> 5.41 us  [on_device(): lax.ppermute(third[64:], 'col', [(2 * i, 2 * i + 1) for i in range(8)])]
    ppermute x3, starting transfers between devices: 6.86 us -> 3.85 us  [on_device(): swap = lambda value: lax.ppermute(value, 'col', CORE_SWAP)]
    slice x1 -> x0, other arithmetic: 2.04 us -> none  [on_device(): chunks[i]]
  transfers between devices with their start and end apart: 21 -> 21, of which waited for: 9 -> 10; matrix products, arithmetic and copies ran while one was open for 4% -> 3% of each run, Pallas kernels for 16% -> 24%
where the time goes in v3:
time: 158 us
  Pallas kernels  58.4 us (37%)
  starting transfers between devices  45.1 us (29%)
  waiting for transfers between devices  31.1 us (20%)
  between operations  13.8 us (9%)
  local copies, waits for them, and re-layouts  5.71 us (4%)
  other arithmetic  3.49 us (2%)
    pallas_call x1, Pallas kernels, factorize(): pl.pallas_call(lead_kernel, out_shape=(three, three, three), in_specs=[SM...  28.4 us
    pallas_call x1, Pallas kernels, update(): pl.pallas_call(update_kernel, grid=(4,), out_shape=jax.ShapeDtypeStruct(m...  20.1 us
    ppermute x6, starting transfers between devices, on_device(): lax.ppermute(value, 'row', [(x0, 4 * s + x0) for x0 in range(3)])  14.2 us
    all_to_all x2, starting transfers between devices, gather(): return lax.all_to_all(copies, axis, 0, 0, axis_index_groups=groups)  11.1 us
    pallas_call x1, Pallas kernels, across(): pl.pallas_call(across_kernel, out_shape=jax.ShapeDtypeStruct((7 * TILE, 4...  9.92 us
    all_to_all x2, waiting for transfers between devices, gather(): return lax.all_to_all(copies, axis, 0, 0, axis_index_groups=groups)  8.66 us
    ppermute x6, waiting for transfers between devices, on_device(): lax.ppermute(value, 'row', [(x0, 4 * s + x0) for x0 in range(3)])  6.8 us
    ppermute x3, starting transfers between devices, spread(): sent = [lax.ppermute(values[i], 'col', FAR[i]) for i in (1, 2, 3)]  5.89 us
  transfers between devices with their start and end apart: 21, of which 10 were waited for; matrix products, arithmetic and copies ran while one was open for 3% of the time, Pallas kernels for 24%

profile of v3, /device:TPU:1, one launch (start us, length us, event | category | flops | bytes accessed | tf_op | source)
XLA Modules:
  0.0 157.6 jit_solution(7314003187795707870)
XLA Ops:
  6.5 1.0 fusion.7
  7.5 4.0 %collective-permute-start.2 = (f32[64,256]{1,0:T(8,128)S(1)}, f32[64,256]{1,0:T(8,128)S(1)}, u32[]{:S(2)}, u32[]{:S(2)}) collective-permute-start(f32[64,256]{1,0:T(8,128)S(1)} %get-tuple-element.30), channel_id=1, source_target_pairs={{0,64},{16,80},{32,96},{1,65},{17,81},{33,97},{2,66},{18,82},{34,9... | collective-permute-start | bytes 196616 | tf_op jit(solution)/shard_map/ppermute | solution.py:355
  11.6 2.3 %collective-permute-start.1 = (f32[64,256]{1,0:T(8,128)S(1)}, f32[64,256]{1,0:T(8,128)S(1)}, u32[]{:S(2)}, u32[]{:S(2)}) collective-permute-start(f32[64,256]{1,0:T(8,128)S(1)} %get-tuple-element.31), channel_id=1, source_target_pairs={{0,128},{16,144},{32,160},{1,129},{17,145},{33,161},{2,130},{18,14... | collective-permute-start | bytes 196616 | tf_op jit(solution)/shard_map/ppermute | solution.py:355
  13.9 1.3 collective-permute-start
  15.2 0.0 collective-permute-done.2
  15.2 0.0 collective-permute-done.1
  15.2 1.2 collective-permute-done
  16.5 0.9 select_select_fusion.3
  17.4 1.6 %collective-permute-start.3 = (f32[32,256]{1,0:T(8,128)S(1)}, f32[32,256]{1,0:T(8,128)S(1)}, u32[]{:S(2)}, u32[]{:S(2)}) collective-permute-start(f32[32,256]{1,0:T(8,128)S(1)} %constant_dynamic-slice_fusion), channel_id=1, source_target_pairs={{0,1},{1,0},{2,3},{3,2},{4,5},{5,4},{6,7},{7,6},{8,9},{9,8},{10,11... | collective-permute-start | bytes 98312 | tf_op jit(solution)/shard_map/ppermute | solution.py:342
  19.0 0.9 collective-permute-done.3
  19.9 3.5 %collective-permute-start.4 = (f32[2,32,256]{2,1,0:T(8,128)S(1)}, f32[2,32,256]{2,1,0:T(8,128)S(1)}, u32[]{:S(2)}, u32[]{:S(2)}) collective-permute-start(f32[2,32,256]{2,1,0:T(8,128)S(1)} %pad_maximum_fusion.1), channel_id=1, source_target_pairs={{0,2},{1,3},{2,0},{3,1},{16,18},{17,19},{18,16},{19,17},{32,34},{3... | collective-permute-start | bytes 196616 | tf_op jit(solution)/shard_map/ppermute | solution.py:360
  23.5 2.0 %collective-permute-done.4 = f32[2,32,256]{2,1,0:T(8,128)S(1)} collective-permute-done((f32[2,32,256]{2,1,0:T(8,128)S(1)}, f32[2,32,256]{2,1,0:T(8,128)S(1)}, u32[]{:S(2)}, u32[]{:S(2)}) %collective-permute-start.4) | collective-permute-done | bytes 65568 | tf_op jit(solution)/shard_map/ppermute | solution.py:360
  25.5 1.3 collective-permute-start.7
  26.8 3.3 %collective-permute-start.6 = (f32[2,32,256]{2,1,0:T(8,128)S(1)}, f32[2,32,256]{2,1,0:T(8,128)S(1)}, u32[]{:S(2)}, u32[]{:S(2)}) collective-permute-start(f32[2,32,256]{2,1,0:T(8,128)S(1)} %pad_maximum_fusion.2), channel_id=1, source_target_pairs={{0,8},{1,9},{2,10},{3,11},{16,24},{17,25},{18,26},{19,27},{32,40},... | collective-permute-start | bytes 196616 | tf_op jit(solution)/shard_map/ppermute | solution.py:345
  30.2 1.3 collective-permute-start.5
  31.5 1.2 fusion.6
  32.6 1.3 collective-permute-start.10
  33.9 3.6 %collective-permute-start.9 = (f32[256,256]{1,0:T(8,128)S(1)}, f32[256,256]{1,0:T(8,128)S(1)}, u32[]{:S(2)}, u32[]{:S(2)}) collective-permute-start(f32[256,256]{1,0:T(8,128)S(1)} %get-tuple-element.28), channel_id=1, source_target_pairs={{0,128},{16,144},{32,160},{1,129},{17,145},{33,161},{2,130},{18,14... | collective-permute-start | bytes 786440 | tf_op jit(solution)/shard_map/ppermute | solution.py:355
  37.5 0.0 collective-permute-done.7
  37.5 1.7 %collective-permute-start.8 = (f32[256,256]{1,0:T(8,128)S(1)}, f32[256,256]{1,0:T(8,128)S(1)}, u32[]{:S(2)}, u32[]{:S(2)}) collective-permute-start(f32[256,256]{1,0:T(8,128)S(1)} %get-tuple-element.29), channel_id=1, source_target_pairs={{0,192},{16,208},{32,224},{1,193},{17,209},{33,225},{2,194},{18,21... | collective-permute-start | bytes 786440 | tf_op jit(solution)/shard_map/ppermute | solution.py:355
  39.3 0.0 collective-permute-done.5
  39.3 5.5 %collective-permute-done.9 = f32[256,256]{1,0:T(8,128)S(1)} collective-permute-done((f32[256,256]{1,0:T(8,128)S(1)}, f32[256,256]{1,0:T(8,128)S(1)}, u32[]{:S(2)}, u32[]{:S(2)}) %collective-permute-start.9) | collective-permute-done | bytes 262176 | tf_op jit(solution)/shard_map/ppermute | solution.py:355
  44.9 1.7 %select_select_fusion.1 = f32[256,256]{1,0:T(8,128)} fusion(f32[256,256]{1,0:T(8,128)S(1)} %collective-permute-done.8, f32[256,256]{1,0:T(8,128)S(1)} %collective-permute-done.9, f32[256,256]{1,0:T(8,128)S(1)} %collective-permute-done.10, f32[1024,1024]{1,0:T(8,128)} %a.1, pred[]{:T(512)S(6)} %eq.72, pred[]{:T(512)S(6)} %eq.71, pred[]{:T(512)S(6)} %eq.70, ...), kind=kLoop, calls=%fused_computation.2 | loop fusion | flops 262144 | bytes 1310724 | tf_op jit(solution)/shard_map/jit(_where)/select_n | solution.py:333
  46.6 0.0 all-gather.3.cloned.1.call-update
  46.6 0.1 slice_select_fusion
  46.7 1.3 collective-permute-start.13
  48.0 1.3 collective-permute-start.12
  49.3 1.3 collective-permute-start.11
  50.7 1.1 broadcast_in_dim.25
  51.8 7.5 %all-to-all-start = ((f32[16,2,32,256]{3,2,1,0:T(8,128)}), f32[16,2,32,256]{3,2,1,0:T(8,128)S(1)}, u32[]{:S(2)}, u32[]{:S(2)}) async-start(f32[16,2,32,256]{3,2,1,0:T(8,128)} %broadcast_in_dim.25), calls=%async_computation | async-start | bytes 2097152 | tf_op jit(solution)/shard_map/all_to_all | solution.py:327
  59.3 2.4 %collective-permute-done.11 = f32[2,128,256]{2,1,0:T(8,128)S(1)} collective-permute-done((f32[2,128,256]{2,1,0:T(8,128)S(1)}, f32[2,128,256]{2,1,0:T(8,128)S(1)}, u32[]{:S(2)}, u32[]{:S(2)}) %collective-permute-start.11) | collective-permute-done | bytes 262176 | tf_op jit(solution)/shard_map/ppermute | solution.py:370
  61.7 0.1 select_select_fusion
  61.8 1.3 collective-permute-start.14
  63.1 1.9 %collective-permute-done.14 = f32[128,256]{1,0:T(8,128)S(1)} collective-permute-done((f32[128,256]{1,0:T(8,128)S(1)}, f32[128,256]{1,0:T(8,128)S(1)}, u32[]{:S(2)}, u32[]{:S(2)}) %collective-permute-start.14) | collective-permute-done | bytes 131104 | tf_op jit(solution)/shard_map/ppermute | solution.py:376
  65.1 1.3 collective-permute-start.15
  66.4 5.4 %collective-permute-done.15 = f32[64,256]{1,0:T(8,128)S(1)} collective-permute-done((f32[64,256]{1,0:T(8,128)S(1)}, f32[64,256]{1,0:T(8,128)S(1)}, u32[]{:S(2)}, u32[]{:S(2)}) %collective-permute-start.15) | collective-permute-done | bytes 65568 | tf_op jit(solution)/shard_map/ppermute | solution.py:379
  71.8 6.6 %all-to-all-done.mine = f32[16,2,32,256]{3,2,1,0:T(8,128)S(1)} async-done(((f32[16,2,32,256]{3,2,1,0:T(8,128)}), f32[16,2,32,256]{3,2,1,0:T(8,128)S(1)}, u32[]{:S(2)}, u32[]{:S(2)}) %all-to-all-start) | async-done | bytes 1048608 | tf_op jit(solution)/shard_map/all_to_all | solution.py:327
  78.4 1.8 %collective-permute-start.16 = (f32[16,2,32,256]{3,2,1,0:T(8,128)S(1)}, f32[16,2,32,256]{3,2,1,0:T(8,128)}, u32[]{:S(2)}, u32[]{:S(2)}) collective-permute-start(f32[16,2,32,256]{3,2,1,0:T(8,128)S(1)} %all-to-all-done.mine), channel_id=1, source_target_pairs={{0,1},{1,0},{2,3},{3,2},{4,5},{5,4},{6,7},{7,6},{8,9},{9,8},{10,11... | collective-permute-start | bytes 3145736 | tf_op jit(solution)/shard_map/ppermute | solution.py:342
  80.2 0.6 pad_add_fusion.where
  80.8 1.3 broadcast_in_dim.26
  82.1 3.6 %all-to-all-start.1 = ((f32[8,192,256]{2,1,0:T(8,128)}), f32[8,192,256]{2,1,0:T(8,128)S(1)}, u32[]{:S(2)}, u32[]{:S(2)}) async-start(f32[8,192,256]{2,1,0:T(8,128)} %broadcast_in_dim.26), calls=%async_computation.1 | async-start | bytes 3145728 | tf_op jit(solution)/shard_map/all_to_all | solution.py:327
  85.7 28.4 %shard_map.17 = (f32[3,256,256]{2,1,0:T(8,128)}, f32[3,256,256]{2,1,0:T(8,128)}, f32[3,256,256]{2,1,0:T(8,128)}) custom-call(s32[3]{0:T(128)} %pad_add_fusion.where, f32[16,2,32,256]{3,2,1,0:T(8,128)} %copy-done.1, f32[16,2,32,256]{3,2,1,0:T(8,128)} %collective-permute-done.16.other), custom_call_target="tpu_custom_call" | custom-call | flops 30000001024 | bytes 1000000 | tf_op jit(solution)/shard_map/pallas_call | solution.py:167
  114.1 9.9 %shard_map.18.q = bf16[1792,1024]{1,0:T(8,128)(2,1)} custom-call(f32[16,256,256]{2,1,0:T(8,128)} %bitcast.28, f32[3,256,256]{2,1,0:T(8,128)} %get-tuple-element.20.inverses, f32[3,256,256]{2,1,0:T(8,128)} %get-tuple-element.21.sides), custom_call_target="tpu_custom_call" | custom-call | flops 10000000000 | bytes 10000000 | tf_op jit(solution)/shard_map/pallas_call | solution.py:225
  124.0 2.1 %all-to-all-done.1.mine = f32[8,192,256]{2,1,0:T(8,128)S(1)} async-done(((f32[8,192,256]{2,1,0:T(8,128)}), f32[8,192,256]{2,1,0:T(8,128)S(1)}, u32[]{:S(2)}, u32[]{:S(2)}) %all-to-all-start.1) | async-done | bytes 1572896 | tf_op jit(solution)/shard_map/all_to_all | solution.py:327
  126.1 0.4 collective-permute-start.17
  126.5 3.0 %collective-permute-done.17.other = f32[8,192,256]{2,1,0:T(8,128)S(1)} collective-permute-done((f32[8,192,256]{2,1,0:T(8,128)S(1)}, f32[8,192,256]{2,1,0:T(8,128)S(1)}, u32[]{:S(2)}, u32[]{:S(2)}) %collective-permute-start.17) | collective-permute-done | bytes 1572896 | tf_op jit(solution)/shard_map/ppermute | solution.py:342
  129.6 1.1 copy-done.2
  130.7 20.1 %shard_map.19 = f32[1024,1024]{1,0:T(8,128)} custom-call(s32[3]{0:T(128)} %pad_add_fusion.where, f32[1024,1024]{1,0:T(8,128)} %a.1, f32[8,192,256]{2,1,0:T(8,128)} %copy-done, f32[8,192,256]{2,1,0:T(8,128)} %copy-done.2, bf16[1792,1024]{1,0:T(8,128)(2,1)} %shard_map.18.q, f32[3,256,256]{2,1,0:T(8,128)} %get-tuple-element.24.factors, ...), custom_call_target="tpu_custom_call" | custom-call | flops 20000000000 | bytes 10000000 | tf_op jit(solution)/shard_map/pallas_call | solution.py:303
  (28 shorter events, 0.2 us)
Async XLA Ops:
  6.5 40.1 %slice-start = ((f32[1024,1024]{1,0:T(8,128)}), f32[1024,256]{1,0:T(8,128)S(1)}, s32[]{:S(2)}) async-start(f32[1024,1024]{1,0:T(8,128)} %a.1), calls=%async_computation.3 | async-start | bytes 2097152 | tf_op jit(solution)/shard_map/slice | solution.py:354
  6.5 107.5 %all-gather.3.cloned.1.call-start = ((), (), s32[]{:S(2)}) async-start(), calls=%async_computation.2 | async-start | bytes 4456448 | tf_op jit(solution)/shard_map/all_gather | solution.py:372
  7.5 7.7 %collective-permute-start.2 = (f32[64,256]{1,0:T(8,128)S(1)}, f32[64,256]{1,0:T(8,128)S(1)}, u32[]{:S(2)}, u32[]{:S(2)}) collective-permute-start(f32[64,256]{1,0:T(8,128)S(1)} %get-tuple-element.30), channel_id=1, source_target_pairs={{0,64},{16,80},{32,96},{1,65},{17,81},{33,97},{2,66},{18,82},{34,9... | collective-permute-start | bytes 196616 | tf_op jit(solution)/shard_map/ppermute | solution.py:355
  11.6 3.6 %collective-permute-start.1 = (f32[64,256]{1,0:T(8,128)S(1)}, f32[64,256]{1,0:T(8,128)S(1)}, u32[]{:S(2)}, u32[]{:S(2)}) collective-permute-start(f32[64,256]{1,0:T(8,128)S(1)} %get-tuple-element.31), channel_id=1, source_target_pairs={{0,128},{16,144},{32,160},{1,129},{17,145},{33,161},{2,130},{18,14... | collective-permute-start | bytes 196616 | tf_op jit(solution)/shard_map/ppermute | solution.py:355
  13.9 2.6 %collective-permute-start = (f32[64,256]{1,0:T(8,128)S(1)}, f32[64,256]{1,0:T(8,128)S(1)}, u32[]{:S(2)}, u32[]{:S(2)}) collective-permute-start(f32[64,256]{1,0:T(8,128)S(1)} %get-tuple-element.32), channel_id=1, source_target_pairs={{0,192},{16,208},{32,224},{1,193},{17,209},{33,225},{2,194},{18,21... | collective-permute-start | bytes 196616 | tf_op jit(solution)/shard_map/ppermute | solution.py:355
  17.4 2.5 %collective-permute-start.3 = (f32[32,256]{1,0:T(8,128)S(1)}, f32[32,256]{1,0:T(8,128)S(1)}, u32[]{:S(2)}, u32[]{:S(2)}) collective-permute-start(f32[32,256]{1,0:T(8,128)S(1)} %constant_dynamic-slice_fusion), channel_id=1, source_target_pairs={{0,1},{1,0},{2,3},{3,2},{4,5},{5,4},{6,7},{7,6},{8,9},{9,8},{10,11... | collective-permute-start | bytes 98312 | tf_op jit(solution)/shard_map/ppermute | solution.py:342
  19.9 5.6 %collective-permute-start.4 = (f32[2,32,256]{2,1,0:T(8,128)S(1)}, f32[2,32,256]{2,1,0:T(8,128)S(1)}, u32[]{:S(2)}, u32[]{:S(2)}) collective-permute-start(f32[2,32,256]{2,1,0:T(8,128)S(1)} %pad_maximum_fusion.1), channel_id=1, source_target_pairs={{0,2},{1,3},{2,0},{3,1},{16,18},{17,19},{18,16},{19,17},{32,34},{3... | collective-permute-start | bytes 196616 | tf_op jit(solution)/shard_map/ppermute | solution.py:360
  25.5 12.0 %collective-permute-start.7 = (f32[2,32,256]{2,1,0:T(8,128)S(1)}, f32[2,32,256]{2,1,0:T(8,128)S(1)}, u32[]{:S(2)}, u32[]{:S(2)}) collective-permute-start(f32[2,32,256]{2,1,0:T(8,128)S(1)} %pad_maximum_fusion.2), channel_id=1, source_target_pairs={{0,4},{1,5},{2,6},{3,7},{16,20},{17,21},{18,22},{19,23},{32,36},{3... | collective-permute-start | bytes 196616 | tf_op jit(solution)/shard_map/ppermute | solution.py:345
  26.8 12.4 %collective-permute-start.6 = (f32[2,32,256]{2,1,0:T(8,128)S(1)}, f32[2,32,256]{2,1,0:T(8,128)S(1)}, u32[]{:S(2)}, u32[]{:S(2)}) collective-permute-start(f32[2,32,256]{2,1,0:T(8,128)S(1)} %pad_maximum_fusion.2), channel_id=1, source_target_pairs={{0,8},{1,9},{2,10},{3,11},{16,24},{17,25},{18,26},{19,27},{32,40},... | collective-permute-start | bytes 196616 | tf_op jit(solution)/shard_map/ppermute | solution.py:345
  30.2 9.1 %collective-permute-start.5 = (f32[2,32,256]{2,1,0:T(8,128)S(1)}, f32[2,32,256]{2,1,0:T(8,128)S(1)}, u32[]{:S(2)}, u32[]{:S(2)}) collective-permute-start(f32[2,32,256]{2,1,0:T(8,128)S(1)} %pad_maximum_fusion.2), channel_id=1, source_target_pairs={{0,12},{1,13},{2,14},{3,15},{16,28},{17,29},{18,30},{19,31},{32,44... | collective-permute-start | bytes 196616 | tf_op jit(solution)/shard_map/ppermute | solution.py:345
  32.6 6.7 %collective-permute-start.10 = (f32[256,256]{1,0:T(8,128)S(1)}, f32[256,256]{1,0:T(8,128)S(1)}, u32[]{:S(2)}, u32[]{:S(2)}) collective-permute-start(f32[256,256]{1,0:T(8,128)S(1)} %get-tuple-element.27), channel_id=1, source_target_pairs={{0,64},{16,80},{32,96},{1,65},{17,81},{33,97},{2,66},{18,82},{34,9... | collective-permute-start | bytes 786440 | tf_op jit(solution)/shard_map/ppermute | solution.py:355
  33.9 10.9 %collective-permute-start.9 = (f32[256,256]{1,0:T(8,128)S(1)}, f32[256,256]{1,0:T(8,128)S(1)}, u32[]{:S(2)}, u32[]{:S(2)}) collective-permute-start(f32[256,256]{1,0:T(8,128)S(1)} %get-tuple-element.28), channel_id=1, source_target_pairs={{0,128},{16,144},{32,160},{1,129},{17,145},{33,161},{2,130},{18,14... | collective-permute-start | bytes 786440 | tf_op jit(solution)/shard_map/ppermute | solution.py:355
  37.5 7.3 %collective-permute-start.8 = (f32[256,256]{1,0:T(8,128)S(1)}, f32[256,256]{1,0:T(8,128)S(1)}, u32[]{:S(2)}, u32[]{:S(2)}) collective-permute-start(f32[256,256]{1,0:T(8,128)S(1)} %get-tuple-element.29), channel_id=1, source_target_pairs={{0,192},{16,208},{32,224},{1,193},{17,209},{33,225},{2,194},{18,21... | collective-permute-start | bytes 786440 | tf_op jit(solution)/shard_map/ppermute | solution.py:355
  46.7 12.6 %collective-permute-start.13 = (f32[2,128,256]{2,1,0:T(8,128)S(1)}, f32[2,128,256]{2,1,0:T(8,128)S(1)}, u32[]{:S(2)}, u32[]{:S(2)}) collective-permute-start(f32[2,128,256]{2,1,0:T(8,128)S(1)} %bitcast.27), channel_id=1, source_target_pairs={{0,4},{1,5},{2,6},{16,20},{17,21},{18,22},{32,36},{33,37},{34,38},... | collective-permute-start | bytes 786440 | tf_op jit(solution)/shard_map/ppermute | solution.py:370
  48.0 11.3 %collective-permute-start.12 = (f32[2,128,256]{2,1,0:T(8,128)S(1)}, f32[2,128,256]{2,1,0:T(8,128)S(1)}, u32[]{:S(2)}, u32[]{:S(2)}) collective-permute-start(f32[2,128,256]{2,1,0:T(8,128)S(1)} %bitcast.26), channel_id=1, source_target_pairs={{0,8},{1,9},{2,10},{16,24},{17,25},{18,26},{32,40},{33,41},{34,42}... | collective-permute-start | bytes 786440 | tf_op jit(solution)/shard_map/ppermute | solution.py:370
  49.3 12.4 %collective-permute-start.11 = (f32[2,128,256]{2,1,0:T(8,128)S(1)}, f32[2,128,256]{2,1,0:T(8,128)S(1)}, u32[]{:S(2)}, u32[]{:S(2)}) collective-permute-start(f32[2,128,256]{2,1,0:T(8,128)S(1)} %bitcast.25), channel_id=1, source_target_pairs={{0,12},{1,13},{2,14},{16,28},{17,29},{18,30},{32,44},{33,45},{34,4... | collective-permute-start | bytes 786440 | tf_op jit(solution)/shard_map/ppermute | solution.py:370
  51.8 26.6 %all-to-all-start = ((f32[16,2,32,256]{3,2,1,0:T(8,128)}), f32[16,2,32,256]{3,2,1,0:T(8,128)S(1)}, u32[]{:S(2)}, u32[]{:S(2)}) async-start(f32[16,2,32,256]{3,2,1,0:T(8,128)} %broadcast_in_dim.25), calls=%async_computation | async-start | bytes 2097152 | tf_op jit(solution)/shard_map/all_to_all | solution.py:327
  61.8 3.2 %collective-permute-start.14 = (f32[128,256]{1,0:T(8,128)S(1)}, f32[128,256]{1,0:T(8,128)S(1)}, u32[]{:S(2)}, u32[]{:S(2)}) collective-permute-start(f32[128,256]{1,0:T(8,128)S(1)} %fusion.1), channel_id=1, source_target_pairs={{0,2},{1,3},{2,0},{4,6},{5,7},{6,4},{8,10},{9,11},{10,8},{12,14},{... | collective-permute-start | bytes 393224 | tf_op jit(solution)/shard_map/ppermute | solution.py:376
  65.1 6.7 %collective-permute-start.15 = (f32[64,256]{1,0:T(8,128)S(1)}, f32[64,256]{1,0:T(8,128)S(1)}, u32[]{:S(2)}, u32[]{:S(2)}) collective-permute-start(f32[64,256]{1,0:T(8,128)S(1)} %slice.104), channel_id=1, source_target_pairs={{0,1},{2,3},{4,5},{6,7},{8,9},{10,11},{12,13},{14,15},{16,17},{18,... | collective-permute-start | bytes 196616 | tf_op jit(solution)/shard_map/ppermute | solution.py:379
  78.4 7.3 %copy-start.1 = (f32[16,2,32,256]{3,2,1,0:T(8,128)}, f32[16,2,32,256]{3,2,1,0:T(8,128)S(1)}, u32[]{:S(2)}) copy-start(f32[16,2,32,256]{3,2,1,0:T(8,128)S(1)} %all-to-all-done.mine) | copy-start | bytes 3145732
  78.4 7.3 %collective-permute-start.16 = (f32[16,2,32,256]{3,2,1,0:T(8,128)S(1)}, f32[16,2,32,256]{3,2,1,0:T(8,128)}, u32[]{:S(2)}, u32[]{:S(2)}) collective-permute-start(f32[16,2,32,256]{3,2,1,0:T(8,128)S(1)} %all-to-all-done.mine), channel_id=1, source_target_pairs={{0,1},{1,0},{2,3},{3,2},{4,5},{5,4},{6,7},{7,6},{8,9},{9,8},{10,11... | collective-permute-start | bytes 3145736 | tf_op jit(solution)/shard_map/ppermute | solution.py:342
  82.1 44.0 %all-to-all-start.1 = ((f32[8,192,256]{2,1,0:T(8,128)}), f32[8,192,256]{2,1,0:T(8,128)S(1)}, u32[]{:S(2)}, u32[]{:S(2)}) async-start(f32[8,192,256]{2,1,0:T(8,128)} %broadcast_in_dim.26), calls=%async_computation.1 | async-start | bytes 3145728 | tf_op jit(solution)/shard_map/all_to_all | solution.py:327
  126.1 3.5 %copy-start = (f32[8,192,256]{2,1,0:T(8,128)}, f32[8,192,256]{2,1,0:T(8,128)S(1)}, u32[]{:S(2)}) copy-start(f32[8,192,256]{2,1,0:T(8,128)S(1)} %all-to-all-done.1.mine) | copy-start | bytes 4718596
  126.1 3.5 %collective-permute-start.17 = (f32[8,192,256]{2,1,0:T(8,128)S(1)}, f32[8,192,256]{2,1,0:T(8,128)S(1)}, u32[]{:S(2)}, u32[]{:S(2)}) collective-permute-start(f32[8,192,256]{2,1,0:T(8,128)S(1)} %all-to-all-done.1.mine), channel_id=1, source_target_pairs={{0,1},{1,0},{2,3},{3,2},{4,5},{5,4},{6,7},{7,6},{8,9},{9,8},{10,11... | collective-permute-start | bytes 4718600 | tf_op jit(solution)/shard_map/ppermute | solution.py:342
  129.6 1.1 copy-start.2
Sparse Core Ops, SparseCore 0:
  46.7 59.9 all-gather.2

commit v4 on v3

--- a/solution.py
+++ b/solution.py
@@ -233,42 +233,51 @@
 
 
 def update_kernel(
-    where, a, mine, other, q, factors, inverses, sides, out, panel, block, right0, right1, rights
+    where, a, mine, other, q_far, factors, inverses, sides, out,
+    panel_all, block, right0, right1, rights, q, arrival
 ):
     r, c, core = where[0], where[1], where[2]
     t = pl.program_id(0)
 
+    fetch = pltpu.make_async_copy(q_far, q, arrival)
+
     @pl.when(t == 0)
     def _():
+        fetch.start()
         stack(right0, inverses[0].T, 3)
         stack(right1, jnp.concatenate([sides[0].T, sides[1].T], axis=1), 3)
         for i, value in enumerate((inverses[1], sides[2], inverses[2])):
             stack(rights.at[i], value.T, 2)
 
     def place(lower, upper):
-        for i in range(2):
-            z, rows = 2 * t + i, 128 * i
+        for z in range(8):
+            rows = 128 * z
             block[rows : rows + 128, :TILE] = lower[z, :128]
             block[rows : rows + 128, TILE : 2 * TILE] = upper[z, :128]
             block[rows : rows + 64, 2 * TILE :] = lower[z, 128:]
             block[rows + 64 : rows + 128, 2 * TILE :] = upper[z, 128:]
 
-    @pl.when(core == 0)
+    @pl.when((t == 0) & (core == 0))
     def _():
         place(mine, other)
 
-    @pl.when(core != 0)
+    @pl.when((t == 0) & (core != 0))
     def _():
         place(other, mine)
 
-    p0 = times(block[:, :TILE], right0, 3)
-    removed = times(p0, right1, 3)
-    p1 = times(block[:, TILE : 2 * TILE] - removed[:, :TILE], rights.at[0], 2)
-    p2 = block[:, 2 * TILE :] - removed[:, TILE:] - times(p1, rights.at[1], 2)
-    p2 = times(p2, rights.at[2], 2)
-    panel[:, :TILE] = p0
-    panel[:, TILE : 2 * TILE] = p1
-    panel[:, 2 * TILE :] = p2
+    @pl.when(t == 0)
+    def _():
+        p0 = times(block[:, :TILE], right0, 3)
+        panel_all[:, :TILE] = p0
+        removed = times(p0, right1, 3)
+        p1 = times(block[:, TILE : 2 * TILE] - removed[:, :TILE], rights.at[0], 2)
+        panel_all[:, TILE : 2 * TILE] = p1
+        p2 = block[:, 2 * TILE :] - removed[:, TILE:] - times(p1, rights.at[1], 2)
+        panel_all[:, 2 * TILE :] = times(p2, rights.at[2], 2)
+        fetch.wait()
+
+    panel = panel_all.at[pl.ds(pl.multiple_of(t * TILE, TILE), TILE)]
+    p0 = panel[:, :TILE]
 
     first, second, third = parts(p0, 3)
     high, low = parts(panel[:, TILE:], 2)
@@ -304,14 +313,18 @@
         update_kernel,
         grid=(4,),
         out_shape=jax.ShapeDtypeStruct(matrix.shape, jnp.float32),
-        in_specs=[SMEM, row_tile] + [whole(x) for x in operands],
+        in_specs=[SMEM, row_tile] + [whole(x) for x in operands[:2]]
+        + [pl.BlockSpec(memory_space=pl.ANY)]
+        + [whole(x) for x in operands[3:]],
         out_specs=row_tile,
         scratch_shapes=[
-            pltpu.VMEM((TILE, LEAD), jnp.float32),
-            pltpu.VMEM((TILE, LEAD), jnp.float32),
+            pltpu.VMEM((4 * TILE, LEAD), jnp.float32),
+            pltpu.VMEM((4 * TILE, LEAD), jnp.float32),
             pltpu.VMEM((3 * TILE, TILE), jnp.bfloat16),
             pltpu.VMEM((3 * TILE, 2 * TILE), jnp.bfloat16),
             pltpu.VMEM((STEPS, 2 * TILE, TILE), jnp.bfloat16),
+            pltpu.VMEM((7 * TILE, 4 * TILE), jnp.bfloat16),
+            pltpu.SemaphoreType.DMA,
         ],
         compiler_params=pltpu.CompilerParams(vmem_limit_bytes=56 * 2**20),
         cost_estimate=pl.CostEstimate(flops=2 * 10**10, bytes_accessed=10**7, transcendentals=0),
@@ -322,9 +335,12 @@
     return lax.optimization_barrier((value,) + others)[0]
 
 
-def gather(value, axis, groups):
-    copies = jnp.broadcast_to(value[None], (len(groups[0]),) + value.shape)
-    return lax.all_to_all(copies, axis, 0, 0, axis_index_groups=groups)
+def copies(value, groups):
+    return jnp.broadcast_to(value[None], (len(groups[0]),) + value.shape)
+
+
+def gather(copied, axis, groups):
+    return lax.all_to_all(copied, axis, 0, 0, axis_index_groups=groups)
 
 
 def choose(index, values):
@@ -370,7 +386,7 @@
     sent = [chunks[0]] + [lax.ppermute(chunks[i], "col", FAR[i][:3]) for i in (1, 2, 3)]
     two, column = lax.optimization_barrier((two, column))
     e = lax.all_gather(column, "row")
-    lead_mine = gather(two, "row", ROW_GROUP)
+    lead_mine = gather(copies(two, ROW_GROUP), "row", ROW_GROUP)
 
     couple = choose(z // 2, sent)
     got = lax.ppermute(jnp.where(z % 2 == 0, couple[1], couple[0]), "col", EXCHANGE)
@@ -378,9 +394,10 @@
     third = jnp.where(z % 2 == 0, got, couple[1])
     got = lax.ppermute(third[64:], "col", [(2 * i, 2 * i + 1) for i in range(8)])
     my_chunk = jnp.concatenate([first, jnp.where(core == 0, third[:64], got)])
-    lead_mine, my_chunk = lax.optimization_barrier((lead_mine, my_chunk))
+    chunk_copies = copies(my_chunk, Z_GROUPS)
+    lead_mine, chunk_copies = lax.optimization_barrier((lead_mine, chunk_copies))
     lead_other = swap(lead_mine)
-    rows_mine = gather(my_chunk, "col", Z_GROUPS)
+    rows_mine = gather(chunk_copies, "col", Z_GROUPS)
     factors, inverses, sides = factorize(where, lead_mine, lead_other)
     q = across(e, inverses, sides)
     rows_mine, q = lax.optimization_barrier((rows_mine, q))

time: 158 us -> 156 us (0.987)
  Pallas kernels: 58.4 us -> 56.3 us
  starting transfers between devices: 45.1 us -> 47.1 us
  waiting for transfers between devices: 31.1 us -> 29.1 us
    pallas_call x1, Pallas kernels: 20.1 us -> 18 us  [update(): pl.pallas_call(update_kernel, grid=(4,), out_shape=jax.ShapeDtypeStruct(m...]
    ppermute x3, starting transfers between devices: 3.85 us -> 5.85 us  [on_device(): swap = lambda value: lax.ppermute(value, 'col', CORE_SWAP)]
    all_to_all x2, waiting for transfers between devices: 8.66 us -> 6.69 us  [gather(): return lax.all_to_all(copied, axis, 0, 0, axis_index_groups=groups)]
  transfers between devices with their start and end apart: 21 -> 21, of which waited for: 10 -> 10; matrix products, arithmetic and copies ran while one was open for 3% -> 3% of each run, Pallas kernels for 24% -> 25%
where the time goes in v4:
time: 156 us
  Pallas kernels  56.3 us (36%)
  starting transfers between devices  47.1 us (30%)
  waiting for transfers between devices  29.1 us (19%)
  between operations  13.9 us (9%)
  local copies, waits for them, and re-layouts  5.84 us (4%)
  other arithmetic  3.49 us (2%)
    pallas_call x1, Pallas kernels, factorize(): pl.pallas_call(lead_kernel, out_shape=(three, three, three), in_specs=[SM...  28.3 us
    pallas_call x1, Pallas kernels, update(): pl.pallas_call(update_kernel, grid=(4,), out_shape=jax.ShapeDtypeStruct(m...  18 us
    ppermute x6, starting transfers between devices, on_device(): lax.ppermute(value, 'row', [(x0, 4 * s + x0) for x0 in range(3)])  14.2 us
    all_to_all x2, starting transfers between devices, gather(): return lax.all_to_all(copied, axis, 0, 0, axis_index_groups=groups)  11.1 us
    pallas_call x1, Pallas kernels, across(): pl.pallas_call(across_kernel, out_shape=jax.ShapeDtypeStruct((7 * TILE, 4...  9.92 us
    ppermute x6, waiting for transfers between devices, on_device(): lax.ppermute(value, 'row', [(x0, 4 * s + x0) for x0 in range(3)])  6.8 us
    all_to_all x2, waiting for transfers between devices, gather(): return lax.all_to_all(copied, axis, 0, 0, axis_index_groups=groups)  6.69 us
    ppermute x3, starting transfers between devices, spread(): sent = [lax.ppermute(values[i], 'col', FAR[i]) for i in (1, 2, 3)]  5.89 us
  transfers between devices with their start and end apart: 21, of which 10 were waited for; matrix products, arithmetic and copies ran while one was open for 3% of the time, Pallas kernels for 25%

profile of v4, /device:TPU:1, one launch (start us, length us, event | category | flops | bytes accessed | tf_op | source)
XLA Modules:
  0.0 155.7 jit_solution(4237995117412718759)
XLA Ops:
  6.5 1.0 fusion.7
  7.5 4.0 %collective-permute-start.2 = (f32[64,256]{1,0:T(8,128)S(1)}, f32[64,256]{1,0:T(8,128)S(1)}, u32[]{:S(2)}, u32[]{:S(2)}) collective-permute-start(f32[64,256]{1,0:T(8,128)S(1)} %get-tuple-element.30), channel_id=1, source_target_pairs={{0,64},{16,80},{32,96},{1,65},{17,81},{33,97},{2,66},{18,82},{34,9... | collective-permute-start | bytes 196616 | tf_op jit(solution)/shard_map/ppermute | solution.py:371
  11.6 2.3 %collective-permute-start.1 = (f32[64,256]{1,0:T(8,128)S(1)}, f32[64,256]{1,0:T(8,128)S(1)}, u32[]{:S(2)}, u32[]{:S(2)}) collective-permute-start(f32[64,256]{1,0:T(8,128)S(1)} %get-tuple-element.31), channel_id=1, source_target_pairs={{0,128},{16,144},{32,160},{1,129},{17,145},{33,161},{2,130},{18,14... | collective-permute-start | bytes 196616 | tf_op jit(solution)/shard_map/ppermute | solution.py:371
  13.9 1.3 collective-permute-start
  15.2 0.0 collective-permute-done.2
  15.2 0.0 collective-permute-done.1
  15.2 1.2 collective-permute-done
  16.5 0.9 select_select_fusion.3
  17.4 1.6 %collective-permute-start.3 = (f32[32,256]{1,0:T(8,128)S(1)}, f32[32,256]{1,0:T(8,128)S(1)}, u32[]{:S(2)}, u32[]{:S(2)}) collective-permute-start(f32[32,256]{1,0:T(8,128)S(1)} %constant_dynamic-slice_fusion), channel_id=1, source_target_pairs={{0,1},{1,0},{2,3},{3,2},{4,5},{5,4},{6,7},{7,6},{8,9},{9,8},{10,11... | collective-permute-start | bytes 98312 | tf_op jit(solution)/shard_map/ppermute | solution.py:358
  19.0 0.9 collective-permute-done.3
  19.9 3.5 %collective-permute-start.4 = (f32[2,32,256]{2,1,0:T(8,128)S(1)}, f32[2,32,256]{2,1,0:T(8,128)S(1)}, u32[]{:S(2)}, u32[]{:S(2)}) collective-permute-start(f32[2,32,256]{2,1,0:T(8,128)S(1)} %pad_maximum_fusion.1), channel_id=1, source_target_pairs={{0,2},{1,3},{2,0},{3,1},{16,18},{17,19},{18,16},{19,17},{32,34},{3... | collective-permute-start | bytes 196616 | tf_op jit(solution)/shard_map/ppermute | solution.py:376
  23.5 2.0 %collective-permute-done.4 = f32[2,32,256]{2,1,0:T(8,128)S(1)} collective-permute-done((f32[2,32,256]{2,1,0:T(8,128)S(1)}, f32[2,32,256]{2,1,0:T(8,128)S(1)}, u32[]{:S(2)}, u32[]{:S(2)}) %collective-permute-start.4) | collective-permute-done | bytes 65568 | tf_op jit(solution)/shard_map/ppermute | solution.py:376
  25.5 1.3 collective-permute-start.7
  26.8 3.3 %collective-permute-start.6 = (f32[2,32,256]{2,1,0:T(8,128)S(1)}, f32[2,32,256]{2,1,0:T(8,128)S(1)}, u32[]{:S(2)}, u32[]{:S(2)}) collective-permute-start(f32[2,32,256]{2,1,0:T(8,128)S(1)} %pad_maximum_fusion.2), channel_id=1, source_target_pairs={{0,8},{1,9},{2,10},{3,11},{16,24},{17,25},{18,26},{19,27},{32,40},... | collective-permute-start | bytes 196616 | tf_op jit(solution)/shard_map/ppermute | solution.py:361
  30.2 1.3 collective-permute-start.5
  31.5 1.2 fusion.6
  32.6 1.3 collective-permute-start.10
  33.9 3.6 %collective-permute-start.9 = (f32[256,256]{1,0:T(8,128)S(1)}, f32[256,256]{1,0:T(8,128)S(1)}, u32[]{:S(2)}, u32[]{:S(2)}) collective-permute-start(f32[256,256]{1,0:T(8,128)S(1)} %get-tuple-element.28), channel_id=1, source_target_pairs={{0,128},{16,144},{32,160},{1,129},{17,145},{33,161},{2,130},{18,14... | collective-permute-start | bytes 786440 | tf_op jit(solution)/shard_map/ppermute | solution.py:371
  37.5 0.0 collective-permute-done.7
  37.5 1.7 %collective-permute-start.8 = (f32[256,256]{1,0:T(8,128)S(1)}, f32[256,256]{1,0:T(8,128)S(1)}, u32[]{:S(2)}, u32[]{:S(2)}) collective-permute-start(f32[256,256]{1,0:T(8,128)S(1)} %get-tuple-element.29), channel_id=1, source_target_pairs={{0,192},{16,208},{32,224},{1,193},{17,209},{33,225},{2,194},{18,21... | collective-permute-start | bytes 786440 | tf_op jit(solution)/shard_map/ppermute | solution.py:371
  39.3 0.0 collective-permute-done.5
  39.3 5.5 %collective-permute-done.9 = f32[256,256]{1,0:T(8,128)S(1)} collective-permute-done((f32[256,256]{1,0:T(8,128)S(1)}, f32[256,256]{1,0:T(8,128)S(1)}, u32[]{:S(2)}, u32[]{:S(2)}) %collective-permute-start.9) | collective-permute-done | bytes 262176 | tf_op jit(solution)/shard_map/ppermute | solution.py:371
  44.9 1.7 %select_select_fusion.1 = f32[256,256]{1,0:T(8,128)} fusion(f32[256,256]{1,0:T(8,128)S(1)} %collective-permute-done.8, f32[256,256]{1,0:T(8,128)S(1)} %collective-permute-done.9, f32[256,256]{1,0:T(8,128)S(1)} %collective-permute-done.10, f32[1024,1024]{1,0:T(8,128)} %a.1, pred[]{:T(512)S(6)} %eq.72, pred[]{:T(512)S(6)} %eq.71, pred[]{:T(512)S(6)} %eq.70, ...), kind=kLoop, calls=%fused_computation.2 | loop fusion | flops 262144 | bytes 1310724 | tf_op jit(solution)/shard_map/jit(_where)/select_n | solution.py:349
  46.6 0.0 all-gather.3.cloned.1.call-update
  46.6 0.1 slice_select_fusion
  46.7 1.3 collective-permute-start.13
  48.0 1.3 collective-permute-start.12
  49.3 1.3 collective-permute-start.11
  50.7 1.1 broadcast_in_dim.25
  51.8 7.5 %all-to-all-start = ((f32[16,2,32,256]{3,2,1,0:T(8,128)}), f32[16,2,32,256]{3,2,1,0:T(8,128)S(1)}, u32[]{:S(2)}, u32[]{:S(2)}) async-start(f32[16,2,32,256]{3,2,1,0:T(8,128)} %broadcast_in_dim.25), calls=%async_computation | async-start | bytes 2097152 | tf_op jit(solution)/shard_map/all_to_all | solution.py:343
  59.3 2.4 %collective-permute-done.11 = f32[2,128,256]{2,1,0:T(8,128)S(1)} collective-permute-done((f32[2,128,256]{2,1,0:T(8,128)S(1)}, f32[2,128,256]{2,1,0:T(8,128)S(1)}, u32[]{:S(2)}, u32[]{:S(2)}) %collective-permute-start.11) | collective-permute-done | bytes 262176 | tf_op jit(solution)/shard_map/ppermute | solution.py:386
  61.7 0.1 select_select_fusion
  61.8 1.3 collective-permute-start.14
  63.1 1.9 %collective-permute-done.14 = f32[128,256]{1,0:T(8,128)S(1)} collective-permute-done((f32[128,256]{1,0:T(8,128)S(1)}, f32[128,256]{1,0:T(8,128)S(1)}, u32[]{:S(2)}, u32[]{:S(2)}) %collective-permute-start.14) | collective-permute-done | bytes 131104 | tf_op jit(solution)/shard_map/ppermute | solution.py:392
  65.1 1.3 collective-permute-start.15
  66.4 5.4 %collective-permute-done.15 = f32[64,256]{1,0:T(8,128)S(1)} collective-permute-done((f32[64,256]{1,0:T(8,128)S(1)}, f32[64,256]{1,0:T(8,128)S(1)}, u32[]{:S(2)}, u32[]{:S(2)}) %collective-permute-start.15) | collective-permute-done | bytes 65568 | tf_op jit(solution)/shard_map/ppermute | solution.py:395
  71.8 6.6 %all-to-all-done.mine = f32[16,2,32,256]{3,2,1,0:T(8,128)S(1)} async-done(((f32[16,2,32,256]{3,2,1,0:T(8,128)}), f32[16,2,32,256]{3,2,1,0:T(8,128)S(1)}, u32[]{:S(2)}, u32[]{:S(2)}) %all-to-all-start) | async-done | bytes 1048608 | tf_op jit(solution)/shard_map/all_to_all | solution.py:343
  78.4 1.4 broadcast_in_dim.26
  79.8 1.8 %collective-permute-start.16 = (f32[16,2,32,256]{3,2,1,0:T(8,128)S(1)}, f32[16,2,32,256]{3,2,1,0:T(8,128)}, u32[]{:S(2)}, u32[]{:S(2)}) collective-permute-start(f32[16,2,32,256]{3,2,1,0:T(8,128)S(1)} %all-to-all-done.mine), channel_id=1, source_target_pairs={{0,1},{1,0},{2,3},{3,2},{4,5},{5,4},{6,7},{7,6},{8,9},{9,8},{10,11... | collective-permute-start | bytes 3145736 | tf_op jit(solution)/shard_map/ppermute | solution.py:358
  81.6 0.6 pad_add_fusion.where
  82.2 3.6 %all-to-all-start.1 = ((f32[8,192,256]{2,1,0:T(8,128)}), f32[8,192,256]{2,1,0:T(8,128)S(1)}, u32[]{:S(2)}, u32[]{:S(2)}) async-start(f32[8,192,256]{2,1,0:T(8,128)} %broadcast_in_dim.26), calls=%async_computation.1 | async-start | bytes 3145728 | tf_op jit(solution)/shard_map/all_to_all | solution.py:343
  85.8 28.3 %shard_map.17 = (f32[3,256,256]{2,1,0:T(8,128)}, f32[3,256,256]{2,1,0:T(8,128)}, f32[3,256,256]{2,1,0:T(8,128)}) custom-call(s32[3]{0:T(128)} %pad_add_fusion.where, f32[16,2,32,256]{3,2,1,0:T(8,128)} %copy-done.1, f32[16,2,32,256]{3,2,1,0:T(8,128)} %collective-permute-done.16.other), custom_call_target="tpu_custom_call" | custom-call | flops 30000001024 | bytes 1000000 | tf_op jit(solution)/shard_map/pallas_call | solution.py:167
  114.1 9.9 %shard_map.18.q_far = bf16[1792,1024]{1,0:T(8,128)(2,1)} custom-call(f32[16,256,256]{2,1,0:T(8,128)} %bitcast.28, f32[3,256,256]{2,1,0:T(8,128)} %get-tuple-element.20.inverses, f32[3,256,256]{2,1,0:T(8,128)} %get-tuple-element.21.sides), custom_call_target="tpu_custom_call" | custom-call | flops 10000000000 | bytes 10000000 | tf_op jit(solution)/shard_map/pallas_call | solution.py:225
  124.1 0.1 all-to-all-done.1.mine
  124.2 2.5 %collective-permute-start.17 = (f32[8,192,256]{2,1,0:T(8,128)S(1)}, f32[8,192,256]{2,1,0:T(8,128)S(1)}, u32[]{:S(2)}, u32[]{:S(2)}) collective-permute-start(f32[8,192,256]{2,1,0:T(8,128)S(1)} %all-to-all-done.1.mine), channel_id=1, source_target_pairs={{0,1},{1,0},{2,3},{3,2},{4,5},{5,4},{6,7},{7,6},{8,9},{9,8},{10,11... | collective-permute-start | bytes 4718600 | tf_op jit(solution)/shard_map/ppermute | solution.py:358
  126.6 3.0 %collective-permute-done.17.other = f32[8,192,256]{2,1,0:T(8,128)S(1)} collective-permute-done((f32[8,192,256]{2,1,0:T(8,128)S(1)}, f32[8,192,256]{2,1,0:T(8,128)S(1)}, u32[]{:S(2)}, u32[]{:S(2)}) %collective-permute-start.17) | collective-permute-done | bytes 1572896 | tf_op jit(solution)/shard_map/ppermute | solution.py:358
  129.7 1.1 copy-done.2
  130.8 18.0 %shard_map.19 = f32[1024,1024]{1,0:T(8,128)} custom-call(s32[3]{0:T(128)} %pad_add_fusion.where, f32[1024,1024]{1,0:T(8,128)} %a.1, f32[8,192,256]{2,1,0:T(8,128)} %copy-done, f32[8,192,256]{2,1,0:T(8,128)} %copy-done.2, bf16[1792,1024]{1,0:T(8,128)(2,1)} %shard_map.18.q_far, f32[3,256,256]{2,1,0:T(8,128)} %get-tuple-element.24.factors, ...), custom_call_target="tpu_custom_call" | custom-call | flops 20000000000 | bytes 10000000 | tf_op jit(solution)/shard_map/pallas_call | solution.py:312
  (28 shorter events, 0.2 us)
Async XLA Ops:
  6.5 40.1 %slice-start = ((f32[1024,1024]{1,0:T(8,128)}), f32[1024,256]{1,0:T(8,128)S(1)}, s32[]{:S(2)}) async-start(f32[1024,1024]{1,0:T(8,128)} %a.1), calls=%async_computation.3 | async-start | bytes 2097152 | tf_op jit(solution)/shard_map/slice | solution.py:370
  6.5 107.6 %all-gather.3.cloned.1.call-start = ((), (), s32[]{:S(2)}) async-start(), calls=%async_computation.2 | async-start | bytes 4456448 | tf_op jit(solution)/shard_map/all_gather | solution.py:388
  7.5 7.7 %collective-permute-start.2 = (f32[64,256]{1,0:T(8,128)S(1)}, f32[64,256]{1,0:T(8,128)S(1)}, u32[]{:S(2)}, u32[]{:S(2)}) collective-permute-start(f32[64,256]{1,0:T(8,128)S(1)} %get-tuple-element.30), channel_id=1, source_target_pairs={{0,64},{16,80},{32,96},{1,65},{17,81},{33,97},{2,66},{18,82},{34,9... | collective-permute-start | bytes 196616 | tf_op jit(solution)/shard_map/ppermute | solution.py:371
  11.6 3.6 %collective-permute-start.1 = (f32[64,256]{1,0:T(8,128)S(1)}, f32[64,256]{1,0:T(8,128)S(1)}, u32[]{:S(2)}, u32[]{:S(2)}) collective-permute-start(f32[64,256]{1,0:T(8,128)S(1)} %get-tuple-element.31), channel_id=1, source_target_pairs={{0,128},{16,144},{32,160},{1,129},{17,145},{33,161},{2,130},{18,14... | collective-permute-start | bytes 196616 | tf_op jit(solution)/shard_map/ppermute | solution.py:371
  13.9 2.6 %collective-permute-start = (f32[64,256]{1,0:T(8,128)S(1)}, f32[64,256]{1,0:T(8,128)S(1)}, u32[]{:S(2)}, u32[]{:S(2)}) collective-permute-start(f32[64,256]{1,0:T(8,128)S(1)} %get-tuple-element.32), channel_id=1, source_target_pairs={{0,192},{16,208},{32,224},{1,193},{17,209},{33,225},{2,194},{18,21... | collective-permute-start | bytes 196616 | tf_op jit(solution)/shard_map/ppermute | solution.py:371
  17.4 2.5 %collective-permute-start.3 = (f32[32,256]{1,0:T(8,128)S(1)}, f32[32,256]{1,0:T(8,128)S(1)}, u32[]{:S(2)}, u32[]{:S(2)}) collective-permute-start(f32[32,256]{1,0:T(8,128)S(1)} %constant_dynamic-slice_fusion), channel_id=1, source_target_pairs={{0,1},{1,0},{2,3},{3,2},{4,5},{5,4},{6,7},{7,6},{8,9},{9,8},{10,11... | collective-permute-start | bytes 98312 | tf_op jit(solution)/shard_map/ppermute | solution.py:358
  19.9 5.6 %collective-permute-start.4 = (f32[2,32,256]{2,1,0:T(8,128)S(1)}, f32[2,32,256]{2,1,0:T(8,128)S(1)}, u32[]{:S(2)}, u32[]{:S(2)}) collective-permute-start(f32[2,32,256]{2,1,0:T(8,128)S(1)} %pad_maximum_fusion.1), channel_id=1, source_target_pairs={{0,2},{1,3},{2,0},{3,1},{16,18},{17,19},{18,16},{19,17},{32,34},{3... | collective-permute-start | bytes 196616 | tf_op jit(solution)/shard_map/ppermute | solution.py:376
  25.5 12.0 %collective-permute-start.7 = (f32[2,32,256]{2,1,0:T(8,128)S(1)}, f32[2,32,256]{2,1,0:T(8,128)S(1)}, u32[]{:S(2)}, u32[]{:S(2)}) collective-permute-start(f32[2,32,256]{2,1,0:T(8,128)S(1)} %pad_maximum_fusion.2), channel_id=1, source_target_pairs={{0,4},{1,5},{2,6},{3,7},{16,20},{17,21},{18,22},{19,23},{32,36},{3... | collective-permute-start | bytes 196616 | tf_op jit(solution)/shard_map/ppermute | solution.py:361
  26.8 12.4 %collective-permute-start.6 = (f32[2,32,256]{2,1,0:T(8,128)S(1)}, f32[2,32,256]{2,1,0:T(8,128)S(1)}, u32[]{:S(2)}, u32[]{:S(2)}) collective-permute-start(f32[2,32,256]{2,1,0:T(8,128)S(1)} %pad_maximum_fusion.2), channel_id=1, source_target_pairs={{0,8},{1,9},{2,10},{3,11},{16,24},{17,25},{18,26},{19,27},{32,40},... | collective-permute-start | bytes 196616 | tf_op jit(solution)/shard_map/ppermute | solution.py:361
  30.2 9.1 %collective-permute-start.5 = (f32[2,32,256]{2,1,0:T(8,128)S(1)}, f32[2,32,256]{2,1,0:T(8,128)S(1)}, u32[]{:S(2)}, u32[]{:S(2)}) collective-permute-start(f32[2,32,256]{2,1,0:T(8,128)S(1)} %pad_maximum_fusion.2), channel_id=1, source_target_pairs={{0,12},{1,13},{2,14},{3,15},{16,28},{17,29},{18,30},{19,31},{32,44... | collective-permute-start | bytes 196616 | tf_op jit(solution)/shard_map/ppermute | solution.py:361
  32.6 6.7 %collective-permute-start.10 = (f32[256,256]{1,0:T(8,128)S(1)}, f32[256,256]{1,0:T(8,128)S(1)}, u32[]{:S(2)}, u32[]{:S(2)}) collective-permute-start(f32[256,256]{1,0:T(8,128)S(1)} %get-tuple-element.27), channel_id=1, source_target_pairs={{0,64},{16,80},{32,96},{1,65},{17,81},{33,97},{2,66},{18,82},{34,9... | collective-permute-start | bytes 786440 | tf_op jit(solution)/shard_map/ppermute | solution.py:371
  33.9 10.9 %collective-permute-start.9 = (f32[256,256]{1,0:T(8,128)S(1)}, f32[256,256]{1,0:T(8,128)S(1)}, u32[]{:S(2)}, u32[]{:S(2)}) collective-permute-start(f32[256,256]{1,0:T(8,128)S(1)} %get-tuple-element.28), channel_id=1, source_target_pairs={{0,128},{16,144},{32,160},{1,129},{17,145},{33,161},{2,130},{18,14... | collective-permute-start | bytes 786440 | tf_op jit(solution)/shard_map/ppermute | solution.py:371
  37.5 7.3 %collective-permute-start.8 = (f32[256,256]{1,0:T(8,128)S(1)}, f32[256,256]{1,0:T(8,128)S(1)}, u32[]{:S(2)}, u32[]{:S(2)}) collective-permute-start(f32[256,256]{1,0:T(8,128)S(1)} %get-tuple-element.29), channel_id=1, source_target_pairs={{0,192},{16,208},{32,224},{1,193},{17,209},{33,225},{2,194},{18,21... | collective-permute-start | bytes 786440 | tf_op jit(solution)/shard_map/ppermute | solution.py:371
  46.7 12.6 %collective-permute-start.13 = (f32[2,128,256]{2,1,0:T(8,128)S(1)}, f32[2,128,256]{2,1,0:T(8,128)S(1)}, u32[]{:S(2)}, u32[]{:S(2)}) collective-permute-start(f32[2,128,256]{2,1,0:T(8,128)S(1)} %bitcast.27), channel_id=1, source_target_pairs={{0,4},{1,5},{2,6},{16,20},{17,21},{18,22},{32,36},{33,37},{34,38},... | collective-permute-start | bytes 786440 | tf_op jit(solution)/shard_map/ppermute | solution.py:386
  48.0 11.3 %collective-permute-start.12 = (f32[2,128,256]{2,1,0:T(8,128)S(1)}, f32[2,128,256]{2,1,0:T(8,128)S(1)}, u32[]{:S(2)}, u32[]{:S(2)}) collective-permute-start(f32[2,128,256]{2,1,0:T(8,128)S(1)} %bitcast.26), channel_id=1, source_target_pairs={{0,8},{1,9},{2,10},{16,24},{17,25},{18,26},{32,40},{33,41},{34,42}... | collective-permute-start | bytes 786440 | tf_op jit(solution)/shard_map/ppermute | solution.py:386
  49.3 12.4 %collective-permute-start.11 = (f32[2,128,256]{2,1,0:T(8,128)S(1)}, f32[2,128,256]{2,1,0:T(8,128)S(1)}, u32[]{:S(2)}, u32[]{:S(2)}) collective-permute-start(f32[2,128,256]{2,1,0:T(8,128)S(1)} %bitcast.25), channel_id=1, source_target_pairs={{0,12},{1,13},{2,14},{16,28},{17,29},{18,30},{32,44},{33,45},{34,4... | collective-permute-start | bytes 786440 | tf_op jit(solution)/shard_map/ppermute | solution.py:386
  51.8 26.6 %all-to-all-start = ((f32[16,2,32,256]{3,2,1,0:T(8,128)}), f32[16,2,32,256]{3,2,1,0:T(8,128)S(1)}, u32[]{:S(2)}, u32[]{:S(2)}) async-start(f32[16,2,32,256]{3,2,1,0:T(8,128)} %broadcast_in_dim.25), calls=%async_computation | async-start | bytes 2097152 | tf_op jit(solution)/shard_map/all_to_all | solution.py:343
  61.8 3.2 %collective-permute-start.14 = (f32[128,256]{1,0:T(8,128)S(1)}, f32[128,256]{1,0:T(8,128)S(1)}, u32[]{:S(2)}, u32[]{:S(2)}) collective-permute-start(f32[128,256]{1,0:T(8,128)S(1)} %fusion.1), channel_id=1, source_target_pairs={{0,2},{1,3},{2,0},{4,6},{5,7},{6,4},{8,10},{9,11},{10,8},{12,14},{... | collective-permute-start | bytes 393224 | tf_op jit(solution)/shard_map/ppermute | solution.py:392
  65.1 6.7 %collective-permute-start.15 = (f32[64,256]{1,0:T(8,128)S(1)}, f32[64,256]{1,0:T(8,128)S(1)}, u32[]{:S(2)}, u32[]{:S(2)}) collective-permute-start(f32[64,256]{1,0:T(8,128)S(1)} %slice.104), channel_id=1, source_target_pairs={{0,1},{2,3},{4,5},{6,7},{8,9},{10,11},{12,13},{14,15},{16,17},{18,... | collective-permute-start | bytes 196616 | tf_op jit(solution)/shard_map/ppermute | solution.py:395
  78.4 7.4 %copy-start.1 = (f32[16,2,32,256]{3,2,1,0:T(8,128)}, f32[16,2,32,256]{3,2,1,0:T(8,128)S(1)}, u32[]{:S(2)}) copy-start(f32[16,2,32,256]{3,2,1,0:T(8,128)S(1)} %all-to-all-done.mine) | copy-start | bytes 3145732
  79.8 6.0 %collective-permute-start.16 = (f32[16,2,32,256]{3,2,1,0:T(8,128)S(1)}, f32[16,2,32,256]{3,2,1,0:T(8,128)}, u32[]{:S(2)}, u32[]{:S(2)}) collective-permute-start(f32[16,2,32,256]{3,2,1,0:T(8,128)S(1)} %all-to-all-done.mine), channel_id=1, source_target_pairs={{0,1},{1,0},{2,3},{3,2},{4,5},{5,4},{6,7},{7,6},{8,9},{9,8},{10,11... | collective-permute-start | bytes 3145736 | tf_op jit(solution)/shard_map/ppermute | solution.py:358
  82.2 42.0 %all-to-all-start.1 = ((f32[8,192,256]{2,1,0:T(8,128)}), f32[8,192,256]{2,1,0:T(8,128)S(1)}, u32[]{:S(2)}, u32[]{:S(2)}) async-start(f32[8,192,256]{2,1,0:T(8,128)} %broadcast_in_dim.26), calls=%async_computation.1 | async-start | bytes 3145728 | tf_op jit(solution)/shard_map/all_to_all | solution.py:343
  124.2 5.5 %copy-start = (f32[8,192,256]{2,1,0:T(8,128)}, f32[8,192,256]{2,1,0:T(8,128)S(1)}, u32[]{:S(2)}) copy-start(f32[8,192,256]{2,1,0:T(8,128)S(1)} %all-to-all-done.1.mine) | copy-start | bytes 4718596
  124.2 5.5 %collective-permute-start.17 = (f32[8,192,256]{2,1,0:T(8,128)S(1)}, f32[8,192,256]{2,1,0:T(8,128)S(1)}, u32[]{:S(2)}, u32[]{:S(2)}) collective-permute-start(f32[8,192,256]{2,1,0:T(8,128)S(1)} %all-to-all-done.1.mine), channel_id=1, source_target_pairs={{0,1},{1,0},{2,3},{3,2},{4,5},{5,4},{6,7},{7,6},{8,9},{9,8},{10,11... | collective-permute-start | bytes 4718600 | tf_op jit(solution)/shard_map/ppermute | solution.py:358
  129.7 1.1 copy-start.2
Sparse Core Ops, SparseCore 0:
  46.7 59.9 all-gather.2

commit v5 on v4

--- a/solution.py
+++ b/solution.py
@@ -175,7 +175,7 @@
             pltpu.VMEM((BLOCK, BLOCK), jnp.float32),
             pltpu.VMEM((2, SUB + 2, SUB, BLOCK), jnp.float32),
         ],
-        compiler_params=pltpu.CompilerParams(vmem_limit_bytes=56 * 2**20),
+        compiler_params=pltpu.CompilerParams(vmem_limit_bytes=16 * 2**20),
         cost_estimate=pl.CostEstimate(flops=3 * 10**10, bytes_accessed=10**6, transcendentals=0),
     )(where, mine, other)
 
@@ -227,7 +227,7 @@
         out_shape=jax.ShapeDtypeStruct((7 * TILE, 4 * TILE), jnp.bfloat16),
         in_specs=[VMEM] * 3,
         out_specs=VMEM,
-        compiler_params=pltpu.CompilerParams(vmem_limit_bytes=56 * 2**20),
+        compiler_params=pltpu.CompilerParams(vmem_limit_bytes=24 * 2**20),
         cost_estimate=pl.CostEstimate(flops=10**10, bytes_accessed=10**7, transcendentals=0),
     )(e, inverses, sides)
 
@@ -395,7 +395,7 @@
     got = lax.ppermute(third[64:], "col", [(2 * i, 2 * i + 1) for i in range(8)])
     my_chunk = jnp.concatenate([first, jnp.where(core == 0, third[:64], got)])
     chunk_copies = copies(my_chunk, Z_GROUPS)
-    lead_mine, chunk_copies = lax.optimization_barrier((lead_mine, chunk_copies))
+    lead_mine, chunk_copies, where = lax.optimization_barrier((lead_mine, chunk_copies, where))
     lead_other = swap(lead_mine)
     rows_mine = gather(chunk_copies, "col", Z_GROUPS)
     factors, inverses, sides = factorize(where, lead_mine, lead_other)

time: 156 us -> 157 us (level)
  local copies, waits for them, and re-layouts: 5.84 us -> 13 us
  Pallas kernels: 56.3 us -> 49.4 us
    unnamed x6 -> x16, local copies, waits for them, and re-layouts: 1.15 us -> 8.48 us
    pallas_call x1, Pallas kernels: 9.92 us -> 5.52 us  [across(): pl.pallas_call(across_kernel, out_shape=jax.ShapeDtypeStruct((7 * TILE, 4...]
    pallas_call x1, Pallas kernels: 28.3 us -> 25.8 us  [factorize(): pl.pallas_call(lead_kernel, out_shape=(three, three, three), in_specs=[SM...]
  transfers between devices with their start and end apart: 21 -> 21, of which waited for: 10 -> 9; matrix products, arithmetic and copies ran while one was open for 3% -> 2% of each run, Pallas kernels for 25% -> 20%
where the time goes in v5:
time: 157 us; the launch traced here: 156 us
  Pallas kernels  49.4 us (31%)
  starting transfers between devices  47.6 us (30%)
  waiting for transfers between devices  29.2 us (19%)
  between operations  13.9 us (9%)
  local copies, waits for them, and re-layouts  13 us (8%)
  other arithmetic  2.95 us (2%)
    pallas_call x1, Pallas kernels, factorize(): pl.pallas_call(lead_kernel, out_shape=(three, three, three), in_specs=[SM...  25.8 us
    pallas_call x1, Pallas kernels, update(): pl.pallas_call(update_kernel, grid=(4,), out_shape=jax.ShapeDtypeStruct(m...  18 us
    ppermute x6, starting transfers between devices, on_device(): lax.ppermute(value, 'row', [(x0, 4 * s + x0) for x0 in range(3)])  14.2 us
    all_to_all x2, starting transfers between devices, gather(): return lax.all_to_all(copied, axis, 0, 0, axis_index_groups=groups)  11.9 us
    unnamed x16, local copies, waits for them, and re-layouts  8.48 us
    ppermute x6, waiting for transfers between devices, on_device(): lax.ppermute(value, 'row', [(x0, 4 * s + x0) for x0 in range(3)])  6.8 us
    all_to_all x2, waiting for transfers between devices, gather(): return lax.all_to_all(copied, axis, 0, 0, axis_index_groups=groups)  6.58 us
    ppermute x3, starting transfers between devices, spread(): sent = [lax.ppermute(values[i], 'col', FAR[i]) for i in (1, 2, 3)]  5.89 us
  transfers between devices with their start and end apart: 21, of which 9 were waited for; matrix products, arithmetic and copies ran while one was open for 2% of the time, Pallas kernels for 20%

profile of v5, /device:TPU:1, one launch (start us, length us, event | category | flops | bytes accessed | tf_op | source)
XLA Modules:
  0.0 156.0 jit_solution(5024165407091736684)
XLA Ops:
  6.5 1.0 fusion.7
  7.5 4.0 %collective-permute-start.2 = (f32[64,256]{1,0:T(8,128)S(1)}, f32[64,256]{1,0:T(8,128)S(1)}, u32[]{:S(2)}, u32[]{:S(2)}) collective-permute-start(f32[64,256]{1,0:T(8,128)S(1)} %get-tuple-element.32), channel_id=1, source_target_pairs={{0,64},{16,80},{32,96},{1,65},{17,81},{33,97},{2,66},{18,82},{34,9... | collective-permute-start | bytes 196616 | tf_op jit(solution)/shard_map/ppermute | solution.py:371
  11.6 2.3 %collective-permute-start.1 = (f32[64,256]{1,0:T(8,128)S(1)}, f32[64,256]{1,0:T(8,128)S(1)}, u32[]{:S(2)}, u32[]{:S(2)}) collective-permute-start(f32[64,256]{1,0:T(8,128)S(1)} %get-tuple-element.33), channel_id=1, source_target_pairs={{0,128},{16,144},{32,160},{1,129},{17,145},{33,161},{2,130},{18,14... | collective-permute-start | bytes 196616 | tf_op jit(solution)/shard_map/ppermute | solution.py:371
  13.9 1.3 collective-permute-start
  15.2 1.2 collective-permute-done
  16.5 0.9 select_select_fusion.3
  17.4 1.6 %collective-permute-start.3 = (f32[32,256]{1,0:T(8,128)S(1)}, f32[32,256]{1,0:T(8,128)S(1)}, u32[]{:S(2)}, u32[]{:S(2)}) collective-permute-start(f32[32,256]{1,0:T(8,128)S(1)} %constant_dynamic-slice_fusion), channel_id=1, source_target_pairs={{0,1},{1,0},{2,3},{3,2},{4,5},{5,4},{6,7},{7,6},{8,9},{9,8},{10,11... | collective-permute-start | bytes 98312 | tf_op jit(solution)/shard_map/ppermute | solution.py:358
  19.0 0.9 collective-permute-done.3
  19.9 3.5 %collective-permute-start.4 = (f32[2,32,256]{2,1,0:T(8,128)S(1)}, f32[2,32,256]{2,1,0:T(8,128)S(1)}, u32[]{:S(2)}, u32[]{:S(2)}) collective-permute-start(f32[2,32,256]{2,1,0:T(8,128)S(1)} %pad_maximum_fusion.1), channel_id=1, source_target_pairs={{0,2},{1,3},{2,0},{3,1},{16,18},{17,19},{18,16},{19,17},{32,34},{3... | collective-permute-start | bytes 196616 | tf_op jit(solution)/shard_map/ppermute | solution.py:376
  23.5 2.0 %collective-permute-done.4 = f32[2,32,256]{2,1,0:T(8,128)S(1)} collective-permute-done((f32[2,32,256]{2,1,0:T(8,128)S(1)}, f32[2,32,256]{2,1,0:T(8,128)S(1)}, u32[]{:S(2)}, u32[]{:S(2)}) %collective-permute-start.4) | collective-permute-done | bytes 65568 | tf_op jit(solution)/shard_map/ppermute | solution.py:376
  25.5 1.3 collective-permute-start.7
  26.8 3.3 %collective-permute-start.6 = (f32[2,32,256]{2,1,0:T(8,128)S(1)}, f32[2,32,256]{2,1,0:T(8,128)S(1)}, u32[]{:S(2)}, u32[]{:S(2)}) collective-permute-start(f32[2,32,256]{2,1,0:T(8,128)S(1)} %pad_maximum_fusion.2), channel_id=1, source_target_pairs={{0,8},{1,9},{2,10},{3,11},{16,24},{17,25},{18,26},{19,27},{32,40},... | collective-permute-start | bytes 196616 | tf_op jit(solution)/shard_map/ppermute | solution.py:361
  30.2 1.3 collective-permute-start.5
  31.5 1.2 fusion.6
  32.6 1.3 collective-permute-start.10
  33.9 3.6 %collective-permute-start.9 = (f32[256,256]{1,0:T(8,128)S(1)}, f32[256,256]{1,0:T(8,128)S(1)}, u32[]{:S(2)}, u32[]{:S(2)}) collective-permute-start(f32[256,256]{1,0:T(8,128)S(1)} %get-tuple-element.30), channel_id=1, source_target_pairs={{0,128},{16,144},{32,160},{1,129},{17,145},{33,161},{2,130},{18,14... | collective-permute-start | bytes 786440 | tf_op jit(solution)/shard_map/ppermute | solution.py:371
  37.5 1.7 %collective-permute-start.8 = (f32[256,256]{1,0:T(8,128)S(1)}, f32[256,256]{1,0:T(8,128)S(1)}, u32[]{:S(2)}, u32[]{:S(2)}) collective-permute-start(f32[256,256]{1,0:T(8,128)S(1)} %get-tuple-element.31), channel_id=1, source_target_pairs={{0,192},{16,208},{32,224},{1,193},{17,209},{33,225},{2,194},{18,21... | collective-permute-start | bytes 786440 | tf_op jit(solution)/shard_map/ppermute | solution.py:371
  39.3 5.5 %collective-permute-done.9 = f32[256,256]{1,0:T(8,128)S(1)} collective-permute-done((f32[256,256]{1,0:T(8,128)S(1)}, f32[256,256]{1,0:T(8,128)S(1)}, u32[]{:S(2)}, u32[]{:S(2)}) %collective-permute-start.9) | collective-permute-done | bytes 262176 | tf_op jit(solution)/shard_map/ppermute | solution.py:371
  44.9 1.7 %select_select_fusion.1 = f32[256,256]{1,0:T(8,128)} fusion(f32[256,256]{1,0:T(8,128)S(1)} %collective-permute-done.8, f32[256,256]{1,0:T(8,128)S(1)} %collective-permute-done.9, f32[256,256]{1,0:T(8,128)S(1)} %collective-permute-done.10, f32[1024,1024]{1,0:T(8,128)} %a.1, pred[]{:T(512)S(6)} %eq.72, pred[]{:T(512)S(6)} %eq.71, pred[]{:T(512)S(6)} %eq.70, ...), kind=kLoop, calls=%fused_computation.2 | loop fusion | flops 262144 | bytes 1310724 | tf_op jit(solution)/shard_map/jit(_where)/select_n | solution.py:349
  46.6 0.0 all-gather.3.cloned.1.call-update
  46.6 0.1 slice_select_fusion
  46.7 1.3 collective-permute-start.13
  48.0 1.3 collective-permute-start.12
  49.3 1.3 collective-permute-start.11
  50.7 1.1 broadcast_in_dim.25
  51.8 7.5 %all-to-all-start = ((f32[16,2,32,256]{3,2,1,0:T(8,128)}), f32[16,2,32,256]{3,2,1,0:T(8,128)S(1)}, u32[]{:S(2)}, u32[]{:S(2)}) async-start(f32[16,2,32,256]{3,2,1,0:T(8,128)} %broadcast_in_dim.25), calls=%async_computation | async-start | bytes 2097152 | tf_op jit(solution)/shard_map/all_to_all | solution.py:343
  59.3 2.4 %collective-permute-done.11 = f32[2,128,256]{2,1,0:T(8,128)S(1)} collective-permute-done((f32[2,128,256]{2,1,0:T(8,128)S(1)}, f32[2,128,256]{2,1,0:T(8,128)S(1)}, u32[]{:S(2)}, u32[]{:S(2)}) %collective-permute-start.11) | collective-permute-done | bytes 262176 | tf_op jit(solution)/shard_map/ppermute | solution.py:386
  61.7 0.1 select_select_fusion
  61.8 1.3 collective-permute-start.14
  63.1 1.9 %collective-permute-done.14 = f32[128,256]{1,0:T(8,128)S(1)} collective-permute-done((f32[128,256]{1,0:T(8,128)S(1)}, f32[128,256]{1,0:T(8,128)S(1)}, u32[]{:S(2)}, u32[]{:S(2)}) %collective-permute-start.14) | collective-permute-done | bytes 131104 | tf_op jit(solution)/shard_map/ppermute | solution.py:392
  65.1 1.3 collective-permute-start.15
  66.4 0.1 pad_add_fusion.where
  66.5 5.3 %collective-permute-done.15 = f32[64,256]{1,0:T(8,128)S(1)} collective-permute-done((f32[64,256]{1,0:T(8,128)S(1)}, f32[64,256]{1,0:T(8,128)S(1)}, u32[]{:S(2)}, u32[]{:S(2)}) %collective-permute-start.15) | collective-permute-done | bytes 65568 | tf_op jit(solution)/shard_map/ppermute | solution.py:395
  71.8 6.6 %all-to-all-done.mine = f32[16,2,32,256]{3,2,1,0:T(8,128)S(1)} async-done(((f32[16,2,32,256]{3,2,1,0:T(8,128)}), f32[16,2,32,256]{3,2,1,0:T(8,128)S(1)}, u32[]{:S(2)}, u32[]{:S(2)}) %all-to-all-start) | async-done | bytes 1048608 | tf_op jit(solution)/shard_map/all_to_all | solution.py:343
  78.4 1.3 broadcast_in_dim.26
  79.7 1.8 %collective-permute-start.16 = (f32[16,2,32,256]{3,2,1,0:T(8,128)S(1)}, f32[16,2,32,256]{3,2,1,0:T(8,128)S(1)}, u32[]{:S(2)}, u32[]{:S(2)}) collective-permute-start(f32[16,2,32,256]{3,2,1,0:T(8,128)S(1)} %all-to-all-done.mine), channel_id=1, source_target_pairs={{0,1},{1,0},{2,3},{3,2},{4,5},{5,4},{6,7},{7,6},{8,9},{9,8},{10,11... | collective-permute-start | bytes 3145736 | tf_op jit(solution)/shard_map/ppermute | solution.py:358
  81.5 4.3 %all-to-all-start.1 = ((f32[8,192,256]{2,1,0:T(8,128)}), f32[8,192,256]{2,1,0:T(8,128)}, u32[]{:S(2)}, u32[]{:S(2)}) async-start(f32[8,192,256]{2,1,0:T(8,128)} %broadcast_in_dim.26), calls=%async_computation.1 | async-start | bytes 3145728 | tf_op jit(solution)/shard_map/all_to_all | solution.py:343
  85.8 25.8 %shard_map.17 = (f32[3,256,256]{2,1,0:T(8,128)S(1)}, f32[3,256,256]{2,1,0:T(8,128)S(1)}, f32[3,256,256]{2,1,0:T(8,128)S(1)}) custom-call(s32[3]{0:T(128)S(1)} %pad_add_fusion.where, f32[16,2,32,256]{3,2,1,0:T(8,128)S(1)} %all-to-all-done.mine, f32[16,2,32,256]{3,2,1,0:T(8,128)S(1)} %collective-permute-done.16.other), custom_call_target="tpu_custom_call" | custom-call | flops 30000001024 | bytes 1000000 | tf_op jit(solution)/shard_map/pallas_call | solution.py:167
  111.6 1.0 copy-done.4
  112.6 1.0 copy-done.6
  113.6 2.5 %copy-done.1 = f32[4096,256]{1,0:T(8,128)S(1)} copy-done((f32[4096,256]{1,0:T(8,128)S(1)}, f32[4096,256]{1,0:T(8,128)}, u32[]{:S(2)}) %copy-start.1) | copy-done | bytes 4194328
  116.0 1.1 copy-done.5
  117.2 5.5 %shard_map.18.q_far = bf16[1792,1024]{1,0:T(8,128)(2,1)S(1)} custom-call(f32[16,256,256]{2,1,0:T(8,128)S(1)} %bitcast.24, f32[3,256,256]{2,1,0:T(8,128)S(1)} %get-tuple-element.22.inverses, f32[3,256,256]{2,1,0:T(8,128)S(1)} %copy-done.5), custom_call_target="tpu_custom_call" | custom-call | flops 10000000000 | bytes 10000000 | tf_op jit(solution)/shard_map/pallas_call | solution.py:225
  122.7 1.8 %copy-done.2 = bf16[1792,1024]{1,0:T(8,128)(2,1)} copy-done((bf16[1792,1024]{1,0:T(8,128)(2,1)}, bf16[1792,1024]{1,0:T(8,128)(2,1)S(1)}, u32[]{:S(2)}) %copy-start.2) | copy-done | bytes 3670040
  124.5 2.2 %collective-permute-start.17 = (f32[8,192,256]{2,1,0:T(8,128)}, f32[8,192,256]{2,1,0:T(8,128)S(1)}, u32[]{:S(2)}, u32[]{:S(2)}) collective-permute-start(f32[8,192,256]{2,1,0:T(8,128)} %all-to-all-done.1.mine), channel_id=1, source_target_pairs={{0,1},{1,0},{2,3},{3,2},{4,5},{5,4},{6,7},{7,6},{8,9},{9,8},{10,11... | collective-permute-start | bytes 4718600 | tf_op jit(solution)/shard_map/ppermute | solution.py:358
  126.7 3.2 %collective-permute-done.17.other = f32[8,192,256]{2,1,0:T(8,128)S(1)} collective-permute-done((f32[8,192,256]{2,1,0:T(8,128)}, f32[8,192,256]{2,1,0:T(8,128)S(1)}, u32[]{:S(2)}, u32[]{:S(2)}) %collective-permute-start.17) | collective-permute-done | bytes 1572896 | tf_op jit(solution)/shard_map/ppermute | solution.py:358
  129.9 1.1 copy-done.7
  131.1 18.0 %shard_map.19 = f32[1024,1024]{1,0:T(8,128)} custom-call(s32[3]{0:T(128)} %copy-done, f32[1024,1024]{1,0:T(8,128)} %a.1, f32[8,192,256]{2,1,0:T(8,128)} %all-to-all-done.1.mine, f32[8,192,256]{2,1,0:T(8,128)} %copy-done.7, bf16[1792,1024]{1,0:T(8,128)(2,1)} %copy-done.2, f32[3,256,256]{2,1,0:T(8,128)} %copy-done.6, f32[3,256,256]{2,1,0:T(8,128)} %copy-done.3, ...), custom_call_target="tpu_custom_call" | custom-call | flops 20000000000 | bytes 10000000 | tf_op jit(solution)/shard_map/pallas_call | solution.py:312
  (38 shorter events, 0.2 us)
Async XLA Ops:
  6.5 40.1 %slice-start = ((f32[1024,1024]{1,0:T(8,128)}), f32[1024,256]{1,0:T(8,128)S(1)}, s32[]{:S(2)}) async-start(f32[1024,1024]{1,0:T(8,128)} %a.1), calls=%async_computation.3 | async-start | bytes 2097152 | tf_op jit(solution)/shard_map/slice | solution.py:370
  6.5 107.0 %all-gather.3.cloned.1.call-start = ((), (), s32[]{:S(2)}) async-start(), calls=%async_computation.2 | async-start | bytes 4456448 | tf_op jit(solution)/shard_map/all_gather | solution.py:388
  7.5 7.7 %collective-permute-start.2 = (f32[64,256]{1,0:T(8,128)S(1)}, f32[64,256]{1,0:T(8,128)S(1)}, u32[]{:S(2)}, u32[]{:S(2)}) collective-permute-start(f32[64,256]{1,0:T(8,128)S(1)} %get-tuple-element.32), channel_id=1, source_target_pairs={{0,64},{16,80},{32,96},{1,65},{17,81},{33,97},{2,66},{18,82},{34,9... | collective-permute-start | bytes 196616 | tf_op jit(solution)/shard_map/ppermute | solution.py:371
  11.6 3.6 %collective-permute-start.1 = (f32[64,256]{1,0:T(8,128)S(1)}, f32[64,256]{1,0:T(8,128)S(1)}, u32[]{:S(2)}, u32[]{:S(2)}) collective-permute-start(f32[64,256]{1,0:T(8,128)S(1)} %get-tuple-element.33), channel_id=1, source_target_pairs={{0,128},{16,144},{32,160},{1,129},{17,145},{33,161},{2,130},{18,14... | collective-permute-start | bytes 196616 | tf_op jit(solution)/shard_map/ppermute | solution.py:371
  13.9 2.6 %collective-permute-start = (f32[64,256]{1,0:T(8,128)S(1)}, f32[64,256]{1,0:T(8,128)S(1)}, u32[]{:S(2)}, u32[]{:S(2)}) collective-permute-start(f32[64,256]{1,0:T(8,128)S(1)} %get-tuple-element.34), channel_id=1, source_target_pairs={{0,192},{16,208},{32,224},{1,193},{17,209},{33,225},{2,194},{18,21... | collective-permute-start | bytes 196616 | tf_op jit(solution)/shard_map/ppermute | solution.py:371
  17.4 2.5 %collective-permute-start.3 = (f32[32,256]{1,0:T(8,128)S(1)}, f32[32,256]{1,0:T(8,128)S(1)}, u32[]{:S(2)}, u32[]{:S(2)}) collective-permute-start(f32[32,256]{1,0:T(8,128)S(1)} %constant_dynamic-slice_fusion), channel_id=1, source_target_pairs={{0,1},{1,0},{2,3},{3,2},{4,5},{5,4},{6,7},{7,6},{8,9},{9,8},{10,11... | collective-permute-start | bytes 98312 | tf_op jit(solution)/shard_map/ppermute | solution.py:358
  19.9 5.6 %collective-permute-start.4 = (f32[2,32,256]{2,1,0:T(8,128)S(1)}, f32[2,32,256]{2,1,0:T(8,128)S(1)}, u32[]{:S(2)}, u32[]{:S(2)}) collective-permute-start(f32[2,32,256]{2,1,0:T(8,128)S(1)} %pad_maximum_fusion.1), channel_id=1, source_target_pairs={{0,2},{1,3},{2,0},{3,1},{16,18},{17,19},{18,16},{19,17},{32,34},{3... | collective-permute-start | bytes 196616 | tf_op jit(solution)/shard_map/ppermute | solution.py:376
  25.5 12.0 %collective-permute-start.7 = (f32[2,32,256]{2,1,0:T(8,128)S(1)}, f32[2,32,256]{2,1,0:T(8,128)S(1)}, u32[]{:S(2)}, u32[]{:S(2)}) collective-permute-start(f32[2,32,256]{2,1,0:T(8,128)S(1)} %pad_maximum_fusion.2), channel_id=1, source_target_pairs={{0,4},{1,5},{2,6},{3,7},{16,20},{17,21},{18,22},{19,23},{32,36},{3... | collective-permute-start | bytes 196616 | tf_op jit(solution)/shard_map/ppermute | solution.py:361
  26.8 12.4 %collective-permute-start.6 = (f32[2,32,256]{2,1,0:T(8,128)S(1)}, f32[2,32,256]{2,1,0:T(8,128)S(1)}, u32[]{:S(2)}, u32[]{:S(2)}) collective-permute-start(f32[2,32,256]{2,1,0:T(8,128)S(1)} %pad_maximum_fusion.2), channel_id=1, source_target_pairs={{0,8},{1,9},{2,10},{3,11},{16,24},{17,25},{18,26},{19,27},{32,40},... | collective-permute-start | bytes 196616 | tf_op jit(solution)/shard_map/ppermute | solution.py:361
  30.2 9.1 %collective-permute-start.5 = (f32[2,32,256]{2,1,0:T(8,128)S(1)}, f32[2,32,256]{2,1,0:T(8,128)S(1)}, u32[]{:S(2)}, u32[]{:S(2)}) collective-permute-start(f32[2,32,256]{2,1,0:T(8,128)S(1)} %pad_maximum_fusion.2), channel_id=1, source_target_pairs={{0,12},{1,13},{2,14},{3,15},{16,28},{17,29},{18,30},{19,31},{32,44... | collective-permute-start | bytes 196616 | tf_op jit(solution)/shard_map/ppermute | solution.py:361
  32.6 6.7 %collective-permute-start.10 = (f32[256,256]{1,0:T(8,128)S(1)}, f32[256,256]{1,0:T(8,128)S(1)}, u32[]{:S(2)}, u32[]{:S(2)}) collective-permute-start(f32[256,256]{1,0:T(8,128)S(1)} %get-tuple-element.29), channel_id=1, source_target_pairs={{0,64},{16,80},{32,96},{1,65},{17,81},{33,97},{2,66},{18,82},{34,9... | collective-permute-start | bytes 786440 | tf_op jit(solution)/shard_map/ppermute | solution.py:371
  33.9 10.9 %collective-permute-start.9 = (f32[256,256]{1,0:T(8,128)S(1)}, f32[256,256]{1,0:T(8,128)S(1)}, u32[]{:S(2)}, u32[]{:S(2)}) collective-permute-start(f32[256,256]{1,0:T(8,128)S(1)} %get-tuple-element.30), channel_id=1, source_target_pairs={{0,128},{16,144},{32,160},{1,129},{17,145},{33,161},{2,130},{18,14... | collective-permute-start | bytes 786440 | tf_op jit(solution)/shard_map/ppermute | solution.py:371
  37.5 7.3 %collective-permute-start.8 = (f32[256,256]{1,0:T(8,128)S(1)}, f32[256,256]{1,0:T(8,128)S(1)}, u32[]{:S(2)}, u32[]{:S(2)}) collective-permute-start(f32[256,256]{1,0:T(8,128)S(1)} %get-tuple-element.31), channel_id=1, source_target_pairs={{0,192},{16,208},{32,224},{1,193},{17,209},{33,225},{2,194},{18,21... | collective-permute-start | bytes 786440 | tf_op jit(solution)/shard_map/ppermute | solution.py:371
  46.7 12.6 %collective-permute-start.13 = (f32[2,128,256]{2,1,0:T(8,128)S(1)}, f32[2,128,256]{2,1,0:T(8,128)S(1)}, u32[]{:S(2)}, u32[]{:S(2)}) collective-permute-start(f32[2,128,256]{2,1,0:T(8,128)S(1)} %bitcast.28), channel_id=1, source_target_pairs={{0,4},{1,5},{2,6},{16,20},{17,21},{18,22},{32,36},{33,37},{34,38},... | collective-permute-start | bytes 786440 | tf_op jit(solution)/shard_map/ppermute | solution.py:386
  48.0 11.3 %collective-permute-start.12 = (f32[2,128,256]{2,1,0:T(8,128)S(1)}, f32[2,128,256]{2,1,0:T(8,128)S(1)}, u32[]{:S(2)}, u32[]{:S(2)}) collective-permute-start(f32[2,128,256]{2,1,0:T(8,128)S(1)} %bitcast.27), channel_id=1, source_target_pairs={{0,8},{1,9},{2,10},{16,24},{17,25},{18,26},{32,40},{33,41},{34,42}... | collective-permute-start | bytes 786440 | tf_op jit(solution)/shard_map/ppermute | solution.py:386
  49.3 12.4 %collective-permute-start.11 = (f32[2,128,256]{2,1,0:T(8,128)S(1)}, f32[2,128,256]{2,1,0:T(8,128)S(1)}, u32[]{:S(2)}, u32[]{:S(2)}) collective-permute-start(f32[2,128,256]{2,1,0:T(8,128)S(1)} %bitcast.26), channel_id=1, source_target_pairs={{0,12},{1,13},{2,14},{16,28},{17,29},{18,30},{32,44},{33,45},{34,4... | collective-permute-start | bytes 786440 | tf_op jit(solution)/shard_map/ppermute | solution.py:386
  51.8 26.6 %all-to-all-start = ((f32[16,2,32,256]{3,2,1,0:T(8,128)}), f32[16,2,32,256]{3,2,1,0:T(8,128)S(1)}, u32[]{:S(2)}, u32[]{:S(2)}) async-start(f32[16,2,32,256]{3,2,1,0:T(8,128)} %broadcast_in_dim.25), calls=%async_computation | async-start | bytes 2097152 | tf_op jit(solution)/shard_map/all_to_all | solution.py:343
  61.8 3.2 %collective-permute-start.14 = (f32[128,256]{1,0:T(8,128)S(1)}, f32[128,256]{1,0:T(8,128)S(1)}, u32[]{:S(2)}, u32[]{:S(2)}) collective-permute-start(f32[128,256]{1,0:T(8,128)S(1)} %fusion.1), channel_id=1, source_target_pairs={{0,2},{1,3},{2,0},{4,6},{5,7},{6,4},{8,10},{9,11},{10,8},{12,14},{... | collective-permute-start | bytes 393224 | tf_op jit(solution)/shard_map/ppermute | solution.py:392
  65.1 6.7 %collective-permute-start.15 = (f32[64,256]{1,0:T(8,128)S(1)}, f32[64,256]{1,0:T(8,128)S(1)}, u32[]{:S(2)}, u32[]{:S(2)}) collective-permute-start(f32[64,256]{1,0:T(8,128)S(1)} %slice.104), channel_id=1, source_target_pairs={{0,1},{2,3},{4,5},{6,7},{8,9},{10,11},{12,13},{14,15},{16,17},{18,... | collective-permute-start | bytes 196616 | tf_op jit(solution)/shard_map/ppermute | solution.py:395
  66.5 45.2 %copy-start = (s32[3]{0:T(128)}, s32[3]{0:T(128)S(1)}, u32[]{:S(2)}) copy-start(s32[3]{0:T(128)S(1)} %pad_add_fusion.where) | copy-start | bytes 40
  79.7 6.1 %collective-permute-start.16 = (f32[16,2,32,256]{3,2,1,0:T(8,128)S(1)}, f32[16,2,32,256]{3,2,1,0:T(8,128)S(1)}, u32[]{:S(2)}, u32[]{:S(2)}) collective-permute-start(f32[16,2,32,256]{3,2,1,0:T(8,128)S(1)} %all-to-all-done.mine), channel_id=1, source_target_pairs={{0,1},{1,0},{2,3},{3,2},{4,5},{5,4},{6,7},{7,6},{8,9},{9,8},{10,11... | collective-permute-start | bytes 3145736 | tf_op jit(solution)/shard_map/ppermute | solution.py:358
  81.5 43.0 %all-to-all-start.1 = ((f32[8,192,256]{2,1,0:T(8,128)}), f32[8,192,256]{2,1,0:T(8,128)}, u32[]{:S(2)}, u32[]{:S(2)}) async-start(f32[8,192,256]{2,1,0:T(8,128)} %broadcast_in_dim.26), calls=%async_computation.1 | async-start | bytes 3145728 | tf_op jit(solution)/shard_map/all_to_all | solution.py:343
  111.6 1.0 copy-start.4
  112.6 1.0 copy-start.6
  113.6 9.1 %copy-start.3 = (f32[3,256,256]{2,1,0:T(8,128)}, f32[3,256,256]{2,1,0:T(8,128)S(1)}, u32[]{:S(2)}) copy-start(f32[3,256,256]{2,1,0:T(8,128)S(1)} %get-tuple-element.22.inverses) | copy-start | bytes 2359300
  113.6 2.5 %copy-start.1 = (f32[4096,256]{1,0:T(8,128)S(1)}, f32[4096,256]{1,0:T(8,128)}, u32[]{:S(2)}) copy-start(f32[4096,256]{1,0:T(8,128)} %all-gather.3.cloned.1.call-done) | copy-start | bytes 12582916
  116.0 1.1 copy-start.5
  122.7 1.8 %copy-start.2 = (bf16[1792,1024]{1,0:T(8,128)(2,1)}, bf16[1792,1024]{1,0:T(8,128)(2,1)S(1)}, u32[]{:S(2)}) copy-start(bf16[1792,1024]{1,0:T(8,128)(2,1)S(1)} %shard_map.18.q_far) | copy-start | bytes 11010052
  124.5 5.4 %collective-permute-start.17 = (f32[8,192,256]{2,1,0:T(8,128)}, f32[8,192,256]{2,1,0:T(8,128)S(1)}, u32[]{:S(2)}, u32[]{:S(2)}) collective-permute-start(f32[8,192,256]{2,1,0:T(8,128)} %all-to-all-done.1.mine), channel_id=1, source_target_pairs={{0,1},{1,0},{2,3},{3,2},{4,5},{5,4},{6,7},{7,6},{8,9},{9,8},{10,11... | collective-permute-start | bytes 4718600 | tf_op jit(solution)/shard_map/ppermute | solution.py:358
  129.9 1.1 copy-start.7
Sparse Core Ops, SparseCore 0:
  46.7 59.8 all-gather.2
